TPU v7x, 128 devices: a whole 4x4x4 slice. The times are simulated.
128 devices in a mesh: dp: 8 (over y, core), inner: 16 (over x, z).
Axes of the slice: x: 4, y: 4, z: 4, core: 2. Of those that a mesh axis runs over, the one named last changes fastest.
Arguments:
- patches: bfloat16 [49152, 1280], P(('dp', 'inner')), may hold values from -5 to 5
- segments: int32 [384, 128], P(('dp', 'inner')), may hold values from 0 to 63, as said below
- owners: int32 [384], P(('dp', 'inner')), may hold values from 0 to 7, as said below
- norm_gain: float32 [1280], replicated, may hold values from 0.1 to 1.9
- qkv_weight: bfloat16 [1280, 3840], P(('dp', 'inner')), may hold values from -0.12633784 to 0.12633784
- cotangent: bfloat16 [49152, 1280], P(('dp', 'inner')), may hold values from -6 to 6
Outputs:
- attended: bfloat16 [49152, 1280], P(('dp', 'inner'))
- grad_patches: bfloat16 [49152, 1280], P(('dp', 'inner'))
- grad_qkv: float32 [1280, 3840], P(('dp', 'inner'))
- grad_gain: float32 [1280], replicated
Inputs may be any that keep to these rules, and one draw needn't show every extreme that they name: `segments`: within a tile the ids start at 0 and grow by 0 or 1 from one patch to the next, growing only at even positions of the tile; patches of one image share an id. `owners`: the 3 tiles of one device go to 3 different groups, and for every inner index each group is owner of exactly 3 tiles.
All inputs are finite; a program needn't handle non-finite values.
Results may differ from a plain program's by a relative error of at most 0.017.
Values may be sent and summed in bfloat16 or wider, within the bound.
No kernel may reach another device: no remote copies, remote signals or barrier semaphores. Data moves between devices by JAX's collectives and lax.ppermute only.
A program may use at most 192 MiB of HBM per device.

v0:
```python
import functools

import jax
import jax.numpy as jnp
from jax import lax
from jax.experimental import pallas as pl
from jax.experimental.pallas import tpu as pltpu
from jax.sharding import PartitionSpec as P

D = 1280
HEADS = 16
HDIM = 80
TILE = 128
TILES = 3
N_DP = 8
N_INNER = 16
ROWS = TILES * TILE
PAIR_ROWS = 2 * ROWS
HALF = D // 2
COLS = 3 * HALF
OWN = 10
BLOCK = 80
PART = 160
PIECES = 8
STRIP = 16
MSG = 16
EPS = 1e-6
MASKED = -1e30
SCALE = HDIM ** (-0.5)
LOG2E = 1.4426950408889634
BF = jnp.bfloat16
F32 = jnp.float32
VM = pl.BlockSpec(memory_space=pltpu.VMEM)
SM = pl.BlockSpec(memory_space=pltpu.SMEM)
ANY = pl.BlockSpec(memory_space=pltpu.HBM)
NT = (((1,), (1,)), ((), ()))
TN = (((0,), (0,)), ((), ()))
NN = (((1,), (0,)), ((), ()))


def params(mib, **more):
    return pltpu.CompilerParams(vmem_limit_bytes=mib * 2**20, **more)


def cost(flops, nbytes, trans=0):
    return pl.CostEstimate(
        flops=flops // 1000, bytes_accessed=nbytes // 1000, transcendentals=trans // 1000
    )


def dot(a, b, dims=NN):
    return lax.dot_general(a, b, dims, preferred_element_type=F32)


def norm_rows(rows):
    wide = rows.astype(F32)
    centred = wide - jnp.mean(wide, axis=-1, keepdims=True)
    variance = jnp.mean(centred * centred, axis=-1, keepdims=True)
    inv_std = lax.rsqrt(variance + EPS)
    return centred * inv_std, inv_std


def build_order(nat_ref, perm_ref):
    for r in range(D // TILE):
        rows = slice(TILE * r, TILE * (r + 1))
        column = jnp.broadcast_to(nat_ref[:, rows], (TILE, TILE)).T
        for a in range(D // TILE):
            feature = lax.broadcasted_iota(jnp.int32, (TILE, TILE), 1) + TILE * a
            hit = column == feature.astype(F32)
            perm_ref[rows, TILE * a : TILE * (a + 1)] = jnp.where(hit, 1.0, 0.0).astype(BF)


def prep_kernel(patches_ref, gain_ref, nat_ref, normed_ref, normed_t_ref, perm_ref):
    build_order(nat_ref, perm_ref)
    standard, _ = norm_rows(patches_ref[...])
    normed = (standard * gain_ref[...]).astype(BF)
    normed_ref[...] = dot(normed, perm_ref[...], NT).astype(BF)
    normed_t_ref[...] = dot(perm_ref[...], normed, NT).astype(BF)


def prep(patches, gain, nat):
    return pl.pallas_call(
        prep_kernel,
        in_specs=[VM] * 3,
        out_specs=[VM] * 2,
        out_shape=[
            jax.ShapeDtypeStruct((ROWS, D), BF),
            jax.ShapeDtypeStruct((D, ROWS), BF),
        ],
        scratch_shapes=[pltpu.VMEM((D, D), BF)],
        compiler_params=params(58),
        cost_estimate=cost(4 * ROWS * D * D, 6 * ROWS * D),
        name="prep",
    )(patches, gain, nat)


def build_kernel(own_ref, w_ref, seg_ref, out_ref):
    lane = lax.broadcasted_iota(jnp.int32, (1, TILE), 1)
    owners = jnp.zeros((1, TILE), jnp.int32)
    for t in range(TILES):
        owners = jnp.where(lane == t, own_ref[t], owners)
    for d in range(N_DP):
        out_ref[d, OWN:MSG, :] = jnp.zeros((MSG - OWN, COLS), BF)
        for t in range(TILES):
            out_ref[d, OWN : OWN + 1, TILE * t : TILE * (t + 1)] = (
                seg_ref[t : t + 1, :].astype(F32).astype(BF)
            )
        out_ref[d, OWN + 1 : OWN + 2, 0:TILE] = owners.astype(F32).astype(BF)
        for a in range(3):
            start = D * a + HALF * (d % 2)
            out_ref[d, 0:OWN, HALF * a : HALF * (a + 1)] = w_ref[:, start : start + HALF]


def build(owners, weight, segments):
    return pl.pallas_call(
        build_kernel,
        in_specs=[SM, VM, VM],
        out_specs=VM,
        out_shape=jax.ShapeDtypeStruct((N_DP, MSG, COLS), BF),
        cost_estimate=cost(0, 2 * N_DP * MSG * COLS),
        compiler_params=params(12),
        name="build",
    )(owners, weight, segments)


def compact_kernel(group_ref, msg_ref, w_ref, seg_ref, own_ref):
    group = group_ref[0]
    seg_ref[...] = jnp.zeros_like(seg_ref)
    for s in range(N_DP):
        w_ref[OWN * s : OWN * (s + 1), :] = msg_ref[s, 0:OWN, :]
        own_ref[s : s + 1, :] = msg_ref[s, OWN + 1 : OWN + 2, 0:TILE].astype(F32)
    for rel in range(2):
        src = group + rel * (1 - 2 * (group % 2))
        for t in range(TILES):
            seg_ref[TILES * rel + t : TILES * rel + t + 1, :] = msg_ref[
                src, OWN : OWN + 1, TILE * t : TILE * (t + 1)
            ].astype(F32)


def compact(group, messages):
    return pl.pallas_call(
        compact_kernel,
        in_specs=[SM, VM],
        out_specs=[VM] * 3,
        out_shape=[
            jax.ShapeDtypeStruct((BLOCK, COLS), BF),
            jax.ShapeDtypeStruct((8, TILE), F32),
            jax.ShapeDtypeStruct((N_DP, TILE), F32),
        ],
        cost_estimate=cost(0, 4 * N_DP * MSG * COLS),
        compiler_params=params(12),
        name="compact",
    )(group, messages)


def to_heads_kernel(fwd_ref, in_ref, out_ref):
    for d in range(N_DP):
        half = slice(HALF * (d % 2), HALF * (d % 2 + 1))
        for k in range(2 * TILES):
            u = TILES * (2 * (d // 2) + ((d % 2) ^ (k // TILES))) + k % TILES
            out_ref[d, k] = in_ref[fwd_ref[u], :, half]


def to_heads(fwd, strips):
    return pl.pallas_call(
        to_heads_kernel,
        in_specs=[SM, VM],
        out_specs=VM,
        out_shape=jax.ShapeDtypeStruct((N_DP, 2 * TILES, STRIP, HALF), BF),
        cost_estimate=cost(0, 4 * ROWS * D),
        compiler_params=params(12),
        name="to_heads",
    )(fwd, strips)


def place_kernel(idx_ref, left_ref, right_ref, out_ref):
    out_ref[0, :, :HALF] = left_ref[0, 0]
    out_ref[0, :, HALF:] = right_ref[0, 0]


def place(index, slots):
    def half(c):
        return pl.BlockSpec(
            (1, 1, TILE, HALF), lambda p, g: (g[p] + c, g[TILES + p], 0, 0)
        )

    spec = pltpu.PrefetchScalarGridSpec(
        num_scalar_prefetch=1,
        grid=(TILES,),
        in_specs=[half(0), half(1)],
        out_specs=pl.BlockSpec((1, TILE, D), lambda p, g: (p, 0, 0)),
    )
    return pl.pallas_call(
        place_kernel,
        grid_spec=spec,
        out_shape=jax.ShapeDtypeStruct((TILES, TILE, D), BF),
        compiler_params=params(12),
        cost_estimate=cost(0, 4 * ROWS * D),
        name="place",
    )(index, slots, slots)


def window_masks(i):
    lane = lax.broadcasted_iota(jnp.int32, (TILE, 256), 1)
    start = 32 * i
    first = (lane >= start) & (lane < start + HDIM)
    second = (lane >= start + HDIM) & (lane < start + 2 * HDIM)
    return first, second


def stack_heads(window, masks):
    zero = jnp.zeros_like(window)
    return jnp.concatenate([jnp.where(m, window, zero) for m in masks], axis=0)


def pick_heads(stacked, masks):
    zero = jnp.zeros((TILE, 256), F32)
    return jnp.where(
        masks[0], stacked[:TILE], jnp.where(masks[1], stacked[TILE:], zero)
    )


def halves(fn, *arrays):
    return jnp.concatenate(
        [fn(*(a[:, :TILE] for a in arrays)), fn(*(a[:, TILE:] for a in arrays))], axis=1
    )


def wide_max(a):
    return jnp.broadcast_to(jnp.max(a, axis=-1, keepdims=True), a.shape)


def wide_sum(a):
    return jnp.broadcast_to(jnp.sum(a, axis=-1, keepdims=True), a.shape)


CHUNKS = [pl.ds(0, 768), pl.ds(768, 768), pl.ds(1536, 384)]


def start(copies):
    for copy in copies:
        copy.start()


def wait(copies):
    for copy in copies:
        copy.wait()


def load_weight(pieces, weight, sems):
    return [
        [
            pltpu.make_async_copy(
                piece.at[:, cols],
                weight.at[pl.ds(PART * b, PART), cols],
                sems.at[n, b],
            )
            for b, piece in enumerate(pieces)
        ]
        for n, cols in enumerate(CHUNKS)
    ]


def load_rows(refs, rows, sems):
    return [
        pltpu.make_async_copy(ref, rows.at[pl.ds(ROWS * h, ROWS)], sems.at[h])
        for h, ref in enumerate(refs)
    ]


def load_features(refs, normed_t, sems):
    return [
        pltpu.make_async_copy(ref, normed_t.at[:, pl.ds(ROWS * h, ROWS)], sems.at[h])
        for h, ref in enumerate(refs)
    ]


def gradient(normed_t, dqkv, weight, outs, staged, gain_part, sems):
    copies = []
    places = [(0, 0), (1, 0), (2, 0), (4, PART), (4, 0), (5, 0), (5, PART), (3, 0)]
    for c, cols in enumerate(CHUNKS):
        for n in range(0, PIECES, 2):
            rows = slice(PART * n, PART * (n + 2))
            both = dot(normed_t[rows, :], dqkv[:, cols])
            product = both * weight[rows, cols].astype(F32)
            lanes = sum(
                product[:, TILE * k : TILE * (k + 1)] for k in range(cols.size // TILE)
            )
            gain_part[rows, :] = lanes if c == 0 else gain_part[rows, :] + lanes
            both = both.astype(BF)
            for k in (n, n + 1):
                staged[k, :, cols] = both[PART * (k - n) : PART * (k - n + 1)]
                copies.append(
                    pltpu.make_async_copy(
                        staged.at[k, :, cols],
                        outs[places[k][0]].at[pl.ds(places[k][1], PART), cols],
                        sems.at[c, k],
                    )
                )
                copies[-1].start()
    wait(copies)


def main_kernel(
    idx_ref,
    seg_ref,
    normed_ref,
    partner_ref,
    normed_t_ref,
    partner_t_ref,
    cot_ref,
    *refs,
):
    pieces, slots_ref, dqkv_ref = refs[:PIECES], refs[PIECES], refs[PIECES + 1]
    grads, gain_ref = refs[PIECES + 2 : PIECES + 8], refs[PIECES + 8]
    (
        normed,
        qkv,
        cot,
        weight,
        normed_t,
        dqkv,
        out_tiles,
        staged,
        row_sems,
        cot_sems,
        w_sems,
        t_sems,
        slot_sems,
        dqkv_sems,
        grad_sems,
    ) = refs[PIECES + 9 :]
    row_copies = load_rows((normed_ref, partner_ref), normed, row_sems)
    w_copies = load_weight(pieces, weight, w_sems)
    cot_copies = [
        pltpu.make_async_copy(cot_ref.at[j], cot.at[:, j], cot_sems.at[j])
        for j in range(N_DP)
    ]
    t_copies = load_features((normed_t_ref, partner_t_ref), normed_t, t_sems)
    start(row_copies)
    for copies in w_copies:
        start(copies)
    start(cot_copies)
    start(t_copies)
    wait(row_copies)
    for c, cols in enumerate(CHUNKS):
        wait(w_copies[c])
        qkv[:, cols] = dot(normed[...], weight[:, cols]).astype(BF)
    wait(cot_copies)

    def leave(t):
        rows = pl.ds(pl.multiple_of(t * TILE, TILE), TILE)
        return [
            pltpu.make_async_copy(
                out_tiles.at[t],
                slots_ref.at[idx_ref[t], idx_ref[2 * TILES + t]],
                slot_sems.at[t],
            ),
            pltpu.make_async_copy(dqkv.at[rows], dqkv_ref.at[rows], dqkv_sems.at[t]),
        ]

    @pl.loop(0, TILES)
    def _(step):
        pairs = range(8)
        tiles = [2 * step, 2 * step + 1]
        rows = [pl.ds(pl.multiple_of(t * TILE, TILE), TILE) for t in tiles]
        same = []
        for t in tiles:
            seg = jnp.broadcast_to(seg_ref[pl.ds(t, 1), :], (TILE, TILE))
            equal = seg == seg.T
            same.append(jnp.concatenate([equal, equal], axis=1))
        masks = [window_masks(i % 4) for i in pairs]
        windows = [slice(128 * (i % 4), 128 * (i % 4) + 256) for i in pairs]

        def window(a, i):
            first = HALF * a + 128 * (i % 4)
            return qkv[rows[i // 4], first : first + 256]

        q = [window(0, i) for i in pairs]
        d_out = [
            cot[tiles[i // 4], :, :, windows[i]].reshape(TILE, 256) for i in pairs
        ]
        kk = [stack_heads(window(1, i), masks[i]) for i in pairs]
        vv = [stack_heads(window(2, i), masks[i]) for i in pairs]
        scores = [dot(q[i], kk[i], NT) for i in pairs]
        d_probs = [dot(d_out[i], vv[i], NT) for i in pairs]
        scores = [
            jnp.where(same[i // 4], scores[i] * (SCALE * LOG2E), MASKED) for i in pairs
        ]
        tops = [halves(wide_max, x) for x in scores]
        expo = [jnp.exp2(x - m) for x, m in zip(scores, tops)]
        sums = [halves(wide_sum, x) for x in expo]
        weights = [x * (1.0 / total) for x, total in zip(expo, sums)]
        rounded = [x.astype(BF) for x in weights]
        outs = [dot(rounded[i], vv[i]) for i in pairs]
        dvs = [dot(rounded[i], d_out[i], TN) for i in pairs]
        inner = [halves(wide_sum, d_probs[i] * weights[i]) for i in pairs]
        d_scores = [
            (weights[i] * (d_probs[i] - inner[i]) * SCALE).astype(BF) for i in pairs
        ]
        dqs = [dot(d_scores[i], kk[i]) for i in pairs]
        dks = [dot(d_scores[i], q[i], TN) for i in pairs]
        dks = [pick_heads(dks[i], masks[i]) for i in pairs]
        dvs = [pick_heads(dvs[i], masks[i]) for i in pairs]

        def lanes(vals):
            parts = [vals[0][:, :TILE]]
            for i in range(3):
                parts.append(vals[i][:, TILE:] + vals[i + 1][:, :TILE])
            parts.append(vals[3][:, TILE:])
            return jnp.concatenate([p.astype(BF) for p in parts], axis=1)

        for n, t in enumerate(tiles):
            part = slice(4 * n, 4 * n + 4)
            out_tiles[t] = lanes(outs[part])
            for a, vals in enumerate((dqs, dks, dvs)):
                dqkv[rows[n], HALF * a : HALF * (a + 1)] = lanes(vals[part])
            start(leave(t))

    wait(t_copies)
    gradient(normed_t, dqkv, weight, grads, staged, gain_ref, grad_sems)
    for t in range(2 * TILES):
        wait(leave(t))


def main(index, seg, normed, normed_t, cot, pieces):
    return pl.pallas_call(
        main_kernel,
        in_specs=[SM, VM] + [ANY] * (5 + PIECES),
        out_specs=[ANY] * 8 + [VM],
        out_shape=[
            jax.ShapeDtypeStruct((N_DP, 2, TILE, HALF), BF),
            jax.ShapeDtypeStruct((PAIR_ROWS, COLS), BF),
        ]
        + [jax.ShapeDtypeStruct((PART, COLS), BF)] * 4
        + [jax.ShapeDtypeStruct((2 * PART, COLS), BF)] * 2
        + [jax.ShapeDtypeStruct((D, TILE), F32)],
        scratch_shapes=[
            pltpu.VMEM((PAIR_ROWS, D), BF),
            pltpu.VMEM((PAIR_ROWS, COLS), BF),
            pltpu.VMEM((2 * TILES, N_DP, STRIP, HALF), BF),
            pltpu.VMEM((D, COLS), BF),
            pltpu.VMEM((D, PAIR_ROWS), BF),
            pltpu.VMEM((PAIR_ROWS, COLS), BF),
            pltpu.VMEM((2 * TILES, TILE, HALF), BF),
            pltpu.VMEM((PIECES, PART, COLS), BF),
            pltpu.SemaphoreType.DMA((2,)),
            pltpu.SemaphoreType.DMA((N_DP,)),
            pltpu.SemaphoreType.DMA((len(CHUNKS), PIECES)),
            pltpu.SemaphoreType.DMA((2,)),
            pltpu.SemaphoreType.DMA((2 * TILES,)),
            pltpu.SemaphoreType.DMA((2 * TILES,)),
            pltpu.SemaphoreType.DMA((len(CHUNKS), PIECES)),
        ],
        compiler_params=params(58),
        cost_estimate=cost(8 * 10**9, 20 * 2**20, 10**6),
        name="main",
    )(index, seg, *normed, *normed_t, cot, *pieces)


def add_kernel(counts, firsts, cuts, *refs):
    outs, used = refs[sum(counts) :], 0
    for n, count in enumerate(counts):
        total = jnp.zeros((PART, COLS), F32)
        for k in range(used, used + count):
            total = total + refs[k][firsts[k] : firsts[k] + PART, :].astype(F32)
        used += count
        size = PART // cuts
        for k in range(cuts):
            outs[cuts * n + k][...] = total[size * k : size * (k + 1)].astype(BF)


def add(groups, cuts=1):
    parts = [part for group in groups for part in group]
    shape = jax.ShapeDtypeStruct((PART // cuts, COLS), BF)
    return pl.pallas_call(
        functools.partial(
            add_kernel, [len(group) for group in groups], [f for _, f in parts], cuts
        ),
        in_specs=[VM] * len(parts),
        out_specs=[VM] * (cuts * len(groups)),
        out_shape=[shape] * (cuts * len(groups)),
        compiler_params=params(12),
        cost_estimate=cost(0, 4 * len(parts) * PART * COLS),
        name="add",
    )(*[array for array, _ in parts])


def gain_kernel(part_ref, nat_ref, gain_ref, out_ref, perm_ref):
    build_order(nat_ref, perm_ref)
    rest = jnp.sum(part_ref[...], axis=1, keepdims=True)
    rest = jnp.broadcast_to(rest, (D, TILE))
    total = jnp.zeros((1, D), F32)
    for _ in range(3):
        term = rest.astype(BF)
        rest = rest - term.astype(F32)
        total = total + dot(term, perm_ref[...], TN)[0:1]
    total = total / gain_ref[...]
    out_ref[...] = jnp.zeros_like(out_ref)
    for k in range(D // TILE):
        out_ref[k : k + 1, :] = total[:, TILE * k : TILE * (k + 1)]


def gain_back(part, nat, gain):
    return pl.pallas_call(
        gain_kernel,
        in_specs=[VM] * 3,
        out_specs=VM,
        out_shape=jax.ShapeDtypeStruct((MSG, TILE), F32),
        scratch_shapes=[pltpu.VMEM((D, D), BF)],
        compiler_params=params(24),
        cost_estimate=cost(0, 4 * D * TILE),
        name="gain",
    )(part, nat, gain)


def back_kernel(half, nat_ref, dqkv_ref, *refs):
    pieces, (out_ref, weight, perm_ref, dqkv, w_sems, q_sem) = (
        refs[:PIECES],
        refs[PIECES:],
    )
    w_copies = load_weight(pieces, weight, w_sems)
    q_copy = pltpu.make_async_copy(dqkv_ref.at[pl.ds(ROWS * half, ROWS)], dqkv, q_sem)
    q_copy.start()
    for copies in w_copies:
        start(copies)
    build_order(nat_ref, perm_ref)
    q_copy.wait()
    for copies in w_copies:
        wait(copies)
    d_normed = dot(dqkv[...], weight[...], NT).astype(BF)
    out_ref[...] = dot(d_normed, perm_ref[...]).astype(BF)


def back(half, dqkv, pieces, nat):
    return pl.pallas_call(
        functools.partial(back_kernel, half),
        in_specs=[VM] + [ANY] * (1 + PIECES),
        out_specs=VM,
        out_shape=jax.ShapeDtypeStruct((ROWS, D), BF),
        scratch_shapes=[
            pltpu.VMEM((D, COLS), BF),
            pltpu.VMEM((D, D), BF),
            pltpu.VMEM((ROWS, COLS), BF),
            pltpu.SemaphoreType.DMA((len(CHUNKS), PIECES)),
            pltpu.SemaphoreType.DMA,
        ],
        compiler_params=params(58),
        cost_estimate=cost(2 * ROWS * D * (D + COLS), 15 * 2**20),
        name="back",
    )(nat, dqkv, *pieces)


def rows_kernel(patches_ref, gain_ref, mine_ref, other_ref, out_ref):
    standard, inv_std = norm_rows(patches_ref[...])
    d_normed = mine_ref[...].astype(F32) + other_ref[...].astype(F32)
    scaled = d_normed * gain_ref[...]
    back_rows = inv_std * (
        scaled
        - jnp.mean(scaled, axis=-1, keepdims=True)
        - standard * jnp.mean(scaled * standard, axis=-1, keepdims=True)
    )
    out_ref[...] = back_rows.astype(BF)


def rows_back(patches, gain, mine, other):
    block = pl.BlockSpec((TILE, D), lambda i: (i, 0))
    return pl.pallas_call(
        rows_kernel,
        grid=(TILES,),
        in_specs=[block, pl.BlockSpec((1, D), lambda i: (0, 0)), block, block],
        out_specs=block,
        out_shape=jax.ShapeDtypeStruct((ROWS, D), BF),
        compiler_params=params(58),
        cost_estimate=cost(20 * ROWS * D, 8 * ROWS * D),
        name="rows_back",
    )(patches, gain, mine, other)


def split_kernel(rows_ref, one_ref, two_ref, three_ref, gain_ref, out_ref):
    gain = gain_ref[...]
    hi = gain.astype(BF).astype(F32)
    lo = gain - hi
    total = rows_ref[...].astype(F32)
    for ref in (one_ref, two_ref, three_ref):
        total = total + ref[...].astype(F32)
    total = total.astype(BF)
    for s in range(N_DP):
        out_ref[s, 0:OWN, :] = total[OWN * s : OWN * (s + 1)]
        out_ref[s, OWN:MSG, :] = jnp.zeros((MSG - OWN, COLS), BF)
        for k in range(D // TILE):
            cols = slice(TILE * k, TILE * (k + 1))
            out_ref[s, OWN : OWN + 1, cols] = hi[k : k + 1].astype(BF)
            out_ref[s, OWN + 1 : OWN + 2, cols] = lo[k : k + 1].astype(BF)


def split(rows, others, gain):
    return pl.pallas_call(
        split_kernel,
        in_specs=[VM] * 5,
        out_specs=VM,
        out_shape=jax.ShapeDtypeStruct((N_DP, MSG, COLS), BF),
        cost_estimate=cost(0, 4 * N_DP * MSG * COLS),
        compiler_params=params(12),
        name="split",
    )(rows, *others, gain)


def finish_kernel(msg_ref, out_ref, gain_ref):
    both = jnp.zeros((MSG, COLS), F32)
    for half in range(2):
        total = msg_ref[half].astype(F32)
        for chip in range(1, 4):
            total = total + msg_ref[2 * chip + half].astype(F32)
        both = both + total
        for a in range(3):
            start = D * a + HALF * half
            out_ref[:, start : start + HALF] = total[0:OWN, HALF * a : HALF * (a + 1)]
    total = both[OWN : OWN + 1, :D] + both[OWN + 1 : OWN + 2, :D]
    for k in range(D // TILE):
        gain_ref[k : k + 1, :] = total[:, TILE * k : TILE * (k + 1)]


def finish(messages):
    return pl.pallas_call(
        finish_kernel,
        in_specs=[VM],
        out_specs=[VM, VM],
        out_shape=[
            jax.ShapeDtypeStruct((OWN, 3 * D), F32),
            jax.ShapeDtypeStruct((D // TILE, TILE), F32),
        ],
        cost_estimate=cost(0, 6 * N_DP * MSG * COLS),
        compiler_params=params(12),
        name="finish",
    )(messages)


def ring_pairs(df, ds):
    pairs = []
    for d in range(N_DP):
        dx, dz = (ds, df) if d % 2 else (df, ds)
        for x in range(4):
            for z in range(4):
                src = 4 * ((x + dx) % 4) + (z + dz) % 4
                pairs.append((N_INNER * d + src, N_INNER * d + 4 * x + z))
    return pairs


def double_pairs(f_bits, s_bits):
    pairs = []
    for d in range(N_DP):
        x_bits, z_bits = (s_bits, f_bits) if d % 2 else (f_bits, s_bits)
        flip = 4 * x_bits + z_bits
        pairs += [(N_INNER * d + (m ^ flip), N_INNER * d + m) for m in range(N_INNER)]
    return pairs


def from_ring(value, df, ds):
    return lax.ppermute(value, ("dp", "inner"), ring_pairs(df, ds))


def swap_cores(value):
    return lax.ppermute(value, "dp", [(d ^ 1, d) for d in range(N_DP)])


def exchange(value, axis="dp"):
    return lax.all_to_all(value, axis, split_axis=0, concat_axis=0, tiled=True)


def on_device(patches, segments, owners, norm_gain, qkv_weight, cotangent):
    group = lax.axis_index("dp")
    inner = lax.axis_index("inner")
    core, x, z = group % 2, inner // 4, inner % 4
    gain = norm_gain.reshape(1, D)

    pos = jnp.arange(N_INNER)
    df, ds = pos % 4, pos // 4
    m = 4 * ((x + jnp.where(core == 0, df, ds)) % 4) + (
        z + jnp.where(core == 0, ds, df)
    ) % 4
    nat = (
        (jnp.arange(N_DP)[None, :, None] * N_INNER + m[:, None, None]) * OWN
        + jnp.arange(OWN)[None, None, :]
    ).reshape(1, D).astype(F32)

    messages = exchange(build(owners, qkv_weight, segments))
    partner_patches = swap_cores(patches)
    own_prep = prep(patches, gain, nat)
    strips = cotangent.reshape(TILES, N_DP, STRIP, D).transpose(1, 0, 2, 3)
    messages, own_prep, strips = lax.optimization_barrier((messages, own_prep, strips))
    block, seg, owners_all = compact(group.reshape(1).astype(jnp.int32), messages)
    strips = exchange(strips)

    owner_of = owners_all[:, :TILES].astype(jnp.int32).reshape(N_DP * TILES)
    u = jnp.arange(N_DP * TILES)
    earlier = (owner_of[:, None] == owner_of[None, :]) & (
        u[None, :] // TILES < u[:, None] // TILES
    )
    fwd = (TILES * owner_of + jnp.sum(earlier, axis=1)).astype(jnp.int32)
    wanted = fwd[None, :] == TILES * group + jnp.arange(TILES)[:, None]
    source = jnp.sum(jnp.where(wanted, u[None, :] // TILES, 0), axis=1)
    place_index = jnp.concatenate([2 * (source // 2), source % 2]).astype(jnp.int32)
    mine = jnp.arange(2)[:, None] ^ core
    tile = (TILES * (group - core + mine) + jnp.arange(TILES)[None, :]).reshape(-1)
    owner_here = jnp.sum(jnp.where(tile[:, None] == u[None, :], owner_of, 0), axis=1)
    slot_index = jnp.concatenate(
        [owner_here, jnp.broadcast_to(mine, (2, TILES)).reshape(-1)]
    ).astype(jnp.int32)

    heads = to_heads(fwd, strips.reshape(N_DP * TILES, STRIP, D))
    cot = exchange(heads)

    ring = [block] + [from_ring(block, f, 0) for f in (1, 2, 3)]
    near_a, near_b = jnp.concatenate(ring[:2]), jnp.concatenate(ring[2:])
    above_a, below_b = from_ring(near_a, 0, 1), from_ring(near_b, 0, -1)
    above_b, below_a = from_ring(near_b, 0, 1), from_ring(near_a, 0, -1)
    above_a, above_b, below_a, below_b = lax.optimization_barrier(
        (above_a, above_b, below_a, below_b)
    )
    far_a, far_b = from_ring(above_a, 0, 1), from_ring(below_b, 0, -1)
    pieces = [near_a, near_b, above_a, above_b, far_a, far_b, below_a, below_b]
    normed, normed_t = zip(own_prep, prep(partner_patches, gain, nat))

    out, dqkv, col_a, col_b, up_a, down_b, up, down, gain_part = main(
        slot_index, seg, normed, normed_t, cot, pieces
    )

    up, down = from_ring(up, 0, -1), from_ring(down, 0, 1)
    slots = exchange(out)
    gain_part = gain_back(gain_part, nat, gain)
    both = ("dp", "inner")
    gain_part = gain_part + lax.ppermute(gain_part, both, double_pairs(0, 1))
    gain_part = gain_part + lax.ppermute(gain_part, both, double_pairs(0, 3))
    partners = back(1, dqkv, pieces, nat)
    up, down, gain_part, partners = lax.optimization_barrier(
        (up, down, gain_part, partners)
    )
    other = swap_cores(partners)
    up_a, down_b = add([[(up_a, 0), (up, 0)], [(down_b, 0), (down, 0)]])
    from_up_a, from_down_b = from_ring(up_a, 0, -1), from_ring(down_b, 0, 1)
    dqkv, gain_part, _ = lax.optimization_barrier((dqkv, gain_part, up_a))
    mine = back(0, dqkv, pieces, nat)
    gain_part = gain_part + lax.ppermute(gain_part, both, double_pairs(1, 0))
    gain_part = gain_part + lax.ppermute(gain_part, both, double_pairs(3, 0))
    from_up_a, from_down_b, mine, gain_part = lax.optimization_barrier(
        (from_up_a, from_down_b, mine, gain_part)
    )
    zero, one, two, three = add(
        [
            [(col_a, 0), (from_up_a, 0), (down, PART)],
            [(col_b, 0), (up, PART), (from_down_b, 0)],
        ],
        2,
    )
    others = [from_ring(two, -2, 0), from_ring(three, 1, 0), from_ring(one, -1, 0)]
    others[0], slots = lax.optimization_barrier((others[0], slots))

    attended = place(place_index, slots).reshape(ROWS, D)
    grad_rows = rows_back(patches, gain, mine, other)
    grad_qkv, grad_gain = finish(exchange(split(zero, others, gain_part)))
    return (attended, grad_rows, grad_qkv, grad_gain.reshape(D))


def solution(mesh):
    both = ("dp", "inner")
    placed = (
        P(both, None),
        P(both, None),
        P(both),
        P(),
        P(both, None),
        P(both, None),
    )
    return jax.shard_map(
        on_device,
        mesh=mesh,
        in_specs=placed,
        out_specs=(P(both, None), P(both, None), P(both, None), P()),
        check_vma=False,
    )
```

profile of v0, /device:TPU:1, one launch (start us, length us, event | category | flops | bytes accessed | tf_op | source)
XLA Modules:
  0.0 174.0 jit_solution(5369192446593355840)
XLA Ops:
  4.3 6.0 %all-to-all-start = ((bf16[8,16,1920]{2,1,0:T(8,128)(2,1)}), bf16[8,16,1920]{2,1,0:T(8,128)(2,1)S(1)}, u32[]{:S(2)}, u32[]{:S(2)}) async-start(bf16[8,16,1920]{2,1,0:T(8,128)(2,1)} %build.1), calls=%async_computation | async-start | bytes 983040 | tf_op jit(solution)/shard_map/all_to_all | solution.py:668
  12.8 6.3 %prep.2 = (bf16[384,1280]{1,0:T(8,128)(2,1)}, bf16[1280,384]{1,0:T(8,128)(2,1)}) custom-call(bf16[384,1280]{1,0:T(8,128)(2,1)} %patches_ref.3, f32[1,1280]{1,0:T(1,128)} %reshape.232.gain_ref, f32[1,1280]{1,0:T(1,128)} %convert_element_type.12.nat_ref), custom_call_target="tpu_custom_call" | custom-call | flops 2516582 | bytes 2949 | tf_op jit(solution)/shard_map/prep/pallas_call | solution.py:82
  20.0 3.8 %collective-permute-start.1 = (bf16[80,1920]{1,0:T(8,128)(2,1)S(1)}, bf16[80,1920]{1,0:T(8,128)(2,1)S(1)}, u32[]{:S(2)}, u32[]{:S(2)}) collective-permute-start(bf16[80,1920]{1,0:T(8,128)(2,1)S(1)} %get-tuple-element.58), channel_id=1, source_target_pairs={{4,0},{5,1},{6,2},{7,3},{8,4},{9,5},{10,6},{11,7},{12,8},{13,9},{1... | collective-permute-start | bytes 921608 | tf_op jit(solution)/shard_map/ppermute | solution.py:660
  25.2 4.7 %all-to-all-start.1 = ((bf16[8,3,16,1280]{3,2,1,0:T(8,128)(2,1)}), bf16[8,3,16,1280]{3,2,1,0:T(8,128)(2,1)S(1)}, u32[]{:S(2)}, u32[]{:S(2)}) async-start(bf16[8,3,16,1280]{3,2,1,0:T(8,128)(2,1)} %bitcast.7), calls=%async_computation.1 | async-start | bytes 1966080 | tf_op jit(solution)/shard_map/all_to_all | solution.py:668
  37.4 6.8 %all-to-all-done.1 = bf16[8,3,16,1280]{3,2,1,0:T(8,128)(2,1)S(1)} async-done(((bf16[8,3,16,1280]{3,2,1,0:T(8,128)(2,1)}), bf16[8,3,16,1280]{3,2,1,0:T(8,128)(2,1)S(1)}, u32[]{:S(2)}, u32[]{:S(2)}) %all-to-all-start.1) | async-done | bytes 983072 | tf_op jit(solution)/shard_map/all_to_all | solution.py:668
  45.8 5.0 %all-to-all-start.2 = ((bf16[8,6,16,640]{3,2,1,0:T(8,128)(2,1)}), bf16[8,6,16,640]{3,2,1,0:T(8,128)(2,1)}, u32[]{:S(2)}, u32[]{:S(2)}) async-start(bf16[8,6,16,640]{3,2,1,0:T(8,128)(2,1)} %to_heads.1), calls=%async_computation.2 | async-start | bytes 1966080 | tf_op jit(solution)/shard_map/all_to_all | solution.py:668
  50.9 2.5 %collective-permute-start.8 = (bf16[160,1920]{1,0:T(8,128)(2,1)}, bf16[160,1920]{1,0:T(8,128)(2,1)S(1)}, u32[]{:S(2)}, u32[]{:S(2)}) collective-permute-start(bf16[160,1920]{1,0:T(8,128)(2,1)} %collective-permute-done.4.refs_2_), channel_id=1, source_target_pairs={{1,0},{2,1},{3,2},{0,3},{5,4},{6,5},{7,6},{4,7},{9,8},{10,9},{11,1... | collective-permute-start | bytes 1843208 | tf_op jit(solution)/shard_map/ppermute | solution.py:660
  54.5 6.3 %prep.3 = (bf16[384,1280]{1,0:T(8,128)(2,1)}, bf16[1280,384]{1,0:T(8,128)(2,1)}) custom-call(bf16[384,1280]{1,0:T(8,128)(2,1)} %collective-permute-done.patches_ref, f32[1,1280]{1,0:T(1,128)} %reshape.232.gain_ref, f32[1,1280]{1,0:T(1,128)} %convert_element_type.12.nat_ref), custom_call_target="tpu_custom_call" | custom-call | flops 2516582 | bytes 2949 | tf_op jit(solution)/shard_map/prep/pallas_call | solution.py:82
  60.8 3.4 %collective-permute-done.9.refs_5_ = bf16[160,1920]{1,0:T(8,128)(2,1)S(1)} collective-permute-done((bf16[160,1920]{1,0:T(8,128)(2,1)}, bf16[160,1920]{1,0:T(8,128)(2,1)S(1)}, u32[]{:S(2)}, u32[]{:S(2)}) %collective-permute-start.9) | collective-permute-done | bytes 614432 | tf_op jit(solution)/shard_map/ppermute | solution.py:660
  65.3 22.6 %main.1 = (bf16[8,2,128,640]{3,2,1,0:T(8,128)(2,1)}, bf16[768,1920]{1,0:T(8,128)(2,1)}, bf16[160,1920]{1,0:T(8,128)(2,1)}, bf16[160,1920]{1,0:T(8,128)(2,1)}, bf...) custom-call(s32[12]{0:T(128)} %pad_add_fusion.1.idx_ref, ...), custom_call_target="tpu_custom_call" | custom-call | flops 8000000 | bytes 20971 | tf_op jit(solution)/shard_map/main/pallas_call | solution.py:427
  88.0 7.0 %all-to-all-start.3 = ((bf16[8,2,128,640]{3,2,1,0:T(8,128)(2,1)}), bf16[8,2,128,640]{3,2,1,0:T(8,128)(2,1)S(1)}, u32[]{:S(2)}, u32[]{:S(2)}) async-start(bf16[8,2,128,640]{3,2,1,0:T(8,128)(2,1)} %get-tuple-element.81), calls=%async_computation.3 | async-start | bytes 5242880 | tf_op jit(solution)/shard_map/all_to_all | solution.py:668
  97.6 2.3 %gain.1 = f32[16,128]{1,0:T(8,128)S(1)} custom-call(f32[1280,128]{1,0:T(8,128)S(1)} %copy-done.1, f32[1,1280]{1,0:T(1,128)S(1)} %copy-done.6, f32[1,1280]{1,0:T(1,128)S(1)} %copy-done.7), custom_call_target="tpu_custom_call" | custom-call | bytes 655 | tf_op jit(solution)/shard_map/gain/pallas_call | solution.py:505
  100.3 12.3 %collective-permute-done.12 = f32[16,128]{1,0:T(8,128)S(1)} collective-permute-done((f32[16,128]{1,0:T(8,128)S(1)}, f32[16,128]{1,0:T(8,128)S(1)}, u32[]{:S(2)}, u32[]{:S(2)}) %collective-permute-start.12) | collective-permute-done | bytes 8224 | tf_op jit(solution)/shard_map/ppermute | solution.py:733
  112.6 8.6 %back.2 = bf16[384,1280]{1,0:T(8,128)(2,1)} custom-call(f32[1,1280]{1,0:T(1,128)} %convert_element_type.12.nat_ref, bf16[768,1920]{1,0:T(8,128)(2,1)} %get-tuple-element.75.dqkv_ref, bf16[160,1920]{1,0:T(8,128)(2,1)} %copy-done.12, bf16[160,1920]{1,0:T(8,128)(2,1)} %copy-done.13, bf16[160,1920]{1,0:T(8,128)(2,1)} %collective-permute-done.4.refs_2_, ...), custom_call_target="tpu_custom_call" | custom-call | flops 3145728 | bytes 15728 | tf_op jit(solution)/shard_map/back/pallas_call | solution.py:536
  123.6 2.7 %collective-permute-start.15 = (bf16[160,1920]{1,0:T(8,128)(2,1)}, bf16[160,1920]{1,0:T(8,128)(2,1)}, u32[]{:S(2)}, u32[]{:S(2)}) collective-permute-start(bf16[160,1920]{1,0:T(8,128)(2,1)} %get-tuple-element.73), channel_id=1, source_target_pairs={{1,0},{2,1},{3,2},{0,3},{5,4},{6,5},{7,6},{4,7},{9,8},{10,9},{11,1... | collective-permute-start | bytes 1843208 | tf_op jit(solution)/shard_map/ppermute | solution.py:660
  129.8 2.5 %collective-permute-start.17 = (f32[16,128]{1,0:T(8,128)S(1)}, f32[16,128]{1,0:T(8,128)S(1)}, u32[]{:S(2)}, u32[]{:S(2)}) collective-permute-start(f32[16,128]{1,0:T(8,128)S(1)} %add.214), channel_id=1, source_target_pairs={{12,0},{13,1},{14,2},{15,3},{8,4},{9,5},{10,6},{11,7},{4,8},{5,9},... | collective-permute-start | bytes 24584 | tf_op jit(solution)/shard_map/ppermute | solution.py:745
  132.3 8.5 %back.3.mine_ref = bf16[384,1280]{1,0:T(8,128)(2,1)} custom-call(f32[1,1280]{1,0:T(1,128)} %convert_element_type.12.nat_ref, bf16[768,1920]{1,0:T(8,128)(2,1)} %get-tuple-element.75.dqkv_ref, bf16[160,1920]{1,0:T(8,128)(2,1)} %copy-done.12, bf16[160,1920]{1,0:T(8,128)(2,1)} %copy-done.13, bf16[160,1920]{1,0:T(8,128)(2,1)} %collective-permute-done.4.refs_2_, ...), custom_call_target="tpu_custom_call" | custom-call | flops 3145728 | bytes 15728 | tf_op jit(solution)/shard_map/back/pallas_call | solution.py:536
  142.0 2.3 %add.256 = (bf16[80,1920]{1,0:T(8,128)(2,1)S(1)}, bf16[80,1920]{1,0:T(8,128)(2,1)}, bf16[80,1920]{1,0:T(8,128)(2,1)}, bf16[80,1920]{1,0:T(8,128)(2,1)}) custom-call(bf16[160,1920]{1,0:T(8,128)(2,1)S(1)} %copy-done.4, bf16[160,1920]{1,0:T(8,128)(2,1)} %collective-permute-done.14.refs_1_, bf16[320,1920]{1,0:T(8,128)(2,1)S(1)} %collective-permute-done.11.refs_3_.refs_2_, ...), custom_call_target="tpu_custom_call" | custom-call | bytes 7372 | tf_op jit(solution)/shard_map/add/pallas_call | solution.py:476
  146.6 5.4 %collective-permute-done.18.one_ref = bf16[80,1920]{1,0:T(8,128)(2,1)S(1)} collective-permute-done((bf16[80,1920]{1,0:T(8,128)(2,1)}, bf16[80,1920]{1,0:T(8,128)(2,1)S(1)}, u32[]{:S(2)}, u32[]{:S(2)}) %collective-permute-start.18) | collective-permute-done | bytes 307232 | tf_op jit(solution)/shard_map/ppermute | solution.py:660
  153.3 2.1 %collective-permute-done.21.three_ref = bf16[80,1920]{1,0:T(8,128)(2,1)} collective-permute-done((bf16[80,1920]{1,0:T(8,128)(2,1)}, bf16[80,1920]{1,0:T(8,128)(2,1)}, u32[]{:S(2)}, u32[]{:S(2)}) %collective-permute-start.21) | collective-permute-done | bytes 307232 | tf_op jit(solution)/shard_map/ppermute | solution.py:660
  157.6 6.6 %all-to-all-start.4 = ((bf16[8,16,1920]{2,1,0:T(8,128)(2,1)}), bf16[8,16,1920]{2,1,0:T(8,128)(2,1)S(1)}, u32[]{:S(2)}, u32[]{:S(2)}) async-start(bf16[8,16,1920]{2,1,0:T(8,128)(2,1)} %copy-done), calls=%async_computation.4 | async-start | bytes 983040 | tf_op jit(solution)/shard_map/all_to_all | solution.py:668
  165.1 4.2 %rows_back.1 = bf16[384,1280]{1,0:T(8,128)(2,1)} custom-call(bf16[384,1280]{1,0:T(8,128)(2,1)} %patches_ref.3, f32[1,1280]{1,0:T(1,128)} %reshape.232.gain_ref, bf16[384,1280]{1,0:T(8,128)(2,1)} %back.3.mine_ref, bf16[384,1280]{1,0:T(8,128)(2,1)} %collective-permute-done.19.other_ref), custom_call_target="tpu_custom_call" | custom-call | flops 9830 | bytes 3932 | tf_op jit(solution)/shard_map/rows_back/pallas_call | solution.py:568
  169.3 2.1 %place.1 = bf16[3,128,1280]{2,1,0:T(8,128)(2,1)} custom-call(s32[6]{0:T(128)S(1)} %pad_add_fusion.idx_ref, bf16[8,2,128,640]{3,2,1,0:T(8,128)(2,1)S(1)} %all-to-all-done.3.left_ref.right_ref, bf16[8,2,128,640]{3,2,1,0:T(8,128)(2,1)S(1)} %all-to-all-done.3.left_ref.right_ref), custom_call_target="tpu_custom_call" | custom-call | bytes 1966 | tf_op jit(solution)/shard_map/place/pallas_call | solution.py:193
  171.3 1.9 %all-to-all-done.4.msg_ref = bf16[8,16,1920]{2,1,0:T(8,128)(2,1)S(1)} async-done(((bf16[8,16,1920]{2,1,0:T(8,128)(2,1)}), bf16[8,16,1920]{2,1,0:T(8,128)(2,1)S(1)}, u32[]{:S(2)}, u32[]{:S(2)}) %all-to-all-start.4) | async-done | bytes 491552 | tf_op jit(solution)/shard_map/all_to_all | solution.py:668
  (117 shorter events, 37.3 us)
Async XLA Ops:
  4.3 15.1 %all-to-all-start = ((bf16[8,16,1920]{2,1,0:T(8,128)(2,1)}), bf16[8,16,1920]{2,1,0:T(8,128)(2,1)S(1)}, u32[]{:S(2)}, u32[]{:S(2)}) async-start(bf16[8,16,1920]{2,1,0:T(8,128)(2,1)} %build.1), calls=%async_computation | async-start | bytes 983040 | tf_op jit(solution)/shard_map/all_to_all | solution.py:668
  10.3 44.2 %collective-permute-start = (bf16[384,1280]{1,0:T(8,128)(2,1)}, bf16[384,1280]{1,0:T(8,128)(2,1)}, u32[]{:S(2)}, u32[]{:S(2)}) collective-permute-start(bf16[384,1280]{1,0:T(8,128)(2,1)} %patches_ref.3), channel_id=1, source_target_pairs={{16,0},{0,16},{48,32},{32,48},{80,64},{64,80},{112,96},{96,112},{1... | collective-permute-start | bytes 2949128 | tf_op jit(solution)/shard_map/ppermute | solution.py:664
  20.0 9.8 %collective-permute-start.1 = (bf16[80,1920]{1,0:T(8,128)(2,1)S(1)}, bf16[80,1920]{1,0:T(8,128)(2,1)S(1)}, u32[]{:S(2)}, u32[]{:S(2)}) collective-permute-start(bf16[80,1920]{1,0:T(8,128)(2,1)S(1)} %get-tuple-element.58), channel_id=1, source_target_pairs={{4,0},{5,1},{6,2},{7,3},{8,4},{9,5},{10,6},{11,7},{12,8},{13,9},{1... | collective-permute-start | bytes 921608 | tf_op jit(solution)/shard_map/ppermute | solution.py:660
  23.8 10.6 %collective-permute-start.3 = (bf16[80,1920]{1,0:T(8,128)(2,1)S(1)}, bf16[80,1920]{1,0:T(8,128)(2,1)S(1)}, u32[]{:S(2)}, u32[]{:S(2)}) collective-permute-start(bf16[80,1920]{1,0:T(8,128)(2,1)S(1)} %get-tuple-element.58), channel_id=1, source_target_pairs={{12,0},{13,1},{14,2},{15,3},{0,4},{1,5},{2,6},{3,7},{4,8},{5,9},{6... | collective-permute-start | bytes 921608 | tf_op jit(solution)/shard_map/ppermute | solution.py:660
  23.9 9.3 %collective-permute-start.2 = (bf16[80,1920]{1,0:T(8,128)(2,1)S(1)}, bf16[80,1920]{1,0:T(8,128)(2,1)}, u32[]{:S(2)}, u32[]{:S(2)}) collective-permute-start(bf16[80,1920]{1,0:T(8,128)(2,1)S(1)} %get-tuple-element.58), channel_id=1, source_target_pairs={{8,0},{9,1},{10,2},{11,3},{12,4},{13,5},{14,6},{15,7},{0,8},{1,9},... | collective-permute-start | bytes 921608 | tf_op jit(solution)/shard_map/ppermute | solution.py:660
  25.2 19.1 %all-to-all-start.1 = ((bf16[8,3,16,1280]{3,2,1,0:T(8,128)(2,1)}), bf16[8,3,16,1280]{3,2,1,0:T(8,128)(2,1)S(1)}, u32[]{:S(2)}, u32[]{:S(2)}) async-start(bf16[8,3,16,1280]{3,2,1,0:T(8,128)(2,1)} %bitcast.7), calls=%async_computation.1 | async-start | bytes 1966080 | tf_op jit(solution)/shard_map/all_to_all | solution.py:668
  29.9 20.9 %collective-permute-start.6 = (bf16[160,1920]{1,0:T(8,128)(2,1)S(1)}, bf16[160,1920]{1,0:T(8,128)(2,1)S(1)}, u32[]{:S(2)}, u32[]{:S(2)}) collective-permute-start(bf16[160,1920]{1,0:T(8,128)(2,1)S(1)} %constant_dynamic-update-slice_fusion.refs_0_), channel_id=1, source_target_pairs={{3,0},{0,1},{1,2},{2,3},{7,4},{4,5},{5,6},{6,7},{11,8},{8,9},{9,10... | collective-permute-start | bytes 1843208 | tf_op jit(solution)/shard_map/ppermute | solution.py:660
  31.5 19.3 %collective-permute-start.4 = (bf16[160,1920]{1,0:T(8,128)(2,1)S(1)}, bf16[160,1920]{1,0:T(8,128)(2,1)}, u32[]{:S(2)}, u32[]{:S(2)}) collective-permute-start(bf16[160,1920]{1,0:T(8,128)(2,1)S(1)} %constant_dynamic-update-slice_fusion.refs_0_), channel_id=1, source_target_pairs={{1,0},{2,1},{3,2},{0,3},{5,4},{6,5},{7,6},{4,7},{9,8},{10,9},{11,1... | collective-permute-start | bytes 1843208 | tf_op jit(solution)/shard_map/ppermute | solution.py:660
  34.4 16.4 %collective-permute-start.7 = (bf16[160,1920]{1,0:T(8,128)(2,1)S(1)}, bf16[160,1920]{1,0:T(8,128)(2,1)}, u32[]{:S(2)}, u32[]{:S(2)}) collective-permute-start(bf16[160,1920]{1,0:T(8,128)(2,1)S(1)} %constant_dynamic-update-slice_fusion.2.refs_1_), channel_id=1, source_target_pairs={{3,0},{0,1},{1,2},{2,3},{7,4},{4,5},{5,6},{6,7},{11,8},{8,9},{9,10... | collective-permute-start | bytes 1843208 | tf_op jit(solution)/shard_map/ppermute | solution.py:660
  35.4 15.4 %collective-permute-start.5 = (bf16[160,1920]{1,0:T(8,128)(2,1)S(1)}, bf16[160,1920]{1,0:T(8,128)(2,1)}, u32[]{:S(2)}, u32[]{:S(2)}) collective-permute-start(bf16[160,1920]{1,0:T(8,128)(2,1)S(1)} %constant_dynamic-update-slice_fusion.2.refs_1_), channel_id=1, source_target_pairs={{1,0},{2,1},{3,2},{0,3},{5,4},{6,5},{7,6},{4,7},{9,8},{10,9},{11,1... | collective-permute-start | bytes 1843208 | tf_op jit(solution)/shard_map/ppermute | solution.py:660
  45.8 19.5 %all-to-all-start.2 = ((bf16[8,6,16,640]{3,2,1,0:T(8,128)(2,1)}), bf16[8,6,16,640]{3,2,1,0:T(8,128)(2,1)}, u32[]{:S(2)}, u32[]{:S(2)}) async-start(bf16[8,6,16,640]{3,2,1,0:T(8,128)(2,1)} %to_heads.1), calls=%async_computation.2 | async-start | bytes 1966080 | tf_op jit(solution)/shard_map/all_to_all | solution.py:668
  50.9 9.9 %collective-permute-start.8 = (bf16[160,1920]{1,0:T(8,128)(2,1)}, bf16[160,1920]{1,0:T(8,128)(2,1)S(1)}, u32[]{:S(2)}, u32[]{:S(2)}) collective-permute-start(bf16[160,1920]{1,0:T(8,128)(2,1)} %collective-permute-done.4.refs_2_), channel_id=1, source_target_pairs={{1,0},{2,1},{3,2},{0,3},{5,4},{6,5},{7,6},{4,7},{9,8},{10,9},{11,1... | collective-permute-start | bytes 1843208 | tf_op jit(solution)/shard_map/ppermute | solution.py:660
  53.4 10.8 %collective-permute-start.9 = (bf16[160,1920]{1,0:T(8,128)(2,1)}, bf16[160,1920]{1,0:T(8,128)(2,1)S(1)}, u32[]{:S(2)}, u32[]{:S(2)}) collective-permute-start(bf16[160,1920]{1,0:T(8,128)(2,1)} %collective-permute-done.7.refs_7_), channel_id=1, source_target_pairs={{3,0},{0,1},{1,2},{2,3},{7,4},{4,5},{5,6},{6,7},{11,8},{8,9},{9,10... | collective-permute-start | bytes 1843208 | tf_op jit(solution)/shard_map/ppermute | solution.py:660
  88.0 64.1 %all-to-all-start.3 = ((bf16[8,2,128,640]{3,2,1,0:T(8,128)(2,1)}), bf16[8,2,128,640]{3,2,1,0:T(8,128)(2,1)S(1)}, u32[]{:S(2)}, u32[]{:S(2)}) async-start(bf16[8,2,128,640]{3,2,1,0:T(8,128)(2,1)} %get-tuple-element.81), calls=%async_computation.3 | async-start | bytes 5242880 | tf_op jit(solution)/shard_map/all_to_all | solution.py:668
  94.9 26.3 %collective-permute-start.10 = (bf16[320,1920]{1,0:T(8,128)(2,1)}, bf16[320,1920]{1,0:T(8,128)(2,1)S(1)}, u32[]{:S(2)}, u32[]{:S(2)}) collective-permute-start(bf16[320,1920]{1,0:T(8,128)(2,1)} %get-tuple-element.65), channel_id=1, source_target_pairs={{3,0},{0,1},{1,2},{2,3},{7,4},{4,5},{5,6},{6,7},{11,8},{8,9},{9,10... | collective-permute-start | bytes 3686408 | tf_op jit(solution)/shard_map/ppermute | solution.py:660
  96.4 24.8 %collective-permute-start.11 = (bf16[320,1920]{1,0:T(8,128)(2,1)}, bf16[320,1920]{1,0:T(8,128)(2,1)S(1)}, u32[]{:S(2)}, u32[]{:S(2)}) collective-permute-start(bf16[320,1920]{1,0:T(8,128)(2,1)} %get-tuple-element.66), channel_id=1, source_target_pairs={{1,0},{2,1},{3,2},{0,3},{5,4},{6,5},{7,6},{4,7},{9,8},{10,9},{11,1... | collective-permute-start | bytes 3686408 | tf_op jit(solution)/shard_map/ppermute | solution.py:660
  100.0 12.6 %collective-permute-start.12 = (f32[16,128]{1,0:T(8,128)S(1)}, f32[16,128]{1,0:T(8,128)S(1)}, u32[]{:S(2)}, u32[]{:S(2)}) collective-permute-start(f32[16,128]{1,0:T(8,128)S(1)} %gain.1), channel_id=1, source_target_pairs={{1,0},{0,1},{3,2},{2,3},{5,4},{4,5},{7,6},{6,7},{9,8},{8,9},{11,10... | collective-permute-start | bytes 24584 | tf_op jit(solution)/shard_map/ppermute | solution.py:733
  112.6 8.6 %collective-permute-start.13 = (f32[16,128]{1,0:T(8,128)S(1)}, f32[16,128]{1,0:T(8,128)S(1)}, u32[]{:S(2)}, u32[]{:S(2)}) collective-permute-start(f32[16,128]{1,0:T(8,128)S(1)} %add.212), channel_id=1, source_target_pairs={{3,0},{2,1},{1,2},{0,3},{7,4},{6,5},{5,6},{4,7},{11,8},{10,9},{9,1... | collective-permute-start | bytes 24584 | tf_op jit(solution)/shard_map/ppermute | solution.py:734
  123.6 17.2 %collective-permute-start.15 = (bf16[160,1920]{1,0:T(8,128)(2,1)}, bf16[160,1920]{1,0:T(8,128)(2,1)}, u32[]{:S(2)}, u32[]{:S(2)}) collective-permute-start(bf16[160,1920]{1,0:T(8,128)(2,1)} %get-tuple-element.73), channel_id=1, source_target_pairs={{1,0},{2,1},{3,2},{0,3},{5,4},{6,5},{7,6},{4,7},{9,8},{10,9},{11,1... | collective-permute-start | bytes 1843208 | tf_op jit(solution)/shard_map/ppermute | solution.py:660
  126.3 14.6 %collective-permute-start.14 = (bf16[160,1920]{1,0:T(8,128)(2,1)}, bf16[160,1920]{1,0:T(8,128)(2,1)}, u32[]{:S(2)}, u32[]{:S(2)}) collective-permute-start(bf16[160,1920]{1,0:T(8,128)(2,1)} %get-tuple-element.72), channel_id=1, source_target_pairs={{3,0},{0,1},{1,2},{2,3},{7,4},{4,5},{5,6},{6,7},{11,8},{8,9},{9,10... | collective-permute-start | bytes 1843208 | tf_op jit(solution)/shard_map/ppermute | solution.py:660
  126.3 38.8 %collective-permute-start.19 = (bf16[384,1280]{1,0:T(8,128)(2,1)}, bf16[384,1280]{1,0:T(8,128)(2,1)}, u32[]{:S(2)}, u32[]{:S(2)}) collective-permute-start(bf16[384,1280]{1,0:T(8,128)(2,1)} %back.2), channel_id=1, source_target_pairs={{16,0},{0,16},{48,32},{32,48},{80,64},{64,80},{112,96},{96,112},{1... | collective-permute-start | bytes 2949128 | tf_op jit(solution)/shard_map/ppermute | solution.py:664
  129.8 11.0 %collective-permute-start.17 = (f32[16,128]{1,0:T(8,128)S(1)}, f32[16,128]{1,0:T(8,128)S(1)}, u32[]{:S(2)}, u32[]{:S(2)}) collective-permute-start(f32[16,128]{1,0:T(8,128)S(1)} %add.214), channel_id=1, source_target_pairs={{12,0},{13,1},{14,2},{15,3},{8,4},{9,5},{10,6},{11,7},{4,8},{5,9},... | collective-permute-start | bytes 24584 | tf_op jit(solution)/shard_map/ppermute | solution.py:745
  146.1 9.3 %collective-permute-start.21 = (bf16[80,1920]{1,0:T(8,128)(2,1)}, bf16[80,1920]{1,0:T(8,128)(2,1)}, u32[]{:S(2)}, u32[]{:S(2)}) collective-permute-start(bf16[80,1920]{1,0:T(8,128)(2,1)} %get-tuple-element.88), channel_id=1, source_target_pairs={{12,0},{13,1},{14,2},{15,3},{0,4},{1,5},{2,6},{3,7},{4,8},{5,9},{6... | collective-permute-start | bytes 921608 | tf_op jit(solution)/shard_map/ppermute | solution.py:660
  157.6 15.7 %all-to-all-start.4 = ((bf16[8,16,1920]{2,1,0:T(8,128)(2,1)}), bf16[8,16,1920]{2,1,0:T(8,128)(2,1)S(1)}, u32[]{:S(2)}, u32[]{:S(2)}) async-start(bf16[8,16,1920]{2,1,0:T(8,128)(2,1)} %copy-done), calls=%async_computation.4 | async-start | bytes 983040 | tf_op jit(solution)/shard_map/all_to_all | solution.py:668
  (23 other events, 151.3 us)
where the time goes:
time: 175 us; the launch traced here: 174 us
  Pallas kernels  69.6 us (40%)
  starting transfers between devices  53.9 us (31%)
  waiting for transfers between devices  37.3 us (21%)
  local copies, waits for them, and re-layouts  9.53 us (5%)
  other arithmetic  2.69 us (2%)
    all_to_all x5, starting transfers between devices, exchange(): return lax.all_to_all(value, axis, split_axis=0, concat_axis=0, tiled=True)  29.2 us
    pallas_call x1, Pallas kernels, main(): pl.pallas_call(main_kernel, in_specs=[SM, VM] + [ANY] * (5 + PIECES), out...  22.6 us
    ppermute x16, starting transfers between devices, from_ring(): return lax.ppermute(value, ('dp', 'inner'), ring_pairs(df, ds))  20.3 us
    pallas_call x2, Pallas kernels, back(): pl.pallas_call(functools.partial(back_kernel, half), in_specs=[VM] + [ANY...  17.1 us
    ppermute x16, waiting for transfers between devices, from_ring(): return lax.ppermute(value, ('dp', 'inner'), ring_pairs(df, ds))  13 us
    pallas_call x2, Pallas kernels, prep(): pl.pallas_call(prep_kernel, in_specs=[VM] * 3, out_specs=[VM] * 2, out_sh...  12.6 us
    ppermute x1, waiting for transfers between devices, on_device(): gain_part = gain_part + lax.ppermute(gain_part, both, double_pairs(0, 1))  12.3 us
    all_to_all x5, waiting for transfers between devices, exchange(): return lax.all_to_all(value, axis, split_axis=0, concat_axis=0, tiled=True)  10.1 us
  transfers between devices with their start and end apart: 27, of which 12 were waited for; matrix products, arithmetic and copies ran while one was open for 4% of the time, Pallas kernels for 26%

commit v1 on v0

--- a/solution.py
+++ b/solution.py
@@ -22,6 +22,7 @@
 BLOCK = 80
 PART = 160
 PIECES = 8
+RIDE = 88
 STRIP = 16
 MSG = 16
 EPS = 1e-6
@@ -118,7 +119,7 @@
         out_specs=VM,
         out_shape=jax.ShapeDtypeStruct((N_DP, MSG, COLS), BF),
         cost_estimate=cost(0, 2 * N_DP * MSG * COLS),
-        compiler_params=params(12),
+        compiler_params=params(58),
         name="build",
     )(owners, weight, segments)
 
@@ -458,32 +459,59 @@
     )(index, seg, *normed, *normed_t, cot, *pieces)
 
 
-def add_kernel(counts, firsts, cuts, *refs):
-    outs, used = refs[sum(counts) :], 0
-    for n, count in enumerate(counts):
+def add_parts(counts, firsts, refs):
+    totals, used = [], 0
+    for count in counts:
         total = jnp.zeros((PART, COLS), F32)
         for k in range(used, used + count):
             total = total + refs[k][firsts[k] : firsts[k] + PART, :].astype(F32)
         used += count
-        size = PART // cuts
-        for k in range(cuts):
-            outs[cuts * n + k][...] = total[size * k : size * (k + 1)].astype(BF)
-
-
-def add(groups, cuts=1):
+        totals.append(total)
+    return totals
+
+
+def add_kernel(counts, firsts, *refs):
+    totals = add_parts(counts, firsts, refs)
+    for out_ref, total in zip(refs[sum(counts) :], totals):
+        out_ref[...] = total.astype(BF)
+
+
+def column_kernel(counts, firsts, gain_ref, other_ref, *refs):
+    gain = gain_ref[...] + other_ref[...]
+    outs = refs[sum(counts) :]
+    totals = add_parts(counts, firsts, refs)
+    for n, out_ref in enumerate(outs):
+        block = totals[n // 2][BLOCK * (n % 2) : BLOCK * (n % 2 + 1)]
+        out_ref[0:BLOCK, :] = block.astype(BF)
+        put_gain(gain, out_ref, BLOCK, RIDE)
+
+
+def put_gain(gain, ref, first, last):
+    hi = gain.astype(BF).astype(F32)
+    lo = gain - hi
+    ref[first:last, :] = jnp.zeros((last - first, COLS), BF)
+    for k in range(D // TILE):
+        cols = slice(TILE * k, TILE * (k + 1))
+        ref[first : first + 1, cols] = hi[k : k + 1].astype(BF)
+        ref[first + 1 : first + 2, cols] = lo[k : k + 1].astype(BF)
+
+
+def add(groups, gains=()):
     parts = [part for group in groups for part in group]
-    shape = jax.ShapeDtypeStruct((PART // cuts, COLS), BF)
+    rows, n = (RIDE, 2 * len(groups)) if gains else (PART, len(groups))
     return pl.pallas_call(
         functools.partial(
-            add_kernel, [len(group) for group in groups], [f for _, f in parts], cuts
+            column_kernel if gains else add_kernel,
+            [len(group) for group in groups],
+            [first for _, first in parts],
         ),
-        in_specs=[VM] * len(parts),
-        out_specs=[VM] * (cuts * len(groups)),
-        out_shape=[shape] * (cuts * len(groups)),
+        in_specs=[VM] * (len(gains) + len(parts)),
+        out_specs=[VM] * n,
+        out_shape=[jax.ShapeDtypeStruct((rows, COLS), BF)] * n,
         compiler_params=params(12),
         cost_estimate=cost(0, 4 * len(parts) * PART * COLS),
         name="add",
-    )(*[array for array, _ in parts])
+    )(*gains, *[array for array, _ in parts])
 
 
 def gain_kernel(part_ref, nat_ref, gain_ref, out_ref, perm_ref):
@@ -577,33 +605,31 @@
     )(patches, gain, mine, other)
 
 
-def split_kernel(rows_ref, one_ref, two_ref, three_ref, gain_ref, out_ref):
-    gain = gain_ref[...]
-    hi = gain.astype(BF).astype(F32)
-    lo = gain - hi
+def split_kernel(rows_ref, one_ref, two_ref, three_ref, out_ref):
     total = rows_ref[...].astype(F32)
     for ref in (one_ref, two_ref, three_ref):
         total = total + ref[...].astype(F32)
+    both = total[BLOCK : BLOCK + 1, :D] + total[BLOCK + 1 : BLOCK + 2, :D]
+    hi = both.astype(BF)
+    lo = (both - hi.astype(F32)).astype(BF)
     total = total.astype(BF)
     for s in range(N_DP):
         out_ref[s, 0:OWN, :] = total[OWN * s : OWN * (s + 1)]
         out_ref[s, OWN:MSG, :] = jnp.zeros((MSG - OWN, COLS), BF)
-        for k in range(D // TILE):
-            cols = slice(TILE * k, TILE * (k + 1))
-            out_ref[s, OWN : OWN + 1, cols] = hi[k : k + 1].astype(BF)
-            out_ref[s, OWN + 1 : OWN + 2, cols] = lo[k : k + 1].astype(BF)
-
-
-def split(rows, others, gain):
+        out_ref[s, OWN : OWN + 1, :D] = hi
+        out_ref[s, OWN + 1 : OWN + 2, :D] = lo
+
+
+def split(rows, others):
     return pl.pallas_call(
         split_kernel,
-        in_specs=[VM] * 5,
+        in_specs=[VM] * 4,
         out_specs=VM,
         out_shape=jax.ShapeDtypeStruct((N_DP, MSG, COLS), BF),
         cost_estimate=cost(0, 4 * N_DP * MSG * COLS),
         compiler_params=params(12),
         name="split",
-    )(rows, *others, gain)
+    )(rows, *others)
 
 
 def finish_kernel(msg_ref, out_ref, gain_ref):
@@ -729,36 +755,31 @@
     up, down = from_ring(up, 0, -1), from_ring(down, 0, 1)
     slots = exchange(out)
     gain_part = gain_back(gain_part, nat, gain)
-    both = ("dp", "inner")
-    gain_part = gain_part + lax.ppermute(gain_part, both, double_pairs(0, 1))
-    gain_part = gain_part + lax.ppermute(gain_part, both, double_pairs(0, 3))
+    gain_other = lax.ppermute(gain_part, ("dp", "inner"), double_pairs(0, 1))
     partners = back(1, dqkv, pieces, nat)
-    up, down, gain_part, partners = lax.optimization_barrier(
-        (up, down, gain_part, partners)
+    up, down, gain_part, gain_other, partners = lax.optimization_barrier(
+        (up, down, gain_part, gain_other, partners)
     )
     other = swap_cores(partners)
     up_a, down_b = add([[(up_a, 0), (up, 0)], [(down_b, 0), (down, 0)]])
     from_up_a, from_down_b = from_ring(up_a, 0, -1), from_ring(down_b, 0, 1)
-    dqkv, gain_part, _ = lax.optimization_barrier((dqkv, gain_part, up_a))
-    mine = back(0, dqkv, pieces, nat)
-    gain_part = gain_part + lax.ppermute(gain_part, both, double_pairs(1, 0))
-    gain_part = gain_part + lax.ppermute(gain_part, both, double_pairs(3, 0))
-    from_up_a, from_down_b, mine, gain_part = lax.optimization_barrier(
-        (from_up_a, from_down_b, mine, gain_part)
-    )
+    gain_part = gain_part + gain_other
+    gain_other = lax.ppermute(gain_part, ("dp", "inner"), double_pairs(0, 3))
     zero, one, two, three = add(
         [
             [(col_a, 0), (from_up_a, 0), (down, PART)],
             [(col_b, 0), (up, PART), (from_down_b, 0)],
         ],
-        2,
-    )
+        (gain_part, gain_other),
+    )
+    dqkv, _ = lax.optimization_barrier((dqkv, zero))
+    mine = back(0, dqkv, pieces, nat)
     others = [from_ring(two, -2, 0), from_ring(three, 1, 0), from_ring(one, -1, 0)]
-    others[0], slots = lax.optimization_barrier((others[0], slots))
+    others[0], slots, mine = lax.optimization_barrier((others[0], slots, mine))
 
     attended = place(place_index, slots).reshape(ROWS, D)
     grad_rows = rows_back(patches, gain, mine, other)
-    grad_qkv, grad_gain = finish(exchange(split(zero, others, gain_part)))
+    grad_qkv, grad_gain = finish(exchange(split(zero, others)))
     return (attended, grad_rows, grad_qkv, grad_gain.reshape(D))
 
 

time: 175 us -> 156 us (0.89)
  waiting for transfers between devices: 37.3 us -> 24.6 us
  local copies, waits for them, and re-layouts: 9.53 us -> 4.85 us
    ppermute x16, waiting for transfers between devices: 13 us -> 4.72 us  [from_ring(): return lax.ppermute(value, ('dp', 'inner'), ring_pairs(df, ds))]
    ppermute x4 -> x2, waiting for transfers between devices: 14.2 us -> 9 us  [the longest x1 5.6 us: on_device(): gain_other = lax.ppermute(gain_part, ('dp', 'inner'), double_pairs(0, 3))]
    unnamed x42 -> x32, local copies, waits for them, and re-layouts: 6.79 us -> 2.14 us
    ppermute x4 -> x2, starting transfers between devices: 3.98 us -> 1.9 us  [the longest x1 1.23 us: on_device(): gain_other = lax.ppermute(gain_part, ('dp', 'inner'), double_pairs(0, 3))]
  transfers between devices with their start and end apart: 27 -> 25, of which waited for: 12 -> 10; matrix products, arithmetic and copies ran while one was open for 4% -> 3% of each run, Pallas kernels for 26% -> 28%
where the time goes in v1:
time: 156 us
  Pallas kernels  69.6 us (45%)
  starting transfers between devices  54.2 us (35%)
  waiting for transfers between devices  24.6 us (16%)
  local copies, waits for them, and re-layouts  4.85 us (3%)
    all_to_all x5, starting transfers between devices, exchange(): return lax.all_to_all(value, axis, split_axis=0, concat_axis=0, tiled=True)  30 us
    pallas_call x1, Pallas kernels, main(): pl.pallas_call(main_kernel, in_specs=[SM, VM] + [ANY] * (5 + PIECES), out...  22.8 us
    ppermute x16, starting transfers between devices, from_ring(): return lax.ppermute(value, ('dp', 'inner'), ring_pairs(df, ds))  21.2 us
    pallas_call x2, Pallas kernels, back(): pl.pallas_call(functools.partial(back_kernel, half), in_specs=[VM] + [ANY...  17.1 us
    pallas_call x2, Pallas kernels, prep(): pl.pallas_call(prep_kernel, in_specs=[VM] * 3, out_specs=[VM] * 2, out_sh...  12.6 us
    all_to_all x5, waiting for transfers between devices, exchange(): return lax.all_to_all(value, axis, split_axis=0, concat_axis=0, tiled=True)  10.9 us
    ppermute x1, waiting for transfers between devices, on_device(): gain_other = lax.ppermute(gain_part, ('dp', 'inner'), double_pairs(0, 3))  5.6 us
    ppermute x16, waiting for transfers between devices, from_ring(): return lax.ppermute(value, ('dp', 'inner'), ring_pairs(df, ds))  4.72 us
  transfers between devices with their start and end apart: 25, of which 10 were waited for; matrix products, arithmetic and copies ran while one was open for 3% of the time, Pallas kernels for 28%

profile of v1, /device:TPU:1, one launch (start us, length us, event | category | flops | bytes accessed | tf_op | source)
XLA Modules:
  0.0 155.7 jit_solution(14847883816367524547)
XLA Ops:
  0.7 1.9 %build.1 = bf16[8,16,1920]{2,1,0:T(8,128)(2,1)} custom-call(s32[3]{0:T(128)} %own_ref.1, bf16[10,3840]{1,0:T(8,128)(2,1)} %w_ref.1, s32[3,128]{1,0:T(4,128)} %seg_ref.1), custom_call_target="tpu_custom_call" | custom-call | bytes 491 | tf_op jit(solution)/shard_map/build/pallas_call | solution.py:116
  2.5 6.0 %all-to-all-start = ((bf16[8,16,1920]{2,1,0:T(8,128)(2,1)}), bf16[8,16,1920]{2,1,0:T(8,128)(2,1)S(1)}, u32[]{:S(2)}, u32[]{:S(2)}) async-start(bf16[8,16,1920]{2,1,0:T(8,128)(2,1)} %build.1), calls=%async_computation | async-start | bytes 983040 | tf_op jit(solution)/shard_map/all_to_all | solution.py:694
  11.0 6.3 %prep.2 = (bf16[384,1280]{1,0:T(8,128)(2,1)}, bf16[1280,384]{1,0:T(8,128)(2,1)}) custom-call(bf16[384,1280]{1,0:T(8,128)(2,1)} %patches_ref.3, f32[1,1280]{1,0:T(1,128)} %reshape.232.gain_ref, f32[1,1280]{1,0:T(1,128)} %convert_element_type.12.nat_ref), custom_call_target="tpu_custom_call" | custom-call | flops 2516582 | bytes 2949 | tf_op jit(solution)/shard_map/prep/pallas_call | solution.py:83
  17.7 3.8 %collective-permute-start.1 = (bf16[80,1920]{1,0:T(8,128)(2,1)S(1)}, bf16[80,1920]{1,0:T(8,128)(2,1)S(1)}, u32[]{:S(2)}, u32[]{:S(2)}) collective-permute-start(bf16[80,1920]{1,0:T(8,128)(2,1)S(1)} %get-tuple-element.55), channel_id=1, source_target_pairs={{4,0},{5,1},{6,2},{7,3},{8,4},{9,5},{10,6},{11,7},{12,8},{13,9},{1... | collective-permute-start | bytes 921608 | tf_op jit(solution)/shard_map/ppermute | solution.py:686
  22.9 4.6 %all-to-all-start.1 = ((bf16[8,3,16,1280]{3,2,1,0:T(8,128)(2,1)}), bf16[8,3,16,1280]{3,2,1,0:T(8,128)(2,1)S(1)}, u32[]{:S(2)}, u32[]{:S(2)}) async-start(bf16[8,3,16,1280]{3,2,1,0:T(8,128)(2,1)} %bitcast.7), calls=%async_computation.1 | async-start | bytes 1966080 | tf_op jit(solution)/shard_map/all_to_all | solution.py:694
  35.1 6.8 %all-to-all-done.1 = bf16[8,3,16,1280]{3,2,1,0:T(8,128)(2,1)S(1)} async-done(((bf16[8,3,16,1280]{3,2,1,0:T(8,128)(2,1)}), bf16[8,3,16,1280]{3,2,1,0:T(8,128)(2,1)S(1)}, u32[]{:S(2)}, u32[]{:S(2)}) %all-to-all-start.1) | async-done | bytes 983072 | tf_op jit(solution)/shard_map/all_to_all | solution.py:694
  43.5 5.0 %all-to-all-start.2 = ((bf16[8,6,16,640]{3,2,1,0:T(8,128)(2,1)}), bf16[8,6,16,640]{3,2,1,0:T(8,128)(2,1)}, u32[]{:S(2)}, u32[]{:S(2)}) async-start(bf16[8,6,16,640]{3,2,1,0:T(8,128)(2,1)} %to_heads.1), calls=%async_computation.2 | async-start | bytes 1966080 | tf_op jit(solution)/shard_map/all_to_all | solution.py:694
  48.5 2.5 %collective-permute-start.8 = (bf16[160,1920]{1,0:T(8,128)(2,1)}, bf16[160,1920]{1,0:T(8,128)(2,1)S(1)}, u32[]{:S(2)}, u32[]{:S(2)}) collective-permute-start(bf16[160,1920]{1,0:T(8,128)(2,1)} %collective-permute-done.4.refs_2_), channel_id=1, source_target_pairs={{1,0},{2,1},{3,2},{0,3},{5,4},{6,5},{7,6},{4,7},{9,8},{10,9},{11,1... | collective-permute-start | bytes 1843208 | tf_op jit(solution)/shard_map/ppermute | solution.py:686
  52.1 6.3 %prep.3 = (bf16[384,1280]{1,0:T(8,128)(2,1)}, bf16[1280,384]{1,0:T(8,128)(2,1)}) custom-call(bf16[384,1280]{1,0:T(8,128)(2,1)} %collective-permute-done.patches_ref, f32[1,1280]{1,0:T(1,128)} %reshape.232.gain_ref, f32[1,1280]{1,0:T(1,128)} %convert_element_type.12.nat_ref), custom_call_target="tpu_custom_call" | custom-call | flops 2516582 | bytes 2949 | tf_op jit(solution)/shard_map/prep/pallas_call | solution.py:83
  58.4 3.4 %collective-permute-done.9.refs_5_ = bf16[160,1920]{1,0:T(8,128)(2,1)S(1)} collective-permute-done((bf16[160,1920]{1,0:T(8,128)(2,1)}, bf16[160,1920]{1,0:T(8,128)(2,1)S(1)}, u32[]{:S(2)}, u32[]{:S(2)}) %collective-permute-start.9) | collective-permute-done | bytes 614432 | tf_op jit(solution)/shard_map/ppermute | solution.py:686
  63.0 22.8 %main.1 = (bf16[8,2,128,640]{3,2,1,0:T(8,128)(2,1)}, bf16[768,1920]{1,0:T(8,128)(2,1)}, bf16[160,1920]{1,0:T(8,128)(2,1)}, bf16[160,1920]{1,0:T(8,128)(2,1)}, bf...) custom-call(s32[12]{0:T(128)} %pad_add_fusion.1.idx_ref, ...), custom_call_target="tpu_custom_call" | custom-call | flops 8000000 | bytes 20971 | tf_op jit(solution)/shard_map/main/pallas_call | solution.py:428
  85.8 6.9 %all-to-all-start.3 = ((bf16[8,2,128,640]{3,2,1,0:T(8,128)(2,1)}), bf16[8,2,128,640]{3,2,1,0:T(8,128)(2,1)S(1)}, u32[]{:S(2)}, u32[]{:S(2)}) async-start(bf16[8,2,128,640]{3,2,1,0:T(8,128)(2,1)} %get-tuple-element.75), calls=%async_computation.3 | async-start | bytes 5242880 | tf_op jit(solution)/shard_map/all_to_all | solution.py:694
  95.4 2.3 %gain.1 = f32[16,128]{1,0:T(8,128)S(1)} custom-call(f32[1280,128]{1,0:T(8,128)S(1)} %copy-done, f32[1,1280]{1,0:T(1,128)S(1)} %copy-done.5, f32[1,1280]{1,0:T(1,128)S(1)} %copy-done.6), custom_call_target="tpu_custom_call" | custom-call | bytes 655 | tf_op jit(solution)/shard_map/gain/pallas_call | solution.py:533
  98.5 8.6 %back.2 = bf16[384,1280]{1,0:T(8,128)(2,1)} custom-call(f32[1,1280]{1,0:T(1,128)} %convert_element_type.12.nat_ref, bf16[768,1920]{1,0:T(8,128)(2,1)} %get-tuple-element.77.dqkv_ref, bf16[160,1920]{1,0:T(8,128)(2,1)} %copy-done.8, bf16[160,1920]{1,0:T(8,128)(2,1)} %copy-done.9, bf16[160,1920]{1,0:T(8,128)(2,1)} %collective-permute-done.4.refs_2_, ...), custom_call_target="tpu_custom_call" | custom-call | flops 3145728 | bytes 15728 | tf_op jit(solution)/shard_map/back/pallas_call | solution.py:564
  107.1 3.4 %collective-permute-done.12 = f32[16,128]{1,0:T(8,128)S(1)} collective-permute-done((f32[16,128]{1,0:T(8,128)S(1)}, f32[16,128]{1,0:T(8,128)S(1)}, u32[]{:S(2)}, u32[]{:S(2)}) %collective-permute-start.12) | collective-permute-done | bytes 8224 | tf_op jit(solution)/shard_map/ppermute | solution.py:758
  111.9 2.7 %collective-permute-start.15 = (bf16[160,1920]{1,0:T(8,128)(2,1)S(1)}, bf16[160,1920]{1,0:T(8,128)(2,1)S(1)}, u32[]{:S(2)}, u32[]{:S(2)}) collective-permute-start(bf16[160,1920]{1,0:T(8,128)(2,1)S(1)} %get-tuple-element.73), channel_id=1, source_target_pairs={{1,0},{2,1},{3,2},{0,3},{5,4},{6,5},{7,6},{4,7},{9,8},{10,9},{11,1... | collective-permute-start | bytes 1843208 | tf_op jit(solution)/shard_map/ppermute | solution.py:686
  116.9 5.6 %collective-permute-done.13.other_ref = f32[16,128]{1,0:T(8,128)S(1)} collective-permute-done((f32[16,128]{1,0:T(8,128)S(1)}, f32[16,128]{1,0:T(8,128)S(1)}, u32[]{:S(2)}, u32[]{:S(2)}) %collective-permute-start.13) | collective-permute-done | bytes 8224 | tf_op jit(solution)/shard_map/ppermute | solution.py:767
  122.5 1.8 %add.244 = (bf16[88,1920]{1,0:T(8,128)(2,1)S(1)}, bf16[88,1920]{1,0:T(8,128)(2,1)}, bf16[88,1920]{1,0:T(8,128)(2,1)}, bf16[88,1920]{1,0:T(8,128)(2,1)}) custom-call(f32[16,128]{1,0:T(8,128)S(1)} %add.203.gain_ref, f32[16,128]{1,0:T(8,128)S(1)} %collective-permute-done.13.other_ref, bf16[160,1920]{1,0:T(8,128)(2,1)S(1)} %copy-done.3, ...), custom_call_target="tpu_custom_call" | custom-call | bytes 7372 | tf_op jit(solution)/shard_map/add/pallas_call | solution.py:502
  127.0 8.5 %back.3.mine_ref = bf16[384,1280]{1,0:T(8,128)(2,1)} custom-call(f32[1,1280]{1,0:T(1,128)} %convert_element_type.12.nat_ref, bf16[768,1920]{1,0:T(8,128)(2,1)} %get-tuple-element.77.dqkv_ref, bf16[160,1920]{1,0:T(8,128)(2,1)} %copy-done.8, bf16[160,1920]{1,0:T(8,128)(2,1)} %copy-done.9, bf16[160,1920]{1,0:T(8,128)(2,1)} %collective-permute-done.4.refs_2_, ...), custom_call_target="tpu_custom_call" | custom-call | flops 3145728 | bytes 15728 | tf_op jit(solution)/shard_map/back/pallas_call | solution.py:564
  136.1 2.2 %split.1 = bf16[8,16,1920]{2,1,0:T(8,128)(2,1)} custom-call(bf16[88,1920]{1,0:T(8,128)(2,1)S(1)} %get-tuple-element.76.rows_ref, bf16[88,1920]{1,0:T(8,128)(2,1)S(1)} %collective-permute-done.16.one_ref, bf16[88,1920]{1,0:T(8,128)(2,1)} %collective-permute-done.18.two_ref, bf16[88,1920]{1,0:T(8,128)(2,1)} %collective-permute-done.19.three_ref), custom_call_target="tpu_custom_call" | custom-call | bytes 983 | tf_op jit(solution)/shard_map/split/pallas_call | solution.py:624
  138.3 7.5 %all-to-all-start.4 = ((bf16[8,16,1920]{2,1,0:T(8,128)(2,1)}), bf16[8,16,1920]{2,1,0:T(8,128)(2,1)S(1)}, u32[]{:S(2)}, u32[]{:S(2)}) async-start(bf16[8,16,1920]{2,1,0:T(8,128)(2,1)} %split.1), calls=%async_computation.4 | async-start | bytes 983040 | tf_op jit(solution)/shard_map/all_to_all | solution.py:694
  146.1 4.2 %rows_back.1 = bf16[384,1280]{1,0:T(8,128)(2,1)} custom-call(bf16[384,1280]{1,0:T(8,128)(2,1)} %patches_ref.3, f32[1,1280]{1,0:T(1,128)} %reshape.232.gain_ref, bf16[384,1280]{1,0:T(8,128)(2,1)} %back.3.mine_ref, bf16[384,1280]{1,0:T(8,128)(2,1)} %collective-permute-done.17.other_ref), custom_call_target="tpu_custom_call" | custom-call | flops 9830 | bytes 3932 | tf_op jit(solution)/shard_map/rows_back/pallas_call | solution.py:596
  150.3 2.1 %place.1 = bf16[3,128,1280]{2,1,0:T(8,128)(2,1)} custom-call(s32[6]{0:T(128)S(1)} %pad_add_fusion.idx_ref, bf16[8,2,128,640]{3,2,1,0:T(8,128)(2,1)S(1)} %all-to-all-done.3.left_ref.right_ref, bf16[8,2,128,640]{3,2,1,0:T(8,128)(2,1)S(1)} %all-to-all-done.3.left_ref.right_ref), custom_call_target="tpu_custom_call" | custom-call | bytes 1966 | tf_op jit(solution)/shard_map/place/pallas_call | solution.py:194
  152.3 2.6 %all-to-all-done.4.msg_ref = bf16[8,16,1920]{2,1,0:T(8,128)(2,1)S(1)} async-done(((bf16[8,16,1920]{2,1,0:T(8,128)(2,1)}), bf16[8,16,1920]{2,1,0:T(8,128)(2,1)S(1)}, u32[]{:S(2)}, u32[]{:S(2)}) %all-to-all-start.4) | async-done | bytes 491552 | tf_op jit(solution)/shard_map/all_to_all | solution.py:694
  (100 shorter events, 27.0 us)
Async XLA Ops:
  2.5 15.1 %all-to-all-start = ((bf16[8,16,1920]{2,1,0:T(8,128)(2,1)}), bf16[8,16,1920]{2,1,0:T(8,128)(2,1)S(1)}, u32[]{:S(2)}, u32[]{:S(2)}) async-start(bf16[8,16,1920]{2,1,0:T(8,128)(2,1)} %build.1), calls=%async_computation | async-start | bytes 983040 | tf_op jit(solution)/shard_map/all_to_all | solution.py:694
  8.5 43.7 %collective-permute-start = (bf16[384,1280]{1,0:T(8,128)(2,1)}, bf16[384,1280]{1,0:T(8,128)(2,1)}, u32[]{:S(2)}, u32[]{:S(2)}) collective-permute-start(bf16[384,1280]{1,0:T(8,128)(2,1)} %patches_ref.3), channel_id=1, source_target_pairs={{16,0},{0,16},{48,32},{32,48},{80,64},{64,80},{112,96},{96,112},{1... | collective-permute-start | bytes 2949128 | tf_op jit(solution)/shard_map/ppermute | solution.py:690
  17.7 9.8 %collective-permute-start.1 = (bf16[80,1920]{1,0:T(8,128)(2,1)S(1)}, bf16[80,1920]{1,0:T(8,128)(2,1)S(1)}, u32[]{:S(2)}, u32[]{:S(2)}) collective-permute-start(bf16[80,1920]{1,0:T(8,128)(2,1)S(1)} %get-tuple-element.55), channel_id=1, source_target_pairs={{4,0},{5,1},{6,2},{7,3},{8,4},{9,5},{10,6},{11,7},{12,8},{13,9},{1... | collective-permute-start | bytes 921608 | tf_op jit(solution)/shard_map/ppermute | solution.py:686
  21.5 10.5 %collective-permute-start.3 = (bf16[80,1920]{1,0:T(8,128)(2,1)S(1)}, bf16[80,1920]{1,0:T(8,128)(2,1)S(1)}, u32[]{:S(2)}, u32[]{:S(2)}) collective-permute-start(bf16[80,1920]{1,0:T(8,128)(2,1)S(1)} %get-tuple-element.55), channel_id=1, source_target_pairs={{12,0},{13,1},{14,2},{15,3},{0,4},{1,5},{2,6},{3,7},{4,8},{5,9},{6... | collective-permute-start | bytes 921608 | tf_op jit(solution)/shard_map/ppermute | solution.py:686
  21.5 9.3 %collective-permute-start.2 = (bf16[80,1920]{1,0:T(8,128)(2,1)S(1)}, bf16[80,1920]{1,0:T(8,128)(2,1)}, u32[]{:S(2)}, u32[]{:S(2)}) collective-permute-start(bf16[80,1920]{1,0:T(8,128)(2,1)S(1)} %get-tuple-element.55), channel_id=1, source_target_pairs={{8,0},{9,1},{10,2},{11,3},{12,4},{13,5},{14,6},{15,7},{0,8},{1,9},... | collective-permute-start | bytes 921608 | tf_op jit(solution)/shard_map/ppermute | solution.py:686
  22.9 19.0 %all-to-all-start.1 = ((bf16[8,3,16,1280]{3,2,1,0:T(8,128)(2,1)}), bf16[8,3,16,1280]{3,2,1,0:T(8,128)(2,1)S(1)}, u32[]{:S(2)}, u32[]{:S(2)}) async-start(bf16[8,3,16,1280]{3,2,1,0:T(8,128)(2,1)} %bitcast.7), calls=%async_computation.1 | async-start | bytes 1966080 | tf_op jit(solution)/shard_map/all_to_all | solution.py:694
  27.6 20.9 %collective-permute-start.6 = (bf16[160,1920]{1,0:T(8,128)(2,1)S(1)}, bf16[160,1920]{1,0:T(8,128)(2,1)S(1)}, u32[]{:S(2)}, u32[]{:S(2)}) collective-permute-start(bf16[160,1920]{1,0:T(8,128)(2,1)S(1)} %constant_dynamic-update-slice_fusion.refs_0_), channel_id=1, source_target_pairs={{3,0},{0,1},{1,2},{2,3},{7,4},{4,5},{5,6},{6,7},{11,8},{8,9},{9,10... | collective-permute-start | bytes 1843208 | tf_op jit(solution)/shard_map/ppermute | solution.py:686
  29.1 19.3 %collective-permute-start.4 = (bf16[160,1920]{1,0:T(8,128)(2,1)S(1)}, bf16[160,1920]{1,0:T(8,128)(2,1)}, u32[]{:S(2)}, u32[]{:S(2)}) collective-permute-start(bf16[160,1920]{1,0:T(8,128)(2,1)S(1)} %constant_dynamic-update-slice_fusion.refs_0_), channel_id=1, source_target_pairs={{1,0},{2,1},{3,2},{0,3},{5,4},{6,5},{7,6},{4,7},{9,8},{10,9},{11,1... | collective-permute-start | bytes 1843208 | tf_op jit(solution)/shard_map/ppermute | solution.py:686
  32.1 16.4 %collective-permute-start.7 = (bf16[160,1920]{1,0:T(8,128)(2,1)S(1)}, bf16[160,1920]{1,0:T(8,128)(2,1)}, u32[]{:S(2)}, u32[]{:S(2)}) collective-permute-start(bf16[160,1920]{1,0:T(8,128)(2,1)S(1)} %constant_dynamic-update-slice_fusion.2.refs_1_), channel_id=1, source_target_pairs={{3,0},{0,1},{1,2},{2,3},{7,4},{4,5},{5,6},{6,7},{11,8},{8,9},{9,10... | collective-permute-start | bytes 1843208 | tf_op jit(solution)/shard_map/ppermute | solution.py:686
  33.1 15.5 %collective-permute-start.5 = (bf16[160,1920]{1,0:T(8,128)(2,1)S(1)}, bf16[160,1920]{1,0:T(8,128)(2,1)}, u32[]{:S(2)}, u32[]{:S(2)}) collective-permute-start(bf16[160,1920]{1,0:T(8,128)(2,1)S(1)} %constant_dynamic-update-slice_fusion.2.refs_1_), channel_id=1, source_target_pairs={{1,0},{2,1},{3,2},{0,3},{5,4},{6,5},{7,6},{4,7},{9,8},{10,9},{11,1... | collective-permute-start | bytes 1843208 | tf_op jit(solution)/shard_map/ppermute | solution.py:686
  43.5 19.5 %all-to-all-start.2 = ((bf16[8,6,16,640]{3,2,1,0:T(8,128)(2,1)}), bf16[8,6,16,640]{3,2,1,0:T(8,128)(2,1)}, u32[]{:S(2)}, u32[]{:S(2)}) async-start(bf16[8,6,16,640]{3,2,1,0:T(8,128)(2,1)} %to_heads.1), calls=%async_computation.2 | async-start | bytes 1966080 | tf_op jit(solution)/shard_map/all_to_all | solution.py:694
  48.5 9.9 %collective-permute-start.8 = (bf16[160,1920]{1,0:T(8,128)(2,1)}, bf16[160,1920]{1,0:T(8,128)(2,1)S(1)}, u32[]{:S(2)}, u32[]{:S(2)}) collective-permute-start(bf16[160,1920]{1,0:T(8,128)(2,1)} %collective-permute-done.4.refs_2_), channel_id=1, source_target_pairs={{1,0},{2,1},{3,2},{0,3},{5,4},{6,5},{7,6},{4,7},{9,8},{10,9},{11,1... | collective-permute-start | bytes 1843208 | tf_op jit(solution)/shard_map/ppermute | solution.py:686
  51.0 10.8 %collective-permute-start.9 = (bf16[160,1920]{1,0:T(8,128)(2,1)}, bf16[160,1920]{1,0:T(8,128)(2,1)S(1)}, u32[]{:S(2)}, u32[]{:S(2)}) collective-permute-start(bf16[160,1920]{1,0:T(8,128)(2,1)} %collective-permute-done.7.refs_7_), channel_id=1, source_target_pairs={{3,0},{0,1},{1,2},{2,3},{7,4},{4,5},{5,6},{6,7},{11,8},{8,9},{9,10... | collective-permute-start | bytes 1843208 | tf_op jit(solution)/shard_map/ppermute | solution.py:686
  85.8 49.7 %all-to-all-start.3 = ((bf16[8,2,128,640]{3,2,1,0:T(8,128)(2,1)}), bf16[8,2,128,640]{3,2,1,0:T(8,128)(2,1)S(1)}, u32[]{:S(2)}, u32[]{:S(2)}) async-start(bf16[8,2,128,640]{3,2,1,0:T(8,128)(2,1)} %get-tuple-element.75), calls=%async_computation.3 | async-start | bytes 5242880 | tf_op jit(solution)/shard_map/all_to_all | solution.py:694
  92.8 17.7 %collective-permute-start.10 = (bf16[320,1920]{1,0:T(8,128)(2,1)}, bf16[320,1920]{1,0:T(8,128)(2,1)S(1)}, u32[]{:S(2)}, u32[]{:S(2)}) collective-permute-start(bf16[320,1920]{1,0:T(8,128)(2,1)} %get-tuple-element.60), channel_id=1, source_target_pairs={{3,0},{0,1},{1,2},{2,3},{7,4},{4,5},{5,6},{6,7},{11,8},{8,9},{9,10... | collective-permute-start | bytes 3686408 | tf_op jit(solution)/shard_map/ppermute | solution.py:686
  94.3 16.2 %collective-permute-start.11 = (bf16[320,1920]{1,0:T(8,128)(2,1)}, bf16[320,1920]{1,0:T(8,128)(2,1)S(1)}, u32[]{:S(2)}, u32[]{:S(2)}) collective-permute-start(bf16[320,1920]{1,0:T(8,128)(2,1)} %get-tuple-element.61), channel_id=1, source_target_pairs={{1,0},{2,1},{3,2},{0,3},{5,4},{6,5},{7,6},{4,7},{9,8},{10,9},{11,1... | collective-permute-start | bytes 3686408 | tf_op jit(solution)/shard_map/ppermute | solution.py:686
  97.8 12.7 %collective-permute-start.12 = (f32[16,128]{1,0:T(8,128)S(1)}, f32[16,128]{1,0:T(8,128)S(1)}, u32[]{:S(2)}, u32[]{:S(2)}) collective-permute-start(f32[16,128]{1,0:T(8,128)S(1)} %gain.1), channel_id=1, source_target_pairs={{1,0},{0,1},{3,2},{2,3},{5,4},{4,5},{7,6},{6,7},{9,8},{8,9},{11,10... | collective-permute-start | bytes 24584 | tf_op jit(solution)/shard_map/ppermute | solution.py:758
  111.9 10.7 %collective-permute-start.14 = (bf16[160,1920]{1,0:T(8,128)(2,1)S(1)}, bf16[160,1920]{1,0:T(8,128)(2,1)S(1)}, u32[]{:S(2)}, u32[]{:S(2)}) collective-permute-start(bf16[160,1920]{1,0:T(8,128)(2,1)S(1)} %get-tuple-element.71), channel_id=1, source_target_pairs={{3,0},{0,1},{1,2},{2,3},{7,4},{4,5},{5,6},{6,7},{11,8},{8,9},{9,10... | collective-permute-start | bytes 1843208 | tf_op jit(solution)/shard_map/ppermute | solution.py:686
  111.9 10.6 %collective-permute-start.15 = (bf16[160,1920]{1,0:T(8,128)(2,1)S(1)}, bf16[160,1920]{1,0:T(8,128)(2,1)S(1)}, u32[]{:S(2)}, u32[]{:S(2)}) collective-permute-start(bf16[160,1920]{1,0:T(8,128)(2,1)S(1)} %get-tuple-element.73), channel_id=1, source_target_pairs={{1,0},{2,1},{3,2},{0,3},{5,4},{6,5},{7,6},{4,7},{9,8},{10,9},{11,1... | collective-permute-start | bytes 1843208 | tf_op jit(solution)/shard_map/ppermute | solution.py:686
  114.6 31.5 %collective-permute-start.17 = (bf16[384,1280]{1,0:T(8,128)(2,1)}, bf16[384,1280]{1,0:T(8,128)(2,1)}, u32[]{:S(2)}, u32[]{:S(2)}) collective-permute-start(bf16[384,1280]{1,0:T(8,128)(2,1)} %back.2), channel_id=1, source_target_pairs={{16,0},{0,16},{48,32},{32,48},{80,64},{64,80},{112,96},{96,112},{1... | collective-permute-start | bytes 2949128 | tf_op jit(solution)/shard_map/ppermute | solution.py:690
  124.3 11.2 %collective-permute-start.16 = (bf16[88,1920]{1,0:T(8,128)(2,1)}, bf16[88,1920]{1,0:T(8,128)(2,1)S(1)}, u32[]{:S(2)}, u32[]{:S(2)}) collective-permute-start(bf16[88,1920]{1,0:T(8,128)(2,1)} %get-tuple-element.74), channel_id=1, source_target_pairs={{8,0},{9,1},{10,2},{11,3},{12,4},{13,5},{14,6},{15,7},{0,8},{1,9},... | collective-permute-start | bytes 1013768 | tf_op jit(solution)/shard_map/ppermute | solution.py:686
  125.5 10.0 %collective-permute-start.18 = (bf16[88,1920]{1,0:T(8,128)(2,1)}, bf16[88,1920]{1,0:T(8,128)(2,1)}, u32[]{:S(2)}, u32[]{:S(2)}) collective-permute-start(bf16[88,1920]{1,0:T(8,128)(2,1)} %get-tuple-element.82), channel_id=1, source_target_pairs={{4,0},{5,1},{6,2},{7,3},{8,4},{9,5},{10,6},{11,7},{12,8},{13,9},{1... | collective-permute-start | bytes 1013768 | tf_op jit(solution)/shard_map/ppermute | solution.py:686
  125.9 10.2 %collective-permute-start.19 = (bf16[88,1920]{1,0:T(8,128)(2,1)}, bf16[88,1920]{1,0:T(8,128)(2,1)}, u32[]{:S(2)}, u32[]{:S(2)}) collective-permute-start(bf16[88,1920]{1,0:T(8,128)(2,1)} %get-tuple-element.83), channel_id=1, source_target_pairs={{12,0},{13,1},{14,2},{15,3},{0,4},{1,5},{2,6},{3,7},{4,8},{5,9},{6... | collective-permute-start | bytes 1013768 | tf_op jit(solution)/shard_map/ppermute | solution.py:686
  138.3 16.7 %all-to-all-start.4 = ((bf16[8,16,1920]{2,1,0:T(8,128)(2,1)}), bf16[8,16,1920]{2,1,0:T(8,128)(2,1)S(1)}, u32[]{:S(2)}, u32[]{:S(2)}) async-start(bf16[8,16,1920]{2,1,0:T(8,128)(2,1)} %split.1), calls=%async_computation.4 | async-start | bytes 983040 | tf_op jit(solution)/shard_map/all_to_all | solution.py:694
  (16 other events, 140.8 us)

commit v2 on v1

--- a/solution.py
+++ b/solution.py
@@ -24,7 +24,8 @@
 PIECES = 8
 RIDE = 88
 STRIP = 16
-MSG = 16
+MSG = 160
+LANES = COLS // TILE
 EPS = 1e-6
 MASKED = -1e30
 SCALE = HDIM ** (-0.5)
@@ -100,16 +101,18 @@
     owners = jnp.zeros((1, TILE), jnp.int32)
     for t in range(TILES):
         owners = jnp.where(lane == t, own_ref[t], owners)
-    for d in range(N_DP):
-        out_ref[d, OWN:MSG, :] = jnp.zeros((MSG - OWN, COLS), BF)
-        for t in range(TILES):
-            out_ref[d, OWN : OWN + 1, TILE * t : TILE * (t + 1)] = (
-                seg_ref[t : t + 1, :].astype(F32).astype(BF)
-            )
-        out_ref[d, OWN + 1 : OWN + 2, 0:TILE] = owners.astype(F32).astype(BF)
-        for a in range(3):
-            start = D * a + HALF * (d % 2)
-            out_ref[d, 0:OWN, HALF * a : HALF * (a + 1)] = w_ref[:, start : start + HALF]
+    for half in range(2):
+        for k in range(LANES):
+            first = D * (k // 5) + HALF * half + TILE * (k % 5)
+            out_ref[half, OWN * k : OWN * (k + 1), :] = w_ref[:, first : first + TILE]
+        extras = OWN * LANES
+        out_ref[half, extras:MSG, :] = jnp.zeros((MSG - extras, TILE), BF)
+        out_ref[half, extras : extras + 1, :] = owners.astype(F32).astype(BF)
+        out_ref[half, extras + 1 : extras + 1 + TILES, :] = (
+            seg_ref[...].astype(F32).astype(BF)
+        )
+    for d in range(2, N_DP):
+        out_ref[d] = out_ref[d % 2]
 
 
 def build(owners, weight, segments):
@@ -117,25 +120,28 @@
         build_kernel,
         in_specs=[SM, VM, VM],
         out_specs=VM,
-        out_shape=jax.ShapeDtypeStruct((N_DP, MSG, COLS), BF),
-        cost_estimate=cost(0, 2 * N_DP * MSG * COLS),
+        out_shape=jax.ShapeDtypeStruct((N_DP, MSG, TILE), BF),
         compiler_params=params(58),
+        cost_estimate=cost(0, 2 * N_DP * MSG * TILE),
         name="build",
     )(owners, weight, segments)
 
 
 def compact_kernel(group_ref, msg_ref, w_ref, seg_ref, own_ref):
     group = group_ref[0]
+    extras = OWN * LANES
     seg_ref[...] = jnp.zeros_like(seg_ref)
     for s in range(N_DP):
-        w_ref[OWN * s : OWN * (s + 1), :] = msg_ref[s, 0:OWN, :]
-        own_ref[s : s + 1, :] = msg_ref[s, OWN + 1 : OWN + 2, 0:TILE].astype(F32)
+        for k in range(LANES):
+            w_ref[OWN * s : OWN * (s + 1), TILE * k : TILE * (k + 1)] = msg_ref[
+                s, OWN * k : OWN * (k + 1), :
+            ]
+        own_ref[s : s + 1, :] = msg_ref[s, extras : extras + 1, :].astype(F32)
     for rel in range(2):
         src = group + rel * (1 - 2 * (group % 2))
-        for t in range(TILES):
-            seg_ref[TILES * rel + t : TILES * rel + t + 1, :] = msg_ref[
-                src, OWN : OWN + 1, TILE * t : TILE * (t + 1)
-            ].astype(F32)
+        seg_ref[TILES * rel : TILES * (rel + 1), :] = msg_ref[
+            src, extras + 1 : extras + 1 + TILES, :
+        ].astype(F32)
 
 
 def compact(group, messages):
@@ -148,8 +154,8 @@
             jax.ShapeDtypeStruct((8, TILE), F32),
             jax.ShapeDtypeStruct((N_DP, TILE), F32),
         ],
-        cost_estimate=cost(0, 4 * N_DP * MSG * COLS),
         compiler_params=params(12),
+        cost_estimate=cost(0, 4 * N_DP * MSG * TILE),
         name="compact",
     )(group, messages)
 
@@ -509,7 +515,7 @@
         out_specs=[VM] * n,
         out_shape=[jax.ShapeDtypeStruct((rows, COLS), BF)] * n,
         compiler_params=params(12),
-        cost_estimate=cost(0, 4 * len(parts) * PART * COLS),
+        cost_estimate=cost(0, (4 if gains else 24000) * len(parts) * PART * COLS),
         name="add",
     )(*gains, *[array for array, _ in parts])
 
@@ -534,7 +540,7 @@
         gain_kernel,
         in_specs=[VM] * 3,
         out_specs=VM,
-        out_shape=jax.ShapeDtypeStruct((MSG, TILE), F32),
+        out_shape=jax.ShapeDtypeStruct((STRIP, TILE), F32),
         scratch_shapes=[pltpu.VMEM((D, D), BF)],
         compiler_params=params(24),
         cost_estimate=cost(0, 4 * D * TILE),
@@ -609,15 +615,19 @@
     total = rows_ref[...].astype(F32)
     for ref in (one_ref, two_ref, three_ref):
         total = total + ref[...].astype(F32)
-    both = total[BLOCK : BLOCK + 1, :D] + total[BLOCK + 1 : BLOCK + 2, :D]
-    hi = both.astype(BF)
-    lo = (both - hi.astype(F32)).astype(BF)
+    gain = total[BLOCK : BLOCK + 1, :D] + total[BLOCK + 1 : BLOCK + 2, :D]
+    gain = gain.astype(BF)
     total = total.astype(BF)
+    extras = OWN * LANES
     for s in range(N_DP):
-        out_ref[s, 0:OWN, :] = total[OWN * s : OWN * (s + 1)]
-        out_ref[s, OWN:MSG, :] = jnp.zeros((MSG - OWN, COLS), BF)
-        out_ref[s, OWN : OWN + 1, :D] = hi
-        out_ref[s, OWN + 1 : OWN + 2, :D] = lo
+        for k in range(LANES):
+            out_ref[s, OWN * k : OWN * (k + 1), :] = total[
+                OWN * s : OWN * (s + 1), TILE * k : TILE * (k + 1)
+            ]
+        for k in range(D // TILE):
+            out_ref[s, extras + k : extras + k + 1, :] = gain[
+                :, TILE * k : TILE * (k + 1)
+            ]
 
 
 def split(rows, others):
@@ -625,26 +635,24 @@
         split_kernel,
         in_specs=[VM] * 4,
         out_specs=VM,
-        out_shape=jax.ShapeDtypeStruct((N_DP, MSG, COLS), BF),
-        cost_estimate=cost(0, 4 * N_DP * MSG * COLS),
+        out_shape=jax.ShapeDtypeStruct((N_DP, MSG, TILE), BF),
         compiler_params=params(12),
+        cost_estimate=cost(0, 4 * N_DP * MSG * TILE),
         name="split",
     )(rows, *others)
 
 
 def finish_kernel(msg_ref, out_ref, gain_ref):
-    both = jnp.zeros((MSG, COLS), F32)
+    both = jnp.zeros((MSG, TILE), F32)
     for half in range(2):
         total = msg_ref[half].astype(F32)
         for chip in range(1, 4):
             total = total + msg_ref[2 * chip + half].astype(F32)
         both = both + total
-        for a in range(3):
-            start = D * a + HALF * half
-            out_ref[:, start : start + HALF] = total[0:OWN, HALF * a : HALF * (a + 1)]
-    total = both[OWN : OWN + 1, :D] + both[OWN + 1 : OWN + 2, :D]
-    for k in range(D // TILE):
-        gain_ref[k : k + 1, :] = total[:, TILE * k : TILE * (k + 1)]
+        for k in range(LANES):
+            first = D * (k // 5) + HALF * half + TILE * (k % 5)
+            out_ref[:, first : first + TILE] = total[OWN * k : OWN * (k + 1)]
+    gain_ref[...] = both[OWN * LANES : MSG]
 
 
 def finish(messages):
@@ -656,8 +664,8 @@
             jax.ShapeDtypeStruct((OWN, 3 * D), F32),
             jax.ShapeDtypeStruct((D // TILE, TILE), F32),
         ],
-        cost_estimate=cost(0, 6 * N_DP * MSG * COLS),
         compiler_params=params(12),
+        cost_estimate=cost(0, 6 * N_DP * MSG * TILE),
         name="finish",
     )(messages)
 

time: 156 us -> 156 us (level)
  waiting for transfers between devices: 24.6 us -> 22.2 us
    all_to_all x5, waiting for transfers between devices: 10.9 us -> 9.04 us  [exchange(): return lax.all_to_all(value, axis, split_axis=0, concat_axis=0, tiled=True)]
  transfers between devices with their start and end apart: 25 -> 25, of which waited for: 10 -> 9; matrix products, arithmetic and copies ran while one was open for 3% -> 4% of each run, Pallas kernels for 28% -> 29%
where the time goes in v2:
time: 156 us; the launch traced here: 155 us
  Pallas kernels  69.5 us (45%)
  starting transfers between devices  54.5 us (35%)
  waiting for transfers between devices  22.2 us (14%)
  local copies, waits for them, and re-layouts  6.13 us (4%)
    all_to_all x5, starting transfers between devices, exchange(): return lax.all_to_all(value, axis, split_axis=0, concat_axis=0, tiled=True)  30.4 us
    pallas_call x1, Pallas kernels, main(): pl.pallas_call(main_kernel, in_specs=[SM, VM] + [ANY] * (5 + PIECES), out...  22.8 us
    ppermute x16, starting transfers between devices, from_ring(): return lax.ppermute(value, ('dp', 'inner'), ring_pairs(df, ds))  21.2 us
    pallas_call x2, Pallas kernels, back(): pl.pallas_call(functools.partial(back_kernel, half), in_specs=[VM] + [ANY...  17.1 us
    pallas_call x2, Pallas kernels, prep(): pl.pallas_call(prep_kernel, in_specs=[VM] * 3, out_specs=[VM] * 2, out_sh...  12.6 us
    all_to_all x5, waiting for transfers between devices, exchange(): return lax.all_to_all(value, axis, split_axis=0, concat_axis=0, tiled=True)  9.04 us
    ppermute x1, waiting for transfers between devices, on_device(): gain_other = lax.ppermute(gain_part, ('dp', 'inner'), double_pairs(0, 3))  5.58 us
    ppermute x16, waiting for transfers between devices, from_ring(): return lax.ppermute(value, ('dp', 'inner'), ring_pairs(df, ds))  4.22 us
  transfers between devices with their start and end apart: 25, of which 9 were waited for; matrix products, arithmetic and copies ran while one was open for 4% of the time, Pallas kernels for 29%

profile of v2, /device:TPU:1, one launch (start us, length us, event | category | flops | bytes accessed | tf_op | source)
XLA Modules:
  0.0 154.9 jit_solution(12782967186179495276)
XLA Ops:
  0.6 1.8 %build.1 = bf16[8,160,128]{2,1,0:T(8,128)(2,1)} custom-call(s32[3]{0:T(128)} %own_ref.1, bf16[10,3840]{1,0:T(8,128)(2,1)} %w_ref.1, s32[3,128]{1,0:T(4,128)} %seg_ref.1), custom_call_target="tpu_custom_call" | custom-call | bytes 327 | tf_op jit(solution)/shard_map/build/pallas_call | solution.py:119
  2.4 6.0 %all-to-all-start = ((bf16[8,160,128]{2,1,0:T(8,128)(2,1)}), bf16[8,160,128]{2,1,0:T(8,128)(2,1)S(1)}, u32[]{:S(2)}, u32[]{:S(2)}) async-start(bf16[8,160,128]{2,1,0:T(8,128)(2,1)} %build.1), calls=%async_computation | async-start | bytes 655360 | tf_op jit(solution)/shard_map/all_to_all | solution.py:702
  11.7 6.3 %prep.2 = (bf16[384,1280]{1,0:T(8,128)(2,1)}, bf16[1280,384]{1,0:T(8,128)(2,1)}) custom-call(bf16[384,1280]{1,0:T(8,128)(2,1)} %patches_ref.3, f32[1,1280]{1,0:T(1,128)} %reshape.232.gain_ref, f32[1,1280]{1,0:T(1,128)} %convert_element_type.12.nat_ref), custom_call_target="tpu_custom_call" | custom-call | flops 2516582 | bytes 2949 | tf_op jit(solution)/shard_map/prep/pallas_call | solution.py:84
  18.7 3.7 %collective-permute-start.1 = (bf16[80,1920]{1,0:T(8,128)(2,1)S(1)}, bf16[80,1920]{1,0:T(8,128)(2,1)S(1)}, u32[]{:S(2)}, u32[]{:S(2)}) collective-permute-start(bf16[80,1920]{1,0:T(8,128)(2,1)S(1)} %get-tuple-element.55), channel_id=1, source_target_pairs={{4,0},{5,1},{6,2},{7,3},{8,4},{9,5},{10,6},{11,7},{12,8},{13,9},{1... | collective-permute-start | bytes 921608 | tf_op jit(solution)/shard_map/ppermute | solution.py:694
  23.8 4.9 %all-to-all-start.1 = ((bf16[8,3,16,1280]{3,2,1,0:T(8,128)(2,1)}), bf16[8,3,16,1280]{3,2,1,0:T(8,128)(2,1)S(1)}, u32[]{:S(2)}, u32[]{:S(2)}) async-start(bf16[8,3,16,1280]{3,2,1,0:T(8,128)(2,1)} %bitcast.7), calls=%async_computation.1 | async-start | bytes 1966080 | tf_op jit(solution)/shard_map/all_to_all | solution.py:702
  34.0 1.7 %collective-permute-start.5 = (bf16[160,1920]{1,0:T(8,128)(2,1)S(1)}, bf16[160,1920]{1,0:T(8,128)(2,1)}, u32[]{:S(2)}, u32[]{:S(2)}) collective-permute-start(bf16[160,1920]{1,0:T(8,128)(2,1)S(1)} %constant_dynamic-update-slice_fusion.2.refs_1_), channel_id=1, source_target_pairs={{1,0},{2,1},{3,2},{0,3},{5,4},{6,5},{7,6},{4,7},{9,8},{10,9},{11,1... | collective-permute-start | bytes 1843208 | tf_op jit(solution)/shard_map/ppermute | solution.py:694
  36.0 7.1 %all-to-all-done.1 = bf16[8,3,16,1280]{3,2,1,0:T(8,128)(2,1)S(1)} async-done(((bf16[8,3,16,1280]{3,2,1,0:T(8,128)(2,1)}), bf16[8,3,16,1280]{3,2,1,0:T(8,128)(2,1)S(1)}, u32[]{:S(2)}, u32[]{:S(2)}) %all-to-all-start.1) | async-done | bytes 983072 | tf_op jit(solution)/shard_map/all_to_all | solution.py:702
  44.7 5.0 %all-to-all-start.2 = ((bf16[8,6,16,640]{3,2,1,0:T(8,128)(2,1)}), bf16[8,6,16,640]{3,2,1,0:T(8,128)(2,1)}, u32[]{:S(2)}, u32[]{:S(2)}) async-start(bf16[8,6,16,640]{3,2,1,0:T(8,128)(2,1)} %to_heads.1), calls=%async_computation.2 | async-start | bytes 1966080 | tf_op jit(solution)/shard_map/all_to_all | solution.py:702
  49.7 2.5 %collective-permute-start.8 = (bf16[160,1920]{1,0:T(8,128)(2,1)}, bf16[160,1920]{1,0:T(8,128)(2,1)S(1)}, u32[]{:S(2)}, u32[]{:S(2)}) collective-permute-start(bf16[160,1920]{1,0:T(8,128)(2,1)} %collective-permute-done.4.refs_2_), channel_id=1, source_target_pairs={{1,0},{2,1},{3,2},{0,3},{5,4},{6,5},{7,6},{4,7},{9,8},{10,9},{11,1... | collective-permute-start | bytes 1843208 | tf_op jit(solution)/shard_map/ppermute | solution.py:694
  53.4 6.3 %prep.3 = (bf16[384,1280]{1,0:T(8,128)(2,1)}, bf16[1280,384]{1,0:T(8,128)(2,1)}) custom-call(bf16[384,1280]{1,0:T(8,128)(2,1)} %collective-permute-done.patches_ref, f32[1,1280]{1,0:T(1,128)} %reshape.232.gain_ref, f32[1,1280]{1,0:T(1,128)} %convert_element_type.12.nat_ref), custom_call_target="tpu_custom_call" | custom-call | flops 2516582 | bytes 2949 | tf_op jit(solution)/shard_map/prep/pallas_call | solution.py:84
  59.7 3.4 %collective-permute-done.9.refs_5_ = bf16[160,1920]{1,0:T(8,128)(2,1)S(1)} collective-permute-done((bf16[160,1920]{1,0:T(8,128)(2,1)}, bf16[160,1920]{1,0:T(8,128)(2,1)S(1)}, u32[]{:S(2)}, u32[]{:S(2)}) %collective-permute-start.9) | collective-permute-done | bytes 614432 | tf_op jit(solution)/shard_map/ppermute | solution.py:694
  64.2 22.8 %main.1 = (bf16[8,2,128,640]{3,2,1,0:T(8,128)(2,1)}, bf16[768,1920]{1,0:T(8,128)(2,1)}, bf16[160,1920]{1,0:T(8,128)(2,1)}, bf16[160,1920]{1,0:T(8,128)(2,1)}, bf...) custom-call(s32[12]{0:T(128)} %pad_add_fusion.1.idx_ref, ...), custom_call_target="tpu_custom_call" | custom-call | flops 8000000 | bytes 20971 | tf_op jit(solution)/shard_map/main/pallas_call | solution.py:434
  87.0 6.9 %all-to-all-start.3 = ((bf16[8,2,128,640]{3,2,1,0:T(8,128)(2,1)}), bf16[8,2,128,640]{3,2,1,0:T(8,128)(2,1)S(1)}, u32[]{:S(2)}, u32[]{:S(2)}) async-start(bf16[8,2,128,640]{3,2,1,0:T(8,128)(2,1)} %get-tuple-element.75), calls=%async_computation.3 | async-start | bytes 5242880 | tf_op jit(solution)/shard_map/all_to_all | solution.py:702
  96.6 2.3 %gain.1 = f32[16,128]{1,0:T(8,128)S(1)} custom-call(f32[1280,128]{1,0:T(8,128)S(1)} %copy-done, f32[1,1280]{1,0:T(1,128)S(1)} %copy-done.5, f32[1,1280]{1,0:T(1,128)S(1)} %copy-done.6), custom_call_target="tpu_custom_call" | custom-call | bytes 655 | tf_op jit(solution)/shard_map/gain/pallas_call | solution.py:539
  99.6 8.6 %back.2 = bf16[384,1280]{1,0:T(8,128)(2,1)} custom-call(f32[1,1280]{1,0:T(1,128)} %convert_element_type.12.nat_ref, bf16[768,1920]{1,0:T(8,128)(2,1)} %get-tuple-element.77.dqkv_ref, bf16[160,1920]{1,0:T(8,128)(2,1)} %copy-done.8, bf16[160,1920]{1,0:T(8,128)(2,1)} %copy-done.9, bf16[160,1920]{1,0:T(8,128)(2,1)} %collective-permute-done.4.refs_2_, ...), custom_call_target="tpu_custom_call" | custom-call | flops 3145728 | bytes 15728 | tf_op jit(solution)/shard_map/back/pallas_call | solution.py:570
  108.2 3.4 %collective-permute-done.12 = f32[16,128]{1,0:T(8,128)S(1)} collective-permute-done((f32[16,128]{1,0:T(8,128)S(1)}, f32[16,128]{1,0:T(8,128)S(1)}, u32[]{:S(2)}, u32[]{:S(2)}) %collective-permute-start.12) | collective-permute-done | bytes 8224 | tf_op jit(solution)/shard_map/ppermute | solution.py:766
  113.1 2.7 %collective-permute-start.15 = (bf16[160,1920]{1,0:T(8,128)(2,1)S(1)}, bf16[160,1920]{1,0:T(8,128)(2,1)S(1)}, u32[]{:S(2)}, u32[]{:S(2)}) collective-permute-start(bf16[160,1920]{1,0:T(8,128)(2,1)S(1)} %get-tuple-element.73), channel_id=1, source_target_pairs={{1,0},{2,1},{3,2},{0,3},{5,4},{6,5},{7,6},{4,7},{9,8},{10,9},{11,1... | collective-permute-start | bytes 1843208 | tf_op jit(solution)/shard_map/ppermute | solution.py:694
  118.1 5.6 %collective-permute-done.13.other_ref = f32[16,128]{1,0:T(8,128)S(1)} collective-permute-done((f32[16,128]{1,0:T(8,128)S(1)}, f32[16,128]{1,0:T(8,128)S(1)}, u32[]{:S(2)}, u32[]{:S(2)}) %collective-permute-start.13) | collective-permute-done | bytes 8224 | tf_op jit(solution)/shard_map/ppermute | solution.py:775
  123.7 1.8 %add.244 = (bf16[88,1920]{1,0:T(8,128)(2,1)S(1)}, bf16[88,1920]{1,0:T(8,128)(2,1)}, bf16[88,1920]{1,0:T(8,128)(2,1)}, bf16[88,1920]{1,0:T(8,128)(2,1)}) custom-call(f32[16,128]{1,0:T(8,128)S(1)} %add.203.gain_ref, f32[16,128]{1,0:T(8,128)S(1)} %collective-permute-done.13.other_ref, bf16[160,1920]{1,0:T(8,128)(2,1)S(1)} %copy-done.3, ...), custom_call_target="tpu_custom_call" | custom-call | bytes 7372 | tf_op jit(solution)/shard_map/add/pallas_call | solution.py:508
  128.3 8.5 %back.3.mine_ref = bf16[384,1280]{1,0:T(8,128)(2,1)} custom-call(f32[1,1280]{1,0:T(1,128)} %convert_element_type.12.nat_ref, bf16[768,1920]{1,0:T(8,128)(2,1)} %get-tuple-element.77.dqkv_ref, bf16[160,1920]{1,0:T(8,128)(2,1)} %copy-done.8, bf16[160,1920]{1,0:T(8,128)(2,1)} %copy-done.9, bf16[160,1920]{1,0:T(8,128)(2,1)} %collective-permute-done.4.refs_2_, ...), custom_call_target="tpu_custom_call" | custom-call | flops 3145728 | bytes 15728 | tf_op jit(solution)/shard_map/back/pallas_call | solution.py:570
  137.2 2.2 %split.1 = bf16[8,160,128]{2,1,0:T(8,128)(2,1)} custom-call(bf16[88,1920]{1,0:T(8,128)(2,1)S(1)} %get-tuple-element.76.rows_ref, bf16[88,1920]{1,0:T(8,128)(2,1)S(1)} %collective-permute-done.16.one_ref, bf16[88,1920]{1,0:T(8,128)(2,1)} %collective-permute-done.18.two_ref, bf16[88,1920]{1,0:T(8,128)(2,1)} %collective-permute-done.19.three_ref), custom_call_target="tpu_custom_call" | custom-call | bytes 655 | tf_op jit(solution)/shard_map/split/pallas_call | solution.py:634
  139.4 7.6 %all-to-all-start.4 = ((bf16[8,160,128]{2,1,0:T(8,128)(2,1)}), bf16[8,160,128]{2,1,0:T(8,128)(2,1)S(1)}, u32[]{:S(2)}, u32[]{:S(2)}) async-start(bf16[8,160,128]{2,1,0:T(8,128)(2,1)} %split.1), calls=%async_computation.4 | async-start | bytes 655360 | tf_op jit(solution)/shard_map/all_to_all | solution.py:702
  147.1 4.2 %rows_back.1 = bf16[384,1280]{1,0:T(8,128)(2,1)} custom-call(bf16[384,1280]{1,0:T(8,128)(2,1)} %patches_ref.3, f32[1,1280]{1,0:T(1,128)} %reshape.232.gain_ref, bf16[384,1280]{1,0:T(8,128)(2,1)} %back.3.mine_ref, bf16[384,1280]{1,0:T(8,128)(2,1)} %collective-permute-done.17.other_ref), custom_call_target="tpu_custom_call" | custom-call | flops 9830 | bytes 3932 | tf_op jit(solution)/shard_map/rows_back/pallas_call | solution.py:602
  151.3 2.1 %place.1 = bf16[3,128,1280]{2,1,0:T(8,128)(2,1)} custom-call(s32[6]{0:T(128)S(1)} %pad_add_fusion.idx_ref, bf16[8,2,128,640]{3,2,1,0:T(8,128)(2,1)S(1)} %all-to-all-done.3.left_ref.right_ref, bf16[8,2,128,640]{3,2,1,0:T(8,128)(2,1)S(1)} %all-to-all-done.3.left_ref.right_ref), custom_call_target="tpu_custom_call" | custom-call | bytes 1966 | tf_op jit(solution)/shard_map/place/pallas_call | solution.py:200
  (98 shorter events, 26.6 us)
Async XLA Ops:
  2.4 15.5 %all-to-all-start = ((bf16[8,160,128]{2,1,0:T(8,128)(2,1)}), bf16[8,160,128]{2,1,0:T(8,128)(2,1)S(1)}, u32[]{:S(2)}, u32[]{:S(2)}) async-start(bf16[8,160,128]{2,1,0:T(8,128)(2,1)} %build.1), calls=%async_computation | async-start | bytes 655360 | tf_op jit(solution)/shard_map/all_to_all | solution.py:702
  8.4 44.9 %collective-permute-start = (bf16[384,1280]{1,0:T(8,128)(2,1)}, bf16[384,1280]{1,0:T(8,128)(2,1)}, u32[]{:S(2)}, u32[]{:S(2)}) collective-permute-start(bf16[384,1280]{1,0:T(8,128)(2,1)} %patches_ref.3), channel_id=1, source_target_pairs={{16,0},{0,16},{48,32},{32,48},{80,64},{64,80},{112,96},{96,112},{1... | collective-permute-start | bytes 2949128 | tf_op jit(solution)/shard_map/ppermute | solution.py:698
  18.7 10.0 %collective-permute-start.1 = (bf16[80,1920]{1,0:T(8,128)(2,1)S(1)}, bf16[80,1920]{1,0:T(8,128)(2,1)S(1)}, u32[]{:S(2)}, u32[]{:S(2)}) collective-permute-start(bf16[80,1920]{1,0:T(8,128)(2,1)S(1)} %get-tuple-element.55), channel_id=1, source_target_pairs={{4,0},{5,1},{6,2},{7,3},{8,4},{9,5},{10,6},{11,7},{12,8},{13,9},{1... | collective-permute-start | bytes 921608 | tf_op jit(solution)/shard_map/ppermute | solution.py:694
  22.4 10.5 %collective-permute-start.3 = (bf16[80,1920]{1,0:T(8,128)(2,1)S(1)}, bf16[80,1920]{1,0:T(8,128)(2,1)S(1)}, u32[]{:S(2)}, u32[]{:S(2)}) collective-permute-start(bf16[80,1920]{1,0:T(8,128)(2,1)S(1)} %get-tuple-element.55), channel_id=1, source_target_pairs={{12,0},{13,1},{14,2},{15,3},{0,4},{1,5},{2,6},{3,7},{4,8},{5,9},{6... | collective-permute-start | bytes 921608 | tf_op jit(solution)/shard_map/ppermute | solution.py:694
  22.4 9.3 %collective-permute-start.2 = (bf16[80,1920]{1,0:T(8,128)(2,1)S(1)}, bf16[80,1920]{1,0:T(8,128)(2,1)}, u32[]{:S(2)}, u32[]{:S(2)}) collective-permute-start(bf16[80,1920]{1,0:T(8,128)(2,1)S(1)} %get-tuple-element.55), channel_id=1, source_target_pairs={{8,0},{9,1},{10,2},{11,3},{12,4},{13,5},{14,6},{15,7},{0,8},{1,9},... | collective-permute-start | bytes 921608 | tf_op jit(solution)/shard_map/ppermute | solution.py:694
  23.8 19.3 %all-to-all-start.1 = ((bf16[8,3,16,1280]{3,2,1,0:T(8,128)(2,1)}), bf16[8,3,16,1280]{3,2,1,0:T(8,128)(2,1)S(1)}, u32[]{:S(2)}, u32[]{:S(2)}) async-start(bf16[8,3,16,1280]{3,2,1,0:T(8,128)(2,1)} %bitcast.7), calls=%async_computation.1 | async-start | bytes 1966080 | tf_op jit(solution)/shard_map/all_to_all | solution.py:702
  28.7 20.9 %collective-permute-start.6 = (bf16[160,1920]{1,0:T(8,128)(2,1)S(1)}, bf16[160,1920]{1,0:T(8,128)(2,1)S(1)}, u32[]{:S(2)}, u32[]{:S(2)}) collective-permute-start(bf16[160,1920]{1,0:T(8,128)(2,1)S(1)} %constant_dynamic-update-slice_fusion.refs_0_), channel_id=1, source_target_pairs={{3,0},{0,1},{1,2},{2,3},{7,4},{4,5},{5,6},{6,7},{11,8},{8,9},{9,10... | collective-permute-start | bytes 1843208 | tf_op jit(solution)/shard_map/ppermute | solution.py:694
  30.3 19.4 %collective-permute-start.4 = (bf16[160,1920]{1,0:T(8,128)(2,1)S(1)}, bf16[160,1920]{1,0:T(8,128)(2,1)}, u32[]{:S(2)}, u32[]{:S(2)}) collective-permute-start(bf16[160,1920]{1,0:T(8,128)(2,1)S(1)} %constant_dynamic-update-slice_fusion.refs_0_), channel_id=1, source_target_pairs={{1,0},{2,1},{3,2},{0,3},{5,4},{6,5},{7,6},{4,7},{9,8},{10,9},{11,1... | collective-permute-start | bytes 1843208 | tf_op jit(solution)/shard_map/ppermute | solution.py:694
  33.0 16.7 %collective-permute-start.7 = (bf16[160,1920]{1,0:T(8,128)(2,1)S(1)}, bf16[160,1920]{1,0:T(8,128)(2,1)}, u32[]{:S(2)}, u32[]{:S(2)}) collective-permute-start(bf16[160,1920]{1,0:T(8,128)(2,1)S(1)} %constant_dynamic-update-slice_fusion.2.refs_1_), channel_id=1, source_target_pairs={{3,0},{0,1},{1,2},{2,3},{7,4},{4,5},{5,6},{6,7},{11,8},{8,9},{9,10... | collective-permute-start | bytes 1843208 | tf_op jit(solution)/shard_map/ppermute | solution.py:694
  34.0 15.7 %collective-permute-start.5 = (bf16[160,1920]{1,0:T(8,128)(2,1)S(1)}, bf16[160,1920]{1,0:T(8,128)(2,1)}, u32[]{:S(2)}, u32[]{:S(2)}) collective-permute-start(bf16[160,1920]{1,0:T(8,128)(2,1)S(1)} %constant_dynamic-update-slice_fusion.2.refs_1_), channel_id=1, source_target_pairs={{1,0},{2,1},{3,2},{0,3},{5,4},{6,5},{7,6},{4,7},{9,8},{10,9},{11,1... | collective-permute-start | bytes 1843208 | tf_op jit(solution)/shard_map/ppermute | solution.py:694
  44.7 19.5 %all-to-all-start.2 = ((bf16[8,6,16,640]{3,2,1,0:T(8,128)(2,1)}), bf16[8,6,16,640]{3,2,1,0:T(8,128)(2,1)}, u32[]{:S(2)}, u32[]{:S(2)}) async-start(bf16[8,6,16,640]{3,2,1,0:T(8,128)(2,1)} %to_heads.1), calls=%async_computation.2 | async-start | bytes 1966080 | tf_op jit(solution)/shard_map/all_to_all | solution.py:702
  49.7 10.0 %collective-permute-start.8 = (bf16[160,1920]{1,0:T(8,128)(2,1)}, bf16[160,1920]{1,0:T(8,128)(2,1)S(1)}, u32[]{:S(2)}, u32[]{:S(2)}) collective-permute-start(bf16[160,1920]{1,0:T(8,128)(2,1)} %collective-permute-done.4.refs_2_), channel_id=1, source_target_pairs={{1,0},{2,1},{3,2},{0,3},{5,4},{6,5},{7,6},{4,7},{9,8},{10,9},{11,1... | collective-permute-start | bytes 1843208 | tf_op jit(solution)/shard_map/ppermute | solution.py:694
  52.2 10.8 %collective-permute-start.9 = (bf16[160,1920]{1,0:T(8,128)(2,1)}, bf16[160,1920]{1,0:T(8,128)(2,1)S(1)}, u32[]{:S(2)}, u32[]{:S(2)}) collective-permute-start(bf16[160,1920]{1,0:T(8,128)(2,1)} %collective-permute-done.7.refs_7_), channel_id=1, source_target_pairs={{3,0},{0,1},{1,2},{2,3},{7,4},{4,5},{5,6},{6,7},{11,8},{8,9},{9,10... | collective-permute-start | bytes 1843208 | tf_op jit(solution)/shard_map/ppermute | solution.py:694
  87.0 49.8 %all-to-all-start.3 = ((bf16[8,2,128,640]{3,2,1,0:T(8,128)(2,1)}), bf16[8,2,128,640]{3,2,1,0:T(8,128)(2,1)S(1)}, u32[]{:S(2)}, u32[]{:S(2)}) async-start(bf16[8,2,128,640]{3,2,1,0:T(8,128)(2,1)} %get-tuple-element.75), calls=%async_computation.3 | async-start | bytes 5242880 | tf_op jit(solution)/shard_map/all_to_all | solution.py:702
  93.9 17.7 %collective-permute-start.10 = (bf16[320,1920]{1,0:T(8,128)(2,1)}, bf16[320,1920]{1,0:T(8,128)(2,1)S(1)}, u32[]{:S(2)}, u32[]{:S(2)}) collective-permute-start(bf16[320,1920]{1,0:T(8,128)(2,1)} %get-tuple-element.60), channel_id=1, source_target_pairs={{3,0},{0,1},{1,2},{2,3},{7,4},{4,5},{5,6},{6,7},{11,8},{8,9},{9,10... | collective-permute-start | bytes 3686408 | tf_op jit(solution)/shard_map/ppermute | solution.py:694
  95.4 16.2 %collective-permute-start.11 = (bf16[320,1920]{1,0:T(8,128)(2,1)}, bf16[320,1920]{1,0:T(8,128)(2,1)S(1)}, u32[]{:S(2)}, u32[]{:S(2)}) collective-permute-start(bf16[320,1920]{1,0:T(8,128)(2,1)} %get-tuple-element.61), channel_id=1, source_target_pairs={{1,0},{2,1},{3,2},{0,3},{5,4},{6,5},{7,6},{4,7},{9,8},{10,9},{11,1... | collective-permute-start | bytes 3686408 | tf_op jit(solution)/shard_map/ppermute | solution.py:694
  99.0 12.7 %collective-permute-start.12 = (f32[16,128]{1,0:T(8,128)S(1)}, f32[16,128]{1,0:T(8,128)S(1)}, u32[]{:S(2)}, u32[]{:S(2)}) collective-permute-start(f32[16,128]{1,0:T(8,128)S(1)} %gain.1), channel_id=1, source_target_pairs={{1,0},{0,1},{3,2},{2,3},{5,4},{4,5},{7,6},{6,7},{9,8},{8,9},{11,10... | collective-permute-start | bytes 24584 | tf_op jit(solution)/shard_map/ppermute | solution.py:766
  113.0 10.7 %collective-permute-start.14 = (bf16[160,1920]{1,0:T(8,128)(2,1)S(1)}, bf16[160,1920]{1,0:T(8,128)(2,1)S(1)}, u32[]{:S(2)}, u32[]{:S(2)}) collective-permute-start(bf16[160,1920]{1,0:T(8,128)(2,1)S(1)} %get-tuple-element.71), channel_id=1, source_target_pairs={{3,0},{0,1},{1,2},{2,3},{7,4},{4,5},{5,6},{6,7},{11,8},{8,9},{9,10... | collective-permute-start | bytes 1843208 | tf_op jit(solution)/shard_map/ppermute | solution.py:694
  113.1 10.6 %collective-permute-start.15 = (bf16[160,1920]{1,0:T(8,128)(2,1)S(1)}, bf16[160,1920]{1,0:T(8,128)(2,1)S(1)}, u32[]{:S(2)}, u32[]{:S(2)}) collective-permute-start(bf16[160,1920]{1,0:T(8,128)(2,1)S(1)} %get-tuple-element.73), channel_id=1, source_target_pairs={{1,0},{2,1},{3,2},{0,3},{5,4},{6,5},{7,6},{4,7},{9,8},{10,9},{11,1... | collective-permute-start | bytes 1843208 | tf_op jit(solution)/shard_map/ppermute | solution.py:694
  115.7 31.4 %collective-permute-start.17 = (bf16[384,1280]{1,0:T(8,128)(2,1)}, bf16[384,1280]{1,0:T(8,128)(2,1)}, u32[]{:S(2)}, u32[]{:S(2)}) collective-permute-start(bf16[384,1280]{1,0:T(8,128)(2,1)} %back.2), channel_id=1, source_target_pairs={{16,0},{0,16},{48,32},{32,48},{80,64},{64,80},{112,96},{96,112},{1... | collective-permute-start | bytes 2949128 | tf_op jit(solution)/shard_map/ppermute | solution.py:698
  125.4 11.4 %collective-permute-start.16 = (bf16[88,1920]{1,0:T(8,128)(2,1)}, bf16[88,1920]{1,0:T(8,128)(2,1)S(1)}, u32[]{:S(2)}, u32[]{:S(2)}) collective-permute-start(bf16[88,1920]{1,0:T(8,128)(2,1)} %get-tuple-element.74), channel_id=1, source_target_pairs={{8,0},{9,1},{10,2},{11,3},{12,4},{13,5},{14,6},{15,7},{0,8},{1,9},... | collective-permute-start | bytes 1013768 | tf_op jit(solution)/shard_map/ppermute | solution.py:694
  126.6 10.2 %collective-permute-start.18 = (bf16[88,1920]{1,0:T(8,128)(2,1)}, bf16[88,1920]{1,0:T(8,128)(2,1)}, u32[]{:S(2)}, u32[]{:S(2)}) collective-permute-start(bf16[88,1920]{1,0:T(8,128)(2,1)} %get-tuple-element.82), channel_id=1, source_target_pairs={{4,0},{5,1},{6,2},{7,3},{8,4},{9,5},{10,6},{11,7},{12,8},{13,9},{1... | collective-permute-start | bytes 1013768 | tf_op jit(solution)/shard_map/ppermute | solution.py:694
  127.1 10.1 %collective-permute-start.19 = (bf16[88,1920]{1,0:T(8,128)(2,1)}, bf16[88,1920]{1,0:T(8,128)(2,1)}, u32[]{:S(2)}, u32[]{:S(2)}) collective-permute-start(bf16[88,1920]{1,0:T(8,128)(2,1)} %get-tuple-element.83), channel_id=1, source_target_pairs={{12,0},{13,1},{14,2},{15,3},{0,4},{1,5},{2,6},{3,7},{4,8},{5,9},{6... | collective-permute-start | bytes 1013768 | tf_op jit(solution)/shard_map/ppermute | solution.py:694
  139.4 14.7 %all-to-all-start.4 = ((bf16[8,160,128]{2,1,0:T(8,128)(2,1)}), bf16[8,160,128]{2,1,0:T(8,128)(2,1)S(1)}, u32[]{:S(2)}, u32[]{:S(2)}) async-start(bf16[8,160,128]{2,1,0:T(8,128)(2,1)} %split.1), calls=%async_computation.4 | async-start | bytes 655360 | tf_op jit(solution)/shard_map/all_to_all | solution.py:702
  (15 other events, 129.2 us)

commit v3 on v2

--- a/solution.py
+++ b/solution.py
@@ -220,11 +220,8 @@
     return jnp.concatenate([jnp.where(m, window, zero) for m in masks], axis=0)
 
 
-def pick_heads(stacked, masks):
-    zero = jnp.zeros((TILE, 256), F32)
-    return jnp.where(
-        masks[0], stacked[:TILE], jnp.where(masks[1], stacked[TILE:], zero)
-    )
+def rows_of_heads(both):
+    return jnp.concatenate([both[:, :TILE], both[:, TILE:]], axis=0)
 
 
 def halves(fn, *arrays):
@@ -400,15 +397,19 @@
         weights = [x * (1.0 / total) for x, total in zip(expo, sums)]
         rounded = [x.astype(BF) for x in weights]
         outs = [dot(rounded[i], vv[i]) for i in pairs]
-        dvs = [dot(rounded[i], d_out[i], TN) for i in pairs]
+        dvs = [
+            dot(rows_of_heads(rounded[i]), stack_heads(d_out[i], masks[i]), TN)
+            for i in pairs
+        ]
         inner = [halves(wide_sum, d_probs[i] * weights[i]) for i in pairs]
         d_scores = [
             (weights[i] * (d_probs[i] - inner[i]) * SCALE).astype(BF) for i in pairs
         ]
         dqs = [dot(d_scores[i], kk[i]) for i in pairs]
-        dks = [dot(d_scores[i], q[i], TN) for i in pairs]
-        dks = [pick_heads(dks[i], masks[i]) for i in pairs]
-        dvs = [pick_heads(dvs[i], masks[i]) for i in pairs]
+        dks = [
+            dot(rows_of_heads(d_scores[i]), stack_heads(q[i], masks[i]), TN)
+            for i in pairs
+        ]
 
         def lanes(vals):
             parts = [vals[0][:, :TILE]]
@@ -515,7 +516,7 @@
         out_specs=[VM] * n,
         out_shape=[jax.ShapeDtypeStruct((rows, COLS), BF)] * n,
         compiler_params=params(12),
-        cost_estimate=cost(0, (4 if gains else 24000) * len(parts) * PART * COLS),
+        cost_estimate=cost(0, (4 if gains else 75000) * len(parts) * PART * COLS),
         name="add",
     )(*gains, *[array for array, _ in parts])
 
@@ -722,9 +723,9 @@
     partner_patches = swap_cores(patches)
     own_prep = prep(patches, gain, nat)
     strips = cotangent.reshape(TILES, N_DP, STRIP, D).transpose(1, 0, 2, 3)
-    messages, own_prep, strips = lax.optimization_barrier((messages, own_prep, strips))
+    messages, strips = lax.optimization_barrier((messages, strips))
     block, seg, owners_all = compact(group.reshape(1).astype(jnp.int32), messages)
-    strips = exchange(strips)
+    strips, own_prep = lax.optimization_barrier((exchange(strips), own_prep))
 
     owner_of = owners_all[:, :TILES].astype(jnp.int32).reshape(N_DP * TILES)
     u = jnp.arange(N_DP * TILES)

time: 156 us -> 155 us (level)
  no operation moved by 1% of the time
where the time goes in v3:
time: 155 us; the launch traced here: 154 us
  Pallas kernels  68.5 us (44%)
  starting transfers between devices  54.7 us (35%)
  waiting for transfers between devices  22.1 us (14%)
  local copies, waits for them, and re-layouts  6.13 us (4%)
    all_to_all x5, starting transfers between devices, exchange(): return lax.all_to_all(value, axis, split_axis=0, concat_axis=0, tiled=True)  30.4 us
    pallas_call x1, Pallas kernels, main(): pl.pallas_call(main_kernel, in_specs=[SM, VM] + [ANY] * (5 + PIECES), out...  21.8 us
    ppermute x16, starting transfers between devices, from_ring(): return lax.ppermute(value, ('dp', 'inner'), ring_pairs(df, ds))  21.4 us
    pallas_call x2, Pallas kernels, back(): pl.pallas_call(functools.partial(back_kernel, half), in_specs=[VM] + [ANY...  17.1 us
    pallas_call x2, Pallas kernels, prep(): pl.pallas_call(prep_kernel, in_specs=[VM] * 3, out_specs=[VM] * 2, out_sh...  12.6 us
    all_to_all x5, waiting for transfers between devices, exchange(): return lax.all_to_all(value, axis, split_axis=0, concat_axis=0, tiled=True)  9.04 us
    ppermute x1, waiting for transfers between devices, on_device(): gain_other = lax.ppermute(gain_part, ('dp', 'inner'), double_pairs(0, 3))  5.36 us
    pallas_call x1, Pallas kernels, rows_back(): pl.pallas_call(rows_kernel, grid=(TILES,), in_specs=[block, pl.BlockSpec(...  4.16 us
  transfers between devices with their start and end apart: 25, of which 9 were waited for; matrix products, arithmetic and copies ran while one was open for 4% of the time, Pallas kernels for 29%

profile of v3, /device:TPU:1, one launch (start us, length us, event | category | flops | bytes accessed | tf_op | source)
XLA Modules:
  0.0 153.9 jit_solution(443266053080645178)
XLA Ops:
  0.6 1.8 %build.1 = bf16[8,160,128]{2,1,0:T(8,128)(2,1)} custom-call(s32[3]{0:T(128)} %own_ref.1, bf16[10,3840]{1,0:T(8,128)(2,1)} %w_ref.1, s32[3,128]{1,0:T(4,128)} %seg_ref.1), custom_call_target="tpu_custom_call" | custom-call | bytes 327 | tf_op jit(solution)/shard_map/build/pallas_call | solution.py:119
  2.4 6.0 %all-to-all-start = ((bf16[8,160,128]{2,1,0:T(8,128)(2,1)}), bf16[8,160,128]{2,1,0:T(8,128)(2,1)S(1)}, u32[]{:S(2)}, u32[]{:S(2)}) async-start(bf16[8,160,128]{2,1,0:T(8,128)(2,1)} %build.1), calls=%async_computation | async-start | bytes 655360 | tf_op jit(solution)/shard_map/all_to_all | solution.py:703
  11.7 6.3 %prep.2 = (bf16[384,1280]{1,0:T(8,128)(2,1)}, bf16[1280,384]{1,0:T(8,128)(2,1)}) custom-call(bf16[384,1280]{1,0:T(8,128)(2,1)} %patches_ref.3, f32[1,1280]{1,0:T(1,128)} %reshape.235.gain_ref, f32[1,1280]{1,0:T(1,128)} %convert_element_type.14.nat_ref), custom_call_target="tpu_custom_call" | custom-call | flops 2516582 | bytes 2949 | tf_op jit(solution)/shard_map/prep/pallas_call | solution.py:84
  18.7 3.7 %collective-permute-start.1 = (bf16[80,1920]{1,0:T(8,128)(2,1)S(1)}, bf16[80,1920]{1,0:T(8,128)(2,1)S(1)}, u32[]{:S(2)}, u32[]{:S(2)}) collective-permute-start(bf16[80,1920]{1,0:T(8,128)(2,1)S(1)} %get-tuple-element.57), channel_id=1, source_target_pairs={{4,0},{5,1},{6,2},{7,3},{8,4},{9,5},{10,6},{11,7},{12,8},{13,9},{1... | collective-permute-start | bytes 921608 | tf_op jit(solution)/shard_map/ppermute | solution.py:695
  23.8 4.9 %all-to-all-start.1 = ((bf16[8,3,16,1280]{3,2,1,0:T(8,128)(2,1)}), bf16[8,3,16,1280]{3,2,1,0:T(8,128)(2,1)S(1)}, u32[]{:S(2)}, u32[]{:S(2)}) async-start(bf16[8,3,16,1280]{3,2,1,0:T(8,128)(2,1)} %bitcast.7), calls=%async_computation.1 | async-start | bytes 1966080 | tf_op jit(solution)/shard_map/all_to_all | solution.py:703
  34.0 1.7 %collective-permute-start.5 = (bf16[160,1920]{1,0:T(8,128)(2,1)S(1)}, bf16[160,1920]{1,0:T(8,128)(2,1)}, u32[]{:S(2)}, u32[]{:S(2)}) collective-permute-start(bf16[160,1920]{1,0:T(8,128)(2,1)S(1)} %constant_dynamic-update-slice_fusion.2.refs_1_), channel_id=1, source_target_pairs={{1,0},{2,1},{3,2},{0,3},{5,4},{6,5},{7,6},{4,7},{9,8},{10,9},{11,1... | collective-permute-start | bytes 1843208 | tf_op jit(solution)/shard_map/ppermute | solution.py:695
  36.0 7.1 %all-to-all-done.1 = bf16[8,3,16,1280]{3,2,1,0:T(8,128)(2,1)S(1)} async-done(((bf16[8,3,16,1280]{3,2,1,0:T(8,128)(2,1)}), bf16[8,3,16,1280]{3,2,1,0:T(8,128)(2,1)S(1)}, u32[]{:S(2)}, u32[]{:S(2)}) %all-to-all-start.1) | async-done | bytes 983072 | tf_op jit(solution)/shard_map/all_to_all | solution.py:703
  44.7 5.0 %all-to-all-start.2 = ((bf16[8,6,16,640]{3,2,1,0:T(8,128)(2,1)}), bf16[8,6,16,640]{3,2,1,0:T(8,128)(2,1)}, u32[]{:S(2)}, u32[]{:S(2)}) async-start(bf16[8,6,16,640]{3,2,1,0:T(8,128)(2,1)} %to_heads.1), calls=%async_computation.2 | async-start | bytes 1966080 | tf_op jit(solution)/shard_map/all_to_all | solution.py:703
  49.7 2.5 %collective-permute-start.8 = (bf16[160,1920]{1,0:T(8,128)(2,1)}, bf16[160,1920]{1,0:T(8,128)(2,1)S(1)}, u32[]{:S(2)}, u32[]{:S(2)}) collective-permute-start(bf16[160,1920]{1,0:T(8,128)(2,1)} %collective-permute-done.4.refs_2_), channel_id=1, source_target_pairs={{1,0},{2,1},{3,2},{0,3},{5,4},{6,5},{7,6},{4,7},{9,8},{10,9},{11,1... | collective-permute-start | bytes 1843208 | tf_op jit(solution)/shard_map/ppermute | solution.py:695
  53.4 6.3 %prep.3 = (bf16[384,1280]{1,0:T(8,128)(2,1)}, bf16[1280,384]{1,0:T(8,128)(2,1)}) custom-call(bf16[384,1280]{1,0:T(8,128)(2,1)} %collective-permute-done.patches_ref, f32[1,1280]{1,0:T(1,128)} %reshape.235.gain_ref, f32[1,1280]{1,0:T(1,128)} %convert_element_type.14.nat_ref), custom_call_target="tpu_custom_call" | custom-call | flops 2516582 | bytes 2949 | tf_op jit(solution)/shard_map/prep/pallas_call | solution.py:84
  59.7 3.4 %collective-permute-done.9.refs_5_ = bf16[160,1920]{1,0:T(8,128)(2,1)S(1)} collective-permute-done((bf16[160,1920]{1,0:T(8,128)(2,1)}, bf16[160,1920]{1,0:T(8,128)(2,1)S(1)}, u32[]{:S(2)}, u32[]{:S(2)}) %collective-permute-start.9) | collective-permute-done | bytes 614432 | tf_op jit(solution)/shard_map/ppermute | solution.py:695
  64.2 21.8 %main.1 = (bf16[8,2,128,640]{3,2,1,0:T(8,128)(2,1)}, bf16[768,1920]{1,0:T(8,128)(2,1)}, bf16[160,1920]{1,0:T(8,128)(2,1)}, bf16[160,1920]{1,0:T(8,128)(2,1)}, bf...) custom-call(s32[12]{0:T(128)} %pad_add_fusion.1.idx_ref, ...), custom_call_target="tpu_custom_call" | custom-call | flops 8000000 | bytes 20971 | tf_op jit(solution)/shard_map/main/pallas_call | solution.py:435
  86.0 6.9 %all-to-all-start.3 = ((bf16[8,2,128,640]{3,2,1,0:T(8,128)(2,1)}), bf16[8,2,128,640]{3,2,1,0:T(8,128)(2,1)S(1)}, u32[]{:S(2)}, u32[]{:S(2)}) async-start(bf16[8,2,128,640]{3,2,1,0:T(8,128)(2,1)} %get-tuple-element.77), calls=%async_computation.3 | async-start | bytes 5242880 | tf_op jit(solution)/shard_map/all_to_all | solution.py:703
  95.6 2.3 %gain.1 = f32[16,128]{1,0:T(8,128)S(1)} custom-call(f32[1280,128]{1,0:T(8,128)S(1)} %copy-done, f32[1,1280]{1,0:T(1,128)S(1)} %copy-done.5, f32[1,1280]{1,0:T(1,128)S(1)} %copy-done.6), custom_call_target="tpu_custom_call" | custom-call | bytes 655 | tf_op jit(solution)/shard_map/gain/pallas_call | solution.py:540
  98.4 8.6 %back.2 = bf16[384,1280]{1,0:T(8,128)(2,1)} custom-call(f32[1,1280]{1,0:T(1,128)} %convert_element_type.14.nat_ref, bf16[768,1920]{1,0:T(8,128)(2,1)} %get-tuple-element.79.dqkv_ref, bf16[160,1920]{1,0:T(8,128)(2,1)} %copy-done.8, bf16[160,1920]{1,0:T(8,128)(2,1)} %copy-done.9, bf16[160,1920]{1,0:T(8,128)(2,1)} %collective-permute-done.4.refs_2_, ...), custom_call_target="tpu_custom_call" | custom-call | flops 3145728 | bytes 15728 | tf_op jit(solution)/shard_map/back/pallas_call | solution.py:571
  107.0 3.7 %collective-permute-done.12 = f32[16,128]{1,0:T(8,128)S(1)} collective-permute-done((f32[16,128]{1,0:T(8,128)S(1)}, f32[16,128]{1,0:T(8,128)S(1)}, u32[]{:S(2)}, u32[]{:S(2)}) %collective-permute-start.12) | collective-permute-done | bytes 8224 | tf_op jit(solution)/shard_map/ppermute | solution.py:767
  112.1 2.7 %collective-permute-start.15 = (bf16[160,1920]{1,0:T(8,128)(2,1)S(1)}, bf16[160,1920]{1,0:T(8,128)(2,1)S(1)}, u32[]{:S(2)}, u32[]{:S(2)}) collective-permute-start(bf16[160,1920]{1,0:T(8,128)(2,1)S(1)} %get-tuple-element.75), channel_id=1, source_target_pairs={{1,0},{2,1},{3,2},{0,3},{5,4},{6,5},{7,6},{4,7},{9,8},{10,9},{11,1... | collective-permute-start | bytes 1843208 | tf_op jit(solution)/shard_map/ppermute | solution.py:695
  117.3 5.4 %collective-permute-done.13.other_ref = f32[16,128]{1,0:T(8,128)S(1)} collective-permute-done((f32[16,128]{1,0:T(8,128)S(1)}, f32[16,128]{1,0:T(8,128)S(1)}, u32[]{:S(2)}, u32[]{:S(2)}) %collective-permute-start.13) | collective-permute-done | bytes 8224 | tf_op jit(solution)/shard_map/ppermute | solution.py:776
  122.7 1.7 %add.244 = (bf16[88,1920]{1,0:T(8,128)(2,1)S(1)}, bf16[88,1920]{1,0:T(8,128)(2,1)}, bf16[88,1920]{1,0:T(8,128)(2,1)}, bf16[88,1920]{1,0:T(8,128)(2,1)}) custom-call(f32[16,128]{1,0:T(8,128)S(1)} %add.203.gain_ref, f32[16,128]{1,0:T(8,128)S(1)} %collective-permute-done.13.other_ref, bf16[160,1920]{1,0:T(8,128)(2,1)S(1)} %copy-done.3, ...), custom_call_target="tpu_custom_call" | custom-call | bytes 7372 | tf_op jit(solution)/shard_map/add/pallas_call | solution.py:509
  127.5 8.5 %back.3.mine_ref = bf16[384,1280]{1,0:T(8,128)(2,1)} custom-call(f32[1,1280]{1,0:T(1,128)} %convert_element_type.14.nat_ref, bf16[768,1920]{1,0:T(8,128)(2,1)} %get-tuple-element.79.dqkv_ref, bf16[160,1920]{1,0:T(8,128)(2,1)} %copy-done.8, bf16[160,1920]{1,0:T(8,128)(2,1)} %copy-done.9, bf16[160,1920]{1,0:T(8,128)(2,1)} %collective-permute-done.4.refs_2_, ...), custom_call_target="tpu_custom_call" | custom-call | flops 3145728 | bytes 15728 | tf_op jit(solution)/shard_map/back/pallas_call | solution.py:571
  136.2 2.2 %split.1 = bf16[8,160,128]{2,1,0:T(8,128)(2,1)} custom-call(bf16[88,1920]{1,0:T(8,128)(2,1)S(1)} %get-tuple-element.78.rows_ref, bf16[88,1920]{1,0:T(8,128)(2,1)S(1)} %collective-permute-done.16.one_ref, bf16[88,1920]{1,0:T(8,128)(2,1)} %collective-permute-done.18.two_ref, bf16[88,1920]{1,0:T(8,128)(2,1)} %collective-permute-done.19.three_ref), custom_call_target="tpu_custom_call" | custom-call | bytes 655 | tf_op jit(solution)/shard_map/split/pallas_call | solution.py:635
  138.4 7.6 %all-to-all-start.4 = ((bf16[8,160,128]{2,1,0:T(8,128)(2,1)}), bf16[8,160,128]{2,1,0:T(8,128)(2,1)S(1)}, u32[]{:S(2)}, u32[]{:S(2)}) async-start(bf16[8,160,128]{2,1,0:T(8,128)(2,1)} %split.1), calls=%async_computation.4 | async-start | bytes 655360 | tf_op jit(solution)/shard_map/all_to_all | solution.py:703
  146.1 4.2 %rows_back.1 = bf16[384,1280]{1,0:T(8,128)(2,1)} custom-call(bf16[384,1280]{1,0:T(8,128)(2,1)} %patches_ref.3, f32[1,1280]{1,0:T(1,128)} %reshape.235.gain_ref, bf16[384,1280]{1,0:T(8,128)(2,1)} %back.3.mine_ref, bf16[384,1280]{1,0:T(8,128)(2,1)} %collective-permute-done.17.other_ref), custom_call_target="tpu_custom_call" | custom-call | flops 9830 | bytes 3932 | tf_op jit(solution)/shard_map/rows_back/pallas_call | solution.py:603
  150.3 2.1 %place.1 = bf16[3,128,1280]{2,1,0:T(8,128)(2,1)} custom-call(s32[6]{0:T(128)S(1)} %pad_add_fusion.idx_ref, bf16[8,2,128,640]{3,2,1,0:T(8,128)(2,1)S(1)} %all-to-all-done.3.left_ref.right_ref, bf16[8,2,128,640]{3,2,1,0:T(8,128)(2,1)S(1)} %all-to-all-done.3.left_ref.right_ref), custom_call_target="tpu_custom_call" | custom-call | bytes 1966 | tf_op jit(solution)/shard_map/place/pallas_call | solution.py:200
  (98 shorter events, 26.6 us)
Async XLA Ops:
  2.4 15.5 %all-to-all-start = ((bf16[8,160,128]{2,1,0:T(8,128)(2,1)}), bf16[8,160,128]{2,1,0:T(8,128)(2,1)S(1)}, u32[]{:S(2)}, u32[]{:S(2)}) async-start(bf16[8,160,128]{2,1,0:T(8,128)(2,1)} %build.1), calls=%async_computation | async-start | bytes 655360 | tf_op jit(solution)/shard_map/all_to_all | solution.py:703
  8.4 44.9 %collective-permute-start = (bf16[384,1280]{1,0:T(8,128)(2,1)}, bf16[384,1280]{1,0:T(8,128)(2,1)}, u32[]{:S(2)}, u32[]{:S(2)}) collective-permute-start(bf16[384,1280]{1,0:T(8,128)(2,1)} %patches_ref.3), channel_id=1, source_target_pairs={{16,0},{0,16},{48,32},{32,48},{80,64},{64,80},{112,96},{96,112},{1... | collective-permute-start | bytes 2949128 | tf_op jit(solution)/shard_map/ppermute | solution.py:699
  18.7 10.0 %collective-permute-start.1 = (bf16[80,1920]{1,0:T(8,128)(2,1)S(1)}, bf16[80,1920]{1,0:T(8,128)(2,1)S(1)}, u32[]{:S(2)}, u32[]{:S(2)}) collective-permute-start(bf16[80,1920]{1,0:T(8,128)(2,1)S(1)} %get-tuple-element.57), channel_id=1, source_target_pairs={{4,0},{5,1},{6,2},{7,3},{8,4},{9,5},{10,6},{11,7},{12,8},{13,9},{1... | collective-permute-start | bytes 921608 | tf_op jit(solution)/shard_map/ppermute | solution.py:695
  22.4 10.5 %collective-permute-start.3 = (bf16[80,1920]{1,0:T(8,128)(2,1)S(1)}, bf16[80,1920]{1,0:T(8,128)(2,1)S(1)}, u32[]{:S(2)}, u32[]{:S(2)}) collective-permute-start(bf16[80,1920]{1,0:T(8,128)(2,1)S(1)} %get-tuple-element.57), channel_id=1, source_target_pairs={{12,0},{13,1},{14,2},{15,3},{0,4},{1,5},{2,6},{3,7},{4,8},{5,9},{6... | collective-permute-start | bytes 921608 | tf_op jit(solution)/shard_map/ppermute | solution.py:695
  22.4 9.3 %collective-permute-start.2 = (bf16[80,1920]{1,0:T(8,128)(2,1)S(1)}, bf16[80,1920]{1,0:T(8,128)(2,1)}, u32[]{:S(2)}, u32[]{:S(2)}) collective-permute-start(bf16[80,1920]{1,0:T(8,128)(2,1)S(1)} %get-tuple-element.57), channel_id=1, source_target_pairs={{8,0},{9,1},{10,2},{11,3},{12,4},{13,5},{14,6},{15,7},{0,8},{1,9},... | collective-permute-start | bytes 921608 | tf_op jit(solution)/shard_map/ppermute | solution.py:695
  23.8 19.3 %all-to-all-start.1 = ((bf16[8,3,16,1280]{3,2,1,0:T(8,128)(2,1)}), bf16[8,3,16,1280]{3,2,1,0:T(8,128)(2,1)S(1)}, u32[]{:S(2)}, u32[]{:S(2)}) async-start(bf16[8,3,16,1280]{3,2,1,0:T(8,128)(2,1)} %bitcast.7), calls=%async_computation.1 | async-start | bytes 1966080 | tf_op jit(solution)/shard_map/all_to_all | solution.py:703
  28.7 20.9 %collective-permute-start.6 = (bf16[160,1920]{1,0:T(8,128)(2,1)S(1)}, bf16[160,1920]{1,0:T(8,128)(2,1)S(1)}, u32[]{:S(2)}, u32[]{:S(2)}) collective-permute-start(bf16[160,1920]{1,0:T(8,128)(2,1)S(1)} %constant_dynamic-update-slice_fusion.refs_0_), channel_id=1, source_target_pairs={{3,0},{0,1},{1,2},{2,3},{7,4},{4,5},{5,6},{6,7},{11,8},{8,9},{9,10... | collective-permute-start | bytes 1843208 | tf_op jit(solution)/shard_map/ppermute | solution.py:695
  30.3 19.4 %collective-permute-start.4 = (bf16[160,1920]{1,0:T(8,128)(2,1)S(1)}, bf16[160,1920]{1,0:T(8,128)(2,1)}, u32[]{:S(2)}, u32[]{:S(2)}) collective-permute-start(bf16[160,1920]{1,0:T(8,128)(2,1)S(1)} %constant_dynamic-update-slice_fusion.refs_0_), channel_id=1, source_target_pairs={{1,0},{2,1},{3,2},{0,3},{5,4},{6,5},{7,6},{4,7},{9,8},{10,9},{11,1... | collective-permute-start | bytes 1843208 | tf_op jit(solution)/shard_map/ppermute | solution.py:695
  33.0 16.7 %collective-permute-start.7 = (bf16[160,1920]{1,0:T(8,128)(2,1)S(1)}, bf16[160,1920]{1,0:T(8,128)(2,1)}, u32[]{:S(2)}, u32[]{:S(2)}) collective-permute-start(bf16[160,1920]{1,0:T(8,128)(2,1)S(1)} %constant_dynamic-update-slice_fusion.2.refs_1_), channel_id=1, source_target_pairs={{3,0},{0,1},{1,2},{2,3},{7,4},{4,5},{5,6},{6,7},{11,8},{8,9},{9,10... | collective-permute-start | bytes 1843208 | tf_op jit(solution)/shard_map/ppermute | solution.py:695
  34.0 15.7 %collective-permute-start.5 = (bf16[160,1920]{1,0:T(8,128)(2,1)S(1)}, bf16[160,1920]{1,0:T(8,128)(2,1)}, u32[]{:S(2)}, u32[]{:S(2)}) collective-permute-start(bf16[160,1920]{1,0:T(8,128)(2,1)S(1)} %constant_dynamic-update-slice_fusion.2.refs_1_), channel_id=1, source_target_pairs={{1,0},{2,1},{3,2},{0,3},{5,4},{6,5},{7,6},{4,7},{9,8},{10,9},{11,1... | collective-permute-start | bytes 1843208 | tf_op jit(solution)/shard_map/ppermute | solution.py:695
  44.7 19.5 %all-to-all-start.2 = ((bf16[8,6,16,640]{3,2,1,0:T(8,128)(2,1)}), bf16[8,6,16,640]{3,2,1,0:T(8,128)(2,1)}, u32[]{:S(2)}, u32[]{:S(2)}) async-start(bf16[8,6,16,640]{3,2,1,0:T(8,128)(2,1)} %to_heads.1), calls=%async_computation.2 | async-start | bytes 1966080 | tf_op jit(solution)/shard_map/all_to_all | solution.py:703
  49.7 10.0 %collective-permute-start.8 = (bf16[160,1920]{1,0:T(8,128)(2,1)}, bf16[160,1920]{1,0:T(8,128)(2,1)S(1)}, u32[]{:S(2)}, u32[]{:S(2)}) collective-permute-start(bf16[160,1920]{1,0:T(8,128)(2,1)} %collective-permute-done.4.refs_2_), channel_id=1, source_target_pairs={{1,0},{2,1},{3,2},{0,3},{5,4},{6,5},{7,6},{4,7},{9,8},{10,9},{11,1... | collective-permute-start | bytes 1843208 | tf_op jit(solution)/shard_map/ppermute | solution.py:695
  52.2 10.8 %collective-permute-start.9 = (bf16[160,1920]{1,0:T(8,128)(2,1)}, bf16[160,1920]{1,0:T(8,128)(2,1)S(1)}, u32[]{:S(2)}, u32[]{:S(2)}) collective-permute-start(bf16[160,1920]{1,0:T(8,128)(2,1)} %collective-permute-done.7.refs_7_), channel_id=1, source_target_pairs={{3,0},{0,1},{1,2},{2,3},{7,4},{4,5},{5,6},{6,7},{11,8},{8,9},{9,10... | collective-permute-start | bytes 1843208 | tf_op jit(solution)/shard_map/ppermute | solution.py:695
  86.0 50.1 %all-to-all-start.3 = ((bf16[8,2,128,640]{3,2,1,0:T(8,128)(2,1)}), bf16[8,2,128,640]{3,2,1,0:T(8,128)(2,1)S(1)}, u32[]{:S(2)}, u32[]{:S(2)}) async-start(bf16[8,2,128,640]{3,2,1,0:T(8,128)(2,1)} %get-tuple-element.77), calls=%async_computation.3 | async-start | bytes 5242880 | tf_op jit(solution)/shard_map/all_to_all | solution.py:703
  93.0 17.7 %collective-permute-start.10 = (bf16[320,1920]{1,0:T(8,128)(2,1)}, bf16[320,1920]{1,0:T(8,128)(2,1)S(1)}, u32[]{:S(2)}, u32[]{:S(2)}) collective-permute-start(bf16[320,1920]{1,0:T(8,128)(2,1)} %get-tuple-element.62), channel_id=1, source_target_pairs={{3,0},{0,1},{1,2},{2,3},{7,4},{4,5},{5,6},{6,7},{11,8},{8,9},{9,10... | collective-permute-start | bytes 3686408 | tf_op jit(solution)/shard_map/ppermute | solution.py:695
  94.5 16.2 %collective-permute-start.11 = (bf16[320,1920]{1,0:T(8,128)(2,1)}, bf16[320,1920]{1,0:T(8,128)(2,1)S(1)}, u32[]{:S(2)}, u32[]{:S(2)}) collective-permute-start(bf16[320,1920]{1,0:T(8,128)(2,1)} %get-tuple-element.63), channel_id=1, source_target_pairs={{1,0},{2,1},{3,2},{0,3},{5,4},{6,5},{7,6},{4,7},{9,8},{10,9},{11,1... | collective-permute-start | bytes 3686408 | tf_op jit(solution)/shard_map/ppermute | solution.py:695
  98.0 12.7 %collective-permute-start.12 = (f32[16,128]{1,0:T(8,128)S(1)}, f32[16,128]{1,0:T(8,128)S(1)}, u32[]{:S(2)}, u32[]{:S(2)}) collective-permute-start(f32[16,128]{1,0:T(8,128)S(1)} %gain.1), channel_id=1, source_target_pairs={{1,0},{0,1},{3,2},{2,3},{5,4},{4,5},{7,6},{6,7},{9,8},{8,9},{11,10... | collective-permute-start | bytes 24584 | tf_op jit(solution)/shard_map/ppermute | solution.py:767
  112.0 10.7 %collective-permute-start.14 = (bf16[160,1920]{1,0:T(8,128)(2,1)S(1)}, bf16[160,1920]{1,0:T(8,128)(2,1)S(1)}, u32[]{:S(2)}, u32[]{:S(2)}) collective-permute-start(bf16[160,1920]{1,0:T(8,128)(2,1)S(1)} %get-tuple-element.73), channel_id=1, source_target_pairs={{3,0},{0,1},{1,2},{2,3},{7,4},{4,5},{5,6},{6,7},{11,8},{8,9},{9,10... | collective-permute-start | bytes 1843208 | tf_op jit(solution)/shard_map/ppermute | solution.py:695
  112.1 10.6 %collective-permute-start.15 = (bf16[160,1920]{1,0:T(8,128)(2,1)S(1)}, bf16[160,1920]{1,0:T(8,128)(2,1)S(1)}, u32[]{:S(2)}, u32[]{:S(2)}) collective-permute-start(bf16[160,1920]{1,0:T(8,128)(2,1)S(1)} %get-tuple-element.75), channel_id=1, source_target_pairs={{1,0},{2,1},{3,2},{0,3},{5,4},{6,5},{7,6},{4,7},{9,8},{10,9},{11,1... | collective-permute-start | bytes 1843208 | tf_op jit(solution)/shard_map/ppermute | solution.py:695
  114.8 31.3 %collective-permute-start.17 = (bf16[384,1280]{1,0:T(8,128)(2,1)}, bf16[384,1280]{1,0:T(8,128)(2,1)}, u32[]{:S(2)}, u32[]{:S(2)}) collective-permute-start(bf16[384,1280]{1,0:T(8,128)(2,1)} %back.2), channel_id=1, source_target_pairs={{16,0},{0,16},{48,32},{32,48},{80,64},{64,80},{112,96},{96,112},{1... | collective-permute-start | bytes 2949128 | tf_op jit(solution)/shard_map/ppermute | solution.py:699
  124.5 11.6 %collective-permute-start.16 = (bf16[88,1920]{1,0:T(8,128)(2,1)}, bf16[88,1920]{1,0:T(8,128)(2,1)S(1)}, u32[]{:S(2)}, u32[]{:S(2)}) collective-permute-start(bf16[88,1920]{1,0:T(8,128)(2,1)} %get-tuple-element.76), channel_id=1, source_target_pairs={{8,0},{9,1},{10,2},{11,3},{12,4},{13,5},{14,6},{15,7},{0,8},{1,9},... | collective-permute-start | bytes 1013768 | tf_op jit(solution)/shard_map/ppermute | solution.py:695
  125.9 10.2 %collective-permute-start.18 = (bf16[88,1920]{1,0:T(8,128)(2,1)}, bf16[88,1920]{1,0:T(8,128)(2,1)}, u32[]{:S(2)}, u32[]{:S(2)}) collective-permute-start(bf16[88,1920]{1,0:T(8,128)(2,1)} %get-tuple-element.84), channel_id=1, source_target_pairs={{4,0},{5,1},{6,2},{7,3},{8,4},{9,5},{10,6},{11,7},{12,8},{13,9},{1... | collective-permute-start | bytes 1013768 | tf_op jit(solution)/shard_map/ppermute | solution.py:695
  126.3 9.9 %collective-permute-start.19 = (bf16[88,1920]{1,0:T(8,128)(2,1)}, bf16[88,1920]{1,0:T(8,128)(2,1)}, u32[]{:S(2)}, u32[]{:S(2)}) collective-permute-start(bf16[88,1920]{1,0:T(8,128)(2,1)} %get-tuple-element.85), channel_id=1, source_target_pairs={{12,0},{13,1},{14,2},{15,3},{0,4},{1,5},{2,6},{3,7},{4,8},{5,9},{6... | collective-permute-start | bytes 1013768 | tf_op jit(solution)/shard_map/ppermute | solution.py:695
  138.4 14.7 %all-to-all-start.4 = ((bf16[8,160,128]{2,1,0:T(8,128)(2,1)}), bf16[8,160,128]{2,1,0:T(8,128)(2,1)S(1)}, u32[]{:S(2)}, u32[]{:S(2)}) async-start(bf16[8,160,128]{2,1,0:T(8,128)(2,1)} %split.1), calls=%async_computation.4 | async-start | bytes 655360 | tf_op jit(solution)/shard_map/all_to_all | solution.py:703
  (15 other events, 129.5 us)

commit v4 on v3

--- a/solution.py
+++ b/solution.py
@@ -234,11 +234,7 @@
     return jnp.broadcast_to(jnp.max(a, axis=-1, keepdims=True), a.shape)
 
 
-def wide_sum(a):
-    return jnp.broadcast_to(jnp.sum(a, axis=-1, keepdims=True), a.shape)
-
-
-CHUNKS = [pl.ds(0, 768), pl.ds(768, 768), pl.ds(1536, 384)]
+CHUNKS = [pl.ds(0, 384), pl.ds(384, 768), pl.ds(1152, 768)]
 
 
 def start(copies):
@@ -374,6 +370,9 @@
             equal = seg == seg.T
             same.append(jnp.concatenate([equal, equal], axis=1))
         masks = [window_masks(i % 4) for i in pairs]
+        row_head = lax.broadcasted_iota(jnp.int32, (256, 256), 0) // TILE
+        lane_head = lax.broadcasted_iota(jnp.int32, (256, 256), 1) // TILE
+        ones = jnp.where(row_head == lane_head, 1.0, 0.0).astype(BF)
         windows = [slice(128 * (i % 4), 128 * (i % 4) + 256) for i in pairs]
 
         def window(a, i):
@@ -393,7 +392,7 @@
         ]
         tops = [halves(wide_max, x) for x in scores]
         expo = [jnp.exp2(x - m) for x, m in zip(scores, tops)]
-        sums = [halves(wide_sum, x) for x in expo]
+        sums = [dot(x.astype(BF), ones) for x in expo]
         weights = [x * (1.0 / total) for x, total in zip(expo, sums)]
         rounded = [x.astype(BF) for x in weights]
         outs = [dot(rounded[i], vv[i]) for i in pairs]
@@ -401,7 +400,7 @@
             dot(rows_of_heads(rounded[i]), stack_heads(d_out[i], masks[i]), TN)
             for i in pairs
         ]
-        inner = [halves(wide_sum, d_probs[i] * weights[i]) for i in pairs]
+        inner = [dot((d_probs[i] * weights[i]).astype(BF), ones) for i in pairs]
         d_scores = [
             (weights[i] * (d_probs[i] - inner[i]) * SCALE).astype(BF) for i in pairs
         ]
@@ -516,7 +515,7 @@
         out_specs=[VM] * n,
         out_shape=[jax.ShapeDtypeStruct((rows, COLS), BF)] * n,
         compiler_params=params(12),
-        cost_estimate=cost(0, (4 if gains else 75000) * len(parts) * PART * COLS),
+        cost_estimate=cost(0, 4 * len(parts) * PART * COLS),
         name="add",
     )(*gains, *[array for array, _ in parts])
 
@@ -721,11 +720,10 @@
 
     messages = exchange(build(owners, qkv_weight, segments))
     partner_patches = swap_cores(patches)
-    own_prep = prep(patches, gain, nat)
     strips = cotangent.reshape(TILES, N_DP, STRIP, D).transpose(1, 0, 2, 3)
     messages, strips = lax.optimization_barrier((messages, strips))
     block, seg, owners_all = compact(group.reshape(1).astype(jnp.int32), messages)
-    strips, own_prep = lax.optimization_barrier((exchange(strips), own_prep))
+    strips = exchange(strips)
 
     owner_of = owners_all[:, :TILES].astype(jnp.int32).reshape(N_DP * TILES)
     u = jnp.arange(N_DP * TILES)
@@ -743,11 +741,15 @@
         [owner_here, jnp.broadcast_to(mine, (2, TILES)).reshape(-1)]
     ).astype(jnp.int32)
 
+    ring = [block] + [from_ring(block, f, 0) for f in (1, 2, 3)]
+    near_a, near_b = jnp.concatenate(ring[:2]), jnp.concatenate(ring[2:])
+    later_patches, near_b = lax.optimization_barrier((patches, near_b))
+    own_prep = prep(later_patches, gain, nat)
+    strips, own_prep = lax.optimization_barrier((strips, own_prep))
+
     heads = to_heads(fwd, strips.reshape(N_DP * TILES, STRIP, D))
     cot = exchange(heads)
 
-    ring = [block] + [from_ring(block, f, 0) for f in (1, 2, 3)]
-    near_a, near_b = jnp.concatenate(ring[:2]), jnp.concatenate(ring[2:])
     above_a, below_b = from_ring(near_a, 0, 1), from_ring(near_b, 0, -1)
     above_b, below_a = from_ring(near_b, 0, 1), from_ring(near_a, 0, -1)
     above_a, above_b, below_a, below_b = lax.optimization_barrier(

time: 155 us -> 152 us (0.981)
  starting transfers between devices: 54.7 us -> 52.8 us
  transfers between devices with their start and end apart: 25 -> 25, of which waited for: 9 -> 10; matrix products, arithmetic and copies ran while one was open for 4% -> 3% of each run, Pallas kernels for 29% -> 29%
where the time goes in v4:
time: 152 us; the launch traced here: 151 us
  Pallas kernels  68.8 us (45%)
  starting transfers between devices  52.8 us (35%)
  waiting for transfers between devices  22.3 us (15%)
  local copies, waits for them, and re-layouts  5.11 us (3%)
  other arithmetic  1.58 us (1%)
    all_to_all x5, starting transfers between devices, exchange(): return lax.all_to_all(value, axis, split_axis=0, concat_axis=0, tiled=True)  30 us
    pallas_call x1, Pallas kernels, main(): pl.pallas_call(main_kernel, in_specs=[SM, VM] + [ANY] * (5 + PIECES), out...  22.2 us
    ppermute x16, starting transfers between devices, from_ring(): return lax.ppermute(value, ('dp', 'inner'), ring_pairs(df, ds))  20.2 us
    pallas_call x2, Pallas kernels, back(): pl.pallas_call(functools.partial(back_kernel, half), in_specs=[VM] + [ANY...  17 us
    pallas_call x2, Pallas kernels, prep(): pl.pallas_call(prep_kernel, in_specs=[VM] * 3, out_specs=[VM] * 2, out_sh...  12.6 us
    all_to_all x5, waiting for transfers between devices, exchange(): return lax.all_to_all(value, axis, split_axis=0, concat_axis=0, tiled=True)  8.42 us
    ppermute x1, waiting for transfers between devices, on_device(): gain_other = lax.ppermute(gain_part, ('dp', 'inner'), double_pairs(0, 3))  5.95 us
    ppermute x16, waiting for transfers between devices, from_ring(): return lax.ppermute(value, ('dp', 'inner'), ring_pairs(df, ds))  4.44 us
  transfers between devices with their start and end apart: 25, of which 10 were waited for; matrix products, arithmetic and copies ran while one was open for 3% of the time, Pallas kernels for 29%

profile of v4, /device:TPU:1, one launch (start us, length us, event | category | flops | bytes accessed | tf_op | source)
XLA Modules:
  0.0 151.5 jit_solution(15168361010791551384)
XLA Ops:
  0.6 1.8 %build.1 = bf16[8,160,128]{2,1,0:T(8,128)(2,1)} custom-call(s32[3]{0:T(128)} %own_ref.1, bf16[10,3840]{1,0:T(8,128)(2,1)} %w_ref.1, s32[3,128]{1,0:T(4,128)} %seg_ref.1), custom_call_target="tpu_custom_call" | custom-call | bytes 327 | tf_op jit(solution)/shard_map/build/pallas_call | solution.py:119
  2.4 6.0 %all-to-all-start = ((bf16[8,160,128]{2,1,0:T(8,128)(2,1)}), bf16[8,160,128]{2,1,0:T(8,128)(2,1)S(1)}, u32[]{:S(2)}, u32[]{:S(2)}) async-start(bf16[8,160,128]{2,1,0:T(8,128)(2,1)} %build.1), calls=%async_computation | async-start | bytes 655360 | tf_op jit(solution)/shard_map/all_to_all | solution.py:702
  11.7 3.9 %all-to-all-done.msg_ref = bf16[8,160,128]{2,1,0:T(8,128)(2,1)S(1)} async-done(((bf16[8,160,128]{2,1,0:T(8,128)(2,1)}), bf16[8,160,128]{2,1,0:T(8,128)(2,1)S(1)}, u32[]{:S(2)}, u32[]{:S(2)}) %all-to-all-start) | async-done | bytes 327712 | tf_op jit(solution)/shard_map/all_to_all | solution.py:702
  16.2 3.8 %collective-permute-start.3 = (bf16[80,1920]{1,0:T(8,128)(2,1)S(1)}, bf16[80,1920]{1,0:T(8,128)(2,1)S(1)}, u32[]{:S(2)}, u32[]{:S(2)}) collective-permute-start(bf16[80,1920]{1,0:T(8,128)(2,1)S(1)} %get-tuple-element.52), channel_id=1, source_target_pairs={{4,0},{5,1},{6,2},{7,3},{8,4},{9,5},{10,6},{11,7},{12,8},{13,9},{1... | collective-permute-start | bytes 921608 | tf_op jit(solution)/shard_map/ppermute | solution.py:694
  21.4 4.6 %all-to-all-start.1 = ((bf16[8,3,16,1280]{3,2,1,0:T(8,128)(2,1)}), bf16[8,3,16,1280]{3,2,1,0:T(8,128)(2,1)S(1)}, u32[]{:S(2)}, u32[]{:S(2)}) async-start(bf16[8,3,16,1280]{3,2,1,0:T(8,128)(2,1)} %bitcast.7), calls=%async_computation.1 | async-start | bytes 1966080 | tf_op jit(solution)/shard_map/all_to_all | solution.py:702
  28.7 1.8 %collective-permute-done.1 = bf16[80,1920]{1,0:T(8,128)(2,1)S(1)} collective-permute-done((bf16[80,1920]{1,0:T(8,128)(2,1)S(1)}, bf16[80,1920]{1,0:T(8,128)(2,1)S(1)}, u32[]{:S(2)}, u32[]{:S(2)}) %collective-permute-start.1) | collective-permute-done | bytes 307232 | tf_op jit(solution)/shard_map/ppermute | solution.py:694
  31.6 1.8 %collective-permute-start.5 = (bf16[160,1920]{1,0:T(8,128)(2,1)S(1)}, bf16[160,1920]{1,0:T(8,128)(2,1)}, u32[]{:S(2)}, u32[]{:S(2)}) collective-permute-start(bf16[160,1920]{1,0:T(8,128)(2,1)S(1)} %pad_maximum_fusion.refs_1_), channel_id=1, source_target_pairs={{1,0},{2,1},{3,2},{0,3},{5,4},{6,5},{7,6},{4,7},{9,8},{10,9},{11,1... | collective-permute-start | bytes 1843208 | tf_op jit(solution)/shard_map/ppermute | solution.py:694
  33.6 6.3 %prep.2 = (bf16[384,1280]{1,0:T(8,128)(2,1)}, bf16[1280,384]{1,0:T(8,128)(2,1)}) custom-call(bf16[384,1280]{1,0:T(8,128)(2,1)} %patches_ref.2, f32[1,1280]{1,0:T(1,128)} %reshape.235.gain_ref, f32[1,1280]{1,0:T(1,128)} %convert_element_type.14.nat_ref), custom_call_target="tpu_custom_call" | custom-call | flops 2516582 | bytes 2949 | tf_op jit(solution)/shard_map/prep/pallas_call | solution.py:84
  41.9 6.3 %all-to-all-start.2 = ((bf16[8,6,16,640]{3,2,1,0:T(8,128)(2,1)}), bf16[8,6,16,640]{3,2,1,0:T(8,128)(2,1)}, u32[]{:S(2)}, u32[]{:S(2)}) async-start(bf16[8,6,16,640]{3,2,1,0:T(8,128)(2,1)} %to_heads.1), calls=%async_computation.2 | async-start | bytes 1966080 | tf_op jit(solution)/shard_map/all_to_all | solution.py:702
  50.9 6.3 %prep.3 = (bf16[384,1280]{1,0:T(8,128)(2,1)}, bf16[1280,384]{1,0:T(8,128)(2,1)}) custom-call(bf16[384,1280]{1,0:T(8,128)(2,1)} %collective-permute-done.2.patches_ref, f32[1,1280]{1,0:T(1,128)} %reshape.235.gain_ref, f32[1,1280]{1,0:T(1,128)} %convert_element_type.14.nat_ref), custom_call_target="tpu_custom_call" | custom-call | flops 2516582 | bytes 2949 | tf_op jit(solution)/shard_map/prep/pallas_call | solution.py:84
  59.4 3.3 %all-to-all-done.2.cot_ref = bf16[8,6,16,640]{3,2,1,0:T(8,128)(2,1)} async-done(((bf16[8,6,16,640]{3,2,1,0:T(8,128)(2,1)}), bf16[8,6,16,640]{3,2,1,0:T(8,128)(2,1)}, u32[]{:S(2)}, u32[]{:S(2)}) %all-to-all-start.2) | async-done | bytes 983072 | tf_op jit(solution)/shard_map/all_to_all | solution.py:702
  62.8 22.2 %main.1 = (bf16[8,2,128,640]{3,2,1,0:T(8,128)(2,1)}, bf16[768,1920]{1,0:T(8,128)(2,1)}, bf16[160,1920]{1,0:T(8,128)(2,1)}, bf16[160,1920]{1,0:T(8,128)(2,1)}, bf...) custom-call(s32[12]{0:T(128)} %pad_add_fusion.1.idx_ref, ...), custom_call_target="tpu_custom_call" | custom-call | flops 8000000 | bytes 20971 | tf_op jit(solution)/shard_map/main/pallas_call | solution.py:434
  85.0 5.6 %all-to-all-start.3 = ((bf16[8,2,128,640]{3,2,1,0:T(8,128)(2,1)}), bf16[8,2,128,640]{3,2,1,0:T(8,128)(2,1)S(1)}, u32[]{:S(2)}, u32[]{:S(2)}) async-start(bf16[8,2,128,640]{3,2,1,0:T(8,128)(2,1)} %get-tuple-element.81), calls=%async_computation.3 | async-start | bytes 5242880 | tf_op jit(solution)/shard_map/all_to_all | solution.py:702
  93.3 2.3 %gain.1 = f32[16,128]{1,0:T(8,128)S(1)} custom-call(f32[1280,128]{1,0:T(8,128)S(1)} %copy-done, f32[1,1280]{1,0:T(1,128)S(1)} %copy-done.5, f32[1,1280]{1,0:T(1,128)S(1)} %copy-done.6), custom_call_target="tpu_custom_call" | custom-call | bytes 655 | tf_op jit(solution)/shard_map/gain/pallas_call | solution.py:539
  96.3 8.5 %back.2 = bf16[384,1280]{1,0:T(8,128)(2,1)} custom-call(f32[1,1280]{1,0:T(1,128)} %convert_element_type.14.nat_ref, bf16[768,1920]{1,0:T(8,128)(2,1)} %get-tuple-element.83.dqkv_ref, bf16[160,1920]{1,0:T(8,128)(2,1)} %copy-done.9, bf16[160,1920]{1,0:T(8,128)(2,1)} %copy-done.8, bf16[160,1920]{1,0:T(8,128)(2,1)} %collective-permute-done.4.refs_2_, ...), custom_call_target="tpu_custom_call" | custom-call | flops 3145728 | bytes 15728 | tf_op jit(solution)/shard_map/back/pallas_call | solution.py:570
  104.8 3.5 %collective-permute-done.12 = f32[16,128]{1,0:T(8,128)S(1)} collective-permute-done((f32[16,128]{1,0:T(8,128)S(1)}, f32[16,128]{1,0:T(8,128)S(1)}, u32[]{:S(2)}, u32[]{:S(2)}) %collective-permute-start.12) | collective-permute-done | bytes 8224 | tf_op jit(solution)/shard_map/ppermute | solution.py:769
  109.8 2.7 %collective-permute-start.15 = (bf16[160,1920]{1,0:T(8,128)(2,1)S(1)}, bf16[160,1920]{1,0:T(8,128)(2,1)S(1)}, u32[]{:S(2)}, u32[]{:S(2)}) collective-permute-start(bf16[160,1920]{1,0:T(8,128)(2,1)S(1)} %get-tuple-element.79), channel_id=1, source_target_pairs={{1,0},{2,1},{3,2},{0,3},{5,4},{6,5},{7,6},{4,7},{9,8},{10,9},{11,1... | collective-permute-start | bytes 1843208 | tf_op jit(solution)/shard_map/ppermute | solution.py:694
  114.4 6.0 %collective-permute-done.13.other_ref = f32[16,128]{1,0:T(8,128)S(1)} collective-permute-done((f32[16,128]{1,0:T(8,128)S(1)}, f32[16,128]{1,0:T(8,128)S(1)}, u32[]{:S(2)}, u32[]{:S(2)}) %collective-permute-start.13) | collective-permute-done | bytes 8224 | tf_op jit(solution)/shard_map/ppermute | solution.py:778
  120.4 1.7 %add.244 = (bf16[88,1920]{1,0:T(8,128)(2,1)S(1)}, bf16[88,1920]{1,0:T(8,128)(2,1)}, bf16[88,1920]{1,0:T(8,128)(2,1)}, bf16[88,1920]{1,0:T(8,128)(2,1)}) custom-call(f32[16,128]{1,0:T(8,128)S(1)} %add.203.gain_ref, f32[16,128]{1,0:T(8,128)S(1)} %collective-permute-done.13.other_ref, bf16[160,1920]{1,0:T(8,128)(2,1)S(1)} %copy-done.3, ...), custom_call_target="tpu_custom_call" | custom-call | bytes 7372 | tf_op jit(solution)/shard_map/add/pallas_call | solution.py:508
  125.0 8.5 %back.3.mine_ref = bf16[384,1280]{1,0:T(8,128)(2,1)} custom-call(f32[1,1280]{1,0:T(1,128)} %convert_element_type.14.nat_ref, bf16[768,1920]{1,0:T(8,128)(2,1)} %get-tuple-element.83.dqkv_ref, bf16[160,1920]{1,0:T(8,128)(2,1)} %copy-done.9, bf16[160,1920]{1,0:T(8,128)(2,1)} %copy-done.8, bf16[160,1920]{1,0:T(8,128)(2,1)} %collective-permute-done.4.refs_2_, ...), custom_call_target="tpu_custom_call" | custom-call | flops 3145728 | bytes 15728 | tf_op jit(solution)/shard_map/back/pallas_call | solution.py:570
  133.9 2.2 %split.1 = bf16[8,160,128]{2,1,0:T(8,128)(2,1)} custom-call(bf16[88,1920]{1,0:T(8,128)(2,1)S(1)} %get-tuple-element.82.rows_ref, bf16[88,1920]{1,0:T(8,128)(2,1)S(1)} %collective-permute-done.16.one_ref, bf16[88,1920]{1,0:T(8,128)(2,1)} %collective-permute-done.18.two_ref, bf16[88,1920]{1,0:T(8,128)(2,1)} %collective-permute-done.19.three_ref), custom_call_target="tpu_custom_call" | custom-call | bytes 655 | tf_op jit(solution)/shard_map/split/pallas_call | solution.py:634
  136.1 7.5 %all-to-all-start.4 = ((bf16[8,160,128]{2,1,0:T(8,128)(2,1)}), bf16[8,160,128]{2,1,0:T(8,128)(2,1)S(1)}, u32[]{:S(2)}, u32[]{:S(2)}) async-start(bf16[8,160,128]{2,1,0:T(8,128)(2,1)} %split.1), calls=%async_computation.4 | async-start | bytes 655360 | tf_op jit(solution)/shard_map/all_to_all | solution.py:702
  143.7 4.2 %rows_back.1 = bf16[384,1280]{1,0:T(8,128)(2,1)} custom-call(bf16[384,1280]{1,0:T(8,128)(2,1)} %patches_ref.2, f32[1,1280]{1,0:T(1,128)} %reshape.235.gain_ref, bf16[384,1280]{1,0:T(8,128)(2,1)} %back.3.mine_ref, bf16[384,1280]{1,0:T(8,128)(2,1)} %collective-permute-done.17.other_ref), custom_call_target="tpu_custom_call" | custom-call | flops 9830 | bytes 3932 | tf_op jit(solution)/shard_map/rows_back/pallas_call | solution.py:602
  147.9 2.1 %place.1 = bf16[3,128,1280]{2,1,0:T(8,128)(2,1)} custom-call(s32[6]{0:T(128)S(1)} %pad_add_fusion.idx_ref, bf16[8,2,128,640]{3,2,1,0:T(8,128)(2,1)S(1)} %all-to-all-done.3.left_ref.right_ref, bf16[8,2,128,640]{3,2,1,0:T(8,128)(2,1)S(1)} %all-to-all-done.3.left_ref.right_ref), custom_call_target="tpu_custom_call" | custom-call | bytes 1966 | tf_op jit(solution)/shard_map/place/pallas_call | solution.py:200
  (97 shorter events, 27.9 us)
Async XLA Ops:
  2.4 13.1 %all-to-all-start = ((bf16[8,160,128]{2,1,0:T(8,128)(2,1)}), bf16[8,160,128]{2,1,0:T(8,128)(2,1)S(1)}, u32[]{:S(2)}, u32[]{:S(2)}) async-start(bf16[8,160,128]{2,1,0:T(8,128)(2,1)} %build.1), calls=%async_computation | async-start | bytes 655360 | tf_op jit(solution)/shard_map/all_to_all | solution.py:702
  8.4 42.5 %collective-permute-start.2 = (bf16[384,1280]{1,0:T(8,128)(2,1)}, bf16[384,1280]{1,0:T(8,128)(2,1)}, u32[]{:S(2)}, u32[]{:S(2)}) collective-permute-start(bf16[384,1280]{1,0:T(8,128)(2,1)} %patches_ref.2), channel_id=1, source_target_pairs={{16,0},{0,16},{48,32},{32,48},{80,64},{64,80},{112,96},{96,112},{1... | collective-permute-start | bytes 2949128 | tf_op jit(solution)/shard_map/ppermute | solution.py:698
  16.2 9.7 %collective-permute-start.3 = (bf16[80,1920]{1,0:T(8,128)(2,1)S(1)}, bf16[80,1920]{1,0:T(8,128)(2,1)S(1)}, u32[]{:S(2)}, u32[]{:S(2)}) collective-permute-start(bf16[80,1920]{1,0:T(8,128)(2,1)S(1)} %get-tuple-element.52), channel_id=1, source_target_pairs={{4,0},{5,1},{6,2},{7,3},{8,4},{9,5},{10,6},{11,7},{12,8},{13,9},{1... | collective-permute-start | bytes 921608 | tf_op jit(solution)/shard_map/ppermute | solution.py:694
  20.0 10.5 %collective-permute-start.1 = (bf16[80,1920]{1,0:T(8,128)(2,1)S(1)}, bf16[80,1920]{1,0:T(8,128)(2,1)S(1)}, u32[]{:S(2)}, u32[]{:S(2)}) collective-permute-start(bf16[80,1920]{1,0:T(8,128)(2,1)S(1)} %get-tuple-element.52), channel_id=1, source_target_pairs={{12,0},{13,1},{14,2},{15,3},{0,4},{1,5},{2,6},{3,7},{4,8},{5,9},{6... | collective-permute-start | bytes 921608 | tf_op jit(solution)/shard_map/ppermute | solution.py:694
  20.0 10.5 %collective-permute-start = (bf16[80,1920]{1,0:T(8,128)(2,1)S(1)}, bf16[80,1920]{1,0:T(8,128)(2,1)S(1)}, u32[]{:S(2)}, u32[]{:S(2)}) collective-permute-start(bf16[80,1920]{1,0:T(8,128)(2,1)S(1)} %get-tuple-element.52), channel_id=1, source_target_pairs={{8,0},{9,1},{10,2},{11,3},{12,4},{13,5},{14,6},{15,7},{0,8},{1,9},... | collective-permute-start | bytes 921608 | tf_op jit(solution)/shard_map/ppermute | solution.py:694
  21.4 19.0 %all-to-all-start.1 = ((bf16[8,3,16,1280]{3,2,1,0:T(8,128)(2,1)}), bf16[8,3,16,1280]{3,2,1,0:T(8,128)(2,1)S(1)}, u32[]{:S(2)}, u32[]{:S(2)}) async-start(bf16[8,3,16,1280]{3,2,1,0:T(8,128)(2,1)} %bitcast.7), calls=%async_computation.1 | async-start | bytes 1966080 | tf_op jit(solution)/shard_map/all_to_all | solution.py:702
  26.0 22.3 %collective-permute-start.6 = (bf16[160,1920]{1,0:T(8,128)(2,1)S(1)}, bf16[160,1920]{1,0:T(8,128)(2,1)S(1)}, u32[]{:S(2)}, u32[]{:S(2)}) collective-permute-start(bf16[160,1920]{1,0:T(8,128)(2,1)S(1)} %constant_dynamic-update-slice_fusion.refs_0_), channel_id=1, source_target_pairs={{3,0},{0,1},{1,2},{2,3},{7,4},{4,5},{5,6},{6,7},{11,8},{8,9},{9,10... | collective-permute-start | bytes 1843208 | tf_op jit(solution)/shard_map/ppermute | solution.py:694
  27.6 20.7 %collective-permute-start.4 = (bf16[160,1920]{1,0:T(8,128)(2,1)S(1)}, bf16[160,1920]{1,0:T(8,128)(2,1)}, u32[]{:S(2)}, u32[]{:S(2)}) collective-permute-start(bf16[160,1920]{1,0:T(8,128)(2,1)S(1)} %constant_dynamic-update-slice_fusion.refs_0_), channel_id=1, source_target_pairs={{1,0},{2,1},{3,2},{0,3},{5,4},{6,5},{7,6},{4,7},{9,8},{10,9},{11,1... | collective-permute-start | bytes 1843208 | tf_op jit(solution)/shard_map/ppermute | solution.py:694
  30.6 17.7 %collective-permute-start.7 = (bf16[160,1920]{1,0:T(8,128)(2,1)S(1)}, bf16[160,1920]{1,0:T(8,128)(2,1)}, u32[]{:S(2)}, u32[]{:S(2)}) collective-permute-start(bf16[160,1920]{1,0:T(8,128)(2,1)S(1)} %pad_maximum_fusion.refs_1_), channel_id=1, source_target_pairs={{3,0},{0,1},{1,2},{2,3},{7,4},{4,5},{5,6},{6,7},{11,8},{8,9},{9,10... | collective-permute-start | bytes 1843208 | tf_op jit(solution)/shard_map/ppermute | solution.py:694
  31.6 16.7 %collective-permute-start.5 = (bf16[160,1920]{1,0:T(8,128)(2,1)S(1)}, bf16[160,1920]{1,0:T(8,128)(2,1)}, u32[]{:S(2)}, u32[]{:S(2)}) collective-permute-start(bf16[160,1920]{1,0:T(8,128)(2,1)S(1)} %pad_maximum_fusion.refs_1_), channel_id=1, source_target_pairs={{1,0},{2,1},{3,2},{0,3},{5,4},{6,5},{7,6},{4,7},{9,8},{10,9},{11,1... | collective-permute-start | bytes 1843208 | tf_op jit(solution)/shard_map/ppermute | solution.py:694
  41.9 20.9 %all-to-all-start.2 = ((bf16[8,6,16,640]{3,2,1,0:T(8,128)(2,1)}), bf16[8,6,16,640]{3,2,1,0:T(8,128)(2,1)}, u32[]{:S(2)}, u32[]{:S(2)}) async-start(bf16[8,6,16,640]{3,2,1,0:T(8,128)(2,1)} %to_heads.1), calls=%async_computation.2 | async-start | bytes 1966080 | tf_op jit(solution)/shard_map/all_to_all | solution.py:702
  48.3 9.7 %collective-permute-start.8 = (bf16[160,1920]{1,0:T(8,128)(2,1)}, bf16[160,1920]{1,0:T(8,128)(2,1)S(1)}, u32[]{:S(2)}, u32[]{:S(2)}) collective-permute-start(bf16[160,1920]{1,0:T(8,128)(2,1)} %collective-permute-done.4.refs_2_), channel_id=1, source_target_pairs={{1,0},{2,1},{3,2},{0,3},{5,4},{6,5},{7,6},{4,7},{9,8},{10,9},{11,1... | collective-permute-start | bytes 1843208 | tf_op jit(solution)/shard_map/ppermute | solution.py:694
  48.4 11.1 %collective-permute-start.9 = (bf16[160,1920]{1,0:T(8,128)(2,1)}, bf16[160,1920]{1,0:T(8,128)(2,1)S(1)}, u32[]{:S(2)}, u32[]{:S(2)}) collective-permute-start(bf16[160,1920]{1,0:T(8,128)(2,1)} %collective-permute-done.7.refs_7_), channel_id=1, source_target_pairs={{3,0},{0,1},{1,2},{2,3},{7,4},{4,5},{5,6},{6,7},{11,8},{8,9},{9,10... | collective-permute-start | bytes 1843208 | tf_op jit(solution)/shard_map/ppermute | solution.py:694
  85.0 48.4 %all-to-all-start.3 = ((bf16[8,2,128,640]{3,2,1,0:T(8,128)(2,1)}), bf16[8,2,128,640]{3,2,1,0:T(8,128)(2,1)S(1)}, u32[]{:S(2)}, u32[]{:S(2)}) async-start(bf16[8,2,128,640]{3,2,1,0:T(8,128)(2,1)} %get-tuple-element.81), calls=%async_computation.3 | async-start | bytes 5242880 | tf_op jit(solution)/shard_map/all_to_all | solution.py:702
  90.6 17.7 %collective-permute-start.10 = (bf16[320,1920]{1,0:T(8,128)(2,1)}, bf16[320,1920]{1,0:T(8,128)(2,1)S(1)}, u32[]{:S(2)}, u32[]{:S(2)}) collective-permute-start(bf16[320,1920]{1,0:T(8,128)(2,1)} %get-tuple-element.66), channel_id=1, source_target_pairs={{3,0},{0,1},{1,2},{2,3},{7,4},{4,5},{5,6},{6,7},{11,8},{8,9},{9,10... | collective-permute-start | bytes 3686408 | tf_op jit(solution)/shard_map/ppermute | solution.py:694
  92.1 16.2 %collective-permute-start.11 = (bf16[320,1920]{1,0:T(8,128)(2,1)}, bf16[320,1920]{1,0:T(8,128)(2,1)S(1)}, u32[]{:S(2)}, u32[]{:S(2)}) collective-permute-start(bf16[320,1920]{1,0:T(8,128)(2,1)} %get-tuple-element.67), channel_id=1, source_target_pairs={{1,0},{2,1},{3,2},{0,3},{5,4},{6,5},{7,6},{4,7},{9,8},{10,9},{11,1... | collective-permute-start | bytes 3686408 | tf_op jit(solution)/shard_map/ppermute | solution.py:694
  95.6 12.7 %collective-permute-start.12 = (f32[16,128]{1,0:T(8,128)S(1)}, f32[16,128]{1,0:T(8,128)S(1)}, u32[]{:S(2)}, u32[]{:S(2)}) collective-permute-start(f32[16,128]{1,0:T(8,128)S(1)} %gain.1), channel_id=1, source_target_pairs={{1,0},{0,1},{3,2},{2,3},{5,4},{4,5},{7,6},{6,7},{9,8},{8,9},{11,10... | collective-permute-start | bytes 24584 | tf_op jit(solution)/shard_map/ppermute | solution.py:769
  109.7 10.7 %collective-permute-start.14 = (bf16[160,1920]{1,0:T(8,128)(2,1)S(1)}, bf16[160,1920]{1,0:T(8,128)(2,1)S(1)}, u32[]{:S(2)}, u32[]{:S(2)}) collective-permute-start(bf16[160,1920]{1,0:T(8,128)(2,1)S(1)} %get-tuple-element.77), channel_id=1, source_target_pairs={{3,0},{0,1},{1,2},{2,3},{7,4},{4,5},{5,6},{6,7},{11,8},{8,9},{9,10... | collective-permute-start | bytes 1843208 | tf_op jit(solution)/shard_map/ppermute | solution.py:694
  109.8 10.6 %collective-permute-start.15 = (bf16[160,1920]{1,0:T(8,128)(2,1)S(1)}, bf16[160,1920]{1,0:T(8,128)(2,1)S(1)}, u32[]{:S(2)}, u32[]{:S(2)}) collective-permute-start(bf16[160,1920]{1,0:T(8,128)(2,1)S(1)} %get-tuple-element.79), channel_id=1, source_target_pairs={{1,0},{2,1},{3,2},{0,3},{5,4},{6,5},{7,6},{4,7},{9,8},{10,9},{11,1... | collective-permute-start | bytes 1843208 | tf_op jit(solution)/shard_map/ppermute | solution.py:694
  112.4 31.3 %collective-permute-start.17 = (bf16[384,1280]{1,0:T(8,128)(2,1)}, bf16[384,1280]{1,0:T(8,128)(2,1)}, u32[]{:S(2)}, u32[]{:S(2)}) collective-permute-start(bf16[384,1280]{1,0:T(8,128)(2,1)} %back.2), channel_id=1, source_target_pairs={{16,0},{0,16},{48,32},{32,48},{80,64},{64,80},{112,96},{96,112},{1... | collective-permute-start | bytes 2949128 | tf_op jit(solution)/shard_map/ppermute | solution.py:698
  122.1 11.3 %collective-permute-start.16 = (bf16[88,1920]{1,0:T(8,128)(2,1)}, bf16[88,1920]{1,0:T(8,128)(2,1)S(1)}, u32[]{:S(2)}, u32[]{:S(2)}) collective-permute-start(bf16[88,1920]{1,0:T(8,128)(2,1)} %get-tuple-element.80), channel_id=1, source_target_pairs={{8,0},{9,1},{10,2},{11,3},{12,4},{13,5},{14,6},{15,7},{0,8},{1,9},... | collective-permute-start | bytes 1013768 | tf_op jit(solution)/shard_map/ppermute | solution.py:694
  123.3 10.1 %collective-permute-start.18 = (bf16[88,1920]{1,0:T(8,128)(2,1)}, bf16[88,1920]{1,0:T(8,128)(2,1)}, u32[]{:S(2)}, u32[]{:S(2)}) collective-permute-start(bf16[88,1920]{1,0:T(8,128)(2,1)} %get-tuple-element.88), channel_id=1, source_target_pairs={{4,0},{5,1},{6,2},{7,3},{8,4},{9,5},{10,6},{11,7},{12,8},{13,9},{1... | collective-permute-start | bytes 1013768 | tf_op jit(solution)/shard_map/ppermute | solution.py:694
  123.7 10.1 %collective-permute-start.19 = (bf16[88,1920]{1,0:T(8,128)(2,1)}, bf16[88,1920]{1,0:T(8,128)(2,1)}, u32[]{:S(2)}, u32[]{:S(2)}) collective-permute-start(bf16[88,1920]{1,0:T(8,128)(2,1)} %get-tuple-element.89), channel_id=1, source_target_pairs={{12,0},{13,1},{14,2},{15,3},{0,4},{1,5},{2,6},{3,7},{4,8},{5,9},{6... | collective-permute-start | bytes 1013768 | tf_op jit(solution)/shard_map/ppermute | solution.py:694
  136.1 14.6 %all-to-all-start.4 = ((bf16[8,160,128]{2,1,0:T(8,128)(2,1)}), bf16[8,160,128]{2,1,0:T(8,128)(2,1)S(1)}, u32[]{:S(2)}, u32[]{:S(2)}) async-start(bf16[8,160,128]{2,1,0:T(8,128)(2,1)} %split.1), calls=%async_computation.4 | async-start | bytes 655360 | tf_op jit(solution)/shard_map/all_to_all | solution.py:702
  (15 other events, 127.3 us)
